TPU v7x, 128 devices: a whole 4x4x4 slice. The times are simulated.
128 devices in a mesh: row: 8 (over y, core), col: 16 (over x, z).
Axes of the slice: x: 4, y: 4, z: 4, core: 2. Of those that a mesh axis runs over, the one named last changes fastest.
Arguments:
- fine_input: bfloat16 [4, 128, 128, 512], P(None, 'row', 'col'), may hold values from -6 to 6
- gain_fine: float32 [512], replicated, may hold values from 0.25 to 1.75
- fine_qkv: bfloat16 [512, 1536], replicated, may hold values from -0.25 to 0.25
- fine_out: bfloat16 [512, 512], replicated, may hold values from -0.75 to 0.75
- fine_scale: float32 [8], replicated, may hold values from 4 to 12
- merge_weight: bfloat16 [2048, 1024], replicated, may hold values from -0.125 to 0.125
- gain_coarse: float32 [1024], replicated, may hold values from 0.25 to 1.75
- coarse_qkv: bfloat16 [3, 1024, 1024], P(None, None, 'col'), may hold values from -0.1875 to 0.1875
- coarse_out: bfloat16 [1024, 1024], P('col'), may hold values from -0.75 to 0.75
- coarse_scale: float32 [16], P('col'), may hold values from 4 to 12
- cotangent: bfloat16 [4, 64, 64, 1024], P(None, 'row', 'col'), may hold values from -6 to 6
Outputs:
- coarse_output: bfloat16 [4, 64, 64, 1024], P(None, 'row', 'col')
- input_grad: float32 [4, 64, 64, 1024], P(None, 'row', 'col')
- qkv_grad: float32 [3, 1024, 1024], P(None, 'row', 'col')
- out_grad: float32 [1024, 1024], P('col', 'row')
All inputs are finite; a program needn't handle non-finite values.
Results may differ from a plain program's by a relative error of at most 0.034.
Values may be sent and summed in bfloat16 or wider, within the bound.
A program may use at most 128 MiB of HBM per device.

v0:
```python
import jax
import jax.numpy as jnp
from jax import lax
from jax.sharding import PartitionSpec as P


def padded(cells, sides, width):
    for axis, dim in sides:
        count = lax.axis_size(axis)
        ends = count - 1
        head = lax.slice_in_dim(cells, 0, width, axis=dim)
        tail = lax.slice_in_dim(cells, cells.shape[dim] - width, cells.shape[dim], axis=dim)
        cells = jnp.concatenate(
            [
                lax.ppermute(tail, axis, [(i, (i + 1) % count) for i in range(ends)]),
                cells,
                lax.ppermute(head, axis, [((i + 1) % count, i) for i in range(ends)]),
            ],
            axis=dim,
        )
    return cells


def normalize(values):
    return values * lax.rsqrt(jnp.mean(values * values, axis=-1, keepdims=True) + 1e-06)


def norm_back(values, upstream):
    factor = lax.rsqrt(jnp.mean(values * values, axis=-1, keepdims=True) + 1e-06)
    unit = values * factor
    return factor * (upstream - unit * jnp.mean(upstream * unit, axis=-1, keepdims=True))


def neighbour_attention(queries, keys_wide, values_wide, row_inside, col_inside, scales):
    rows = queries.shape[1]
    cols = queries.shape[2]
    head_scale = scales / queries.shape[-1]
    totals = jnp.zeros(queries.shape[:4], jnp.float32)
    weighted = jnp.zeros(queries.shape, jnp.float32)
    for row_off in range(7):
        for col_off in range(7):
            keys_here = keys_wide[:, row_off : row_off + rows, col_off : col_off + cols]
            values_here = values_wide[:, row_off : row_off + rows, col_off : col_off + cols].astype(
                jnp.float32
            )
            scores = jnp.sum(queries * keys_here, axis=-1) * head_scale
            inside = (
                row_inside[row_off : row_off + rows][:, None]
                * col_inside[col_off : col_off + cols][None, :]
            )
            powered = jnp.exp(scores) * inside[None, :, :, None]
            totals = totals + powered
            weighted = weighted + powered[..., None] * values_here
    return weighted / totals[..., None]


def attend(queries, keys, values, grads, scales):
    head_size = queries.shape[-1]
    factor = (scales / head_size)[:, None, None]
    head_factor = (scales / head_size)[None, :, None]
    scores = jnp.einsum("qhd,khd->hqk", queries, keys, preferred_element_type=jnp.float32) * factor
    powered = jnp.exp(scores)
    denoms = jnp.sum(powered, axis=-1)
    numerator = jnp.einsum(
        "hqk,khd->qhd", powered.astype(jnp.bfloat16), values, preferred_element_type=jnp.float32
    )
    outputs = numerator / denoms.T[:, :, None]
    chance = powered / denoms[:, :, None]
    deltas = jnp.sum(grads.astype(jnp.float32) * outputs, axis=-1)
    grad_prob = jnp.einsum("qhd,khd->hqk", grads, values, preferred_element_type=jnp.float32)
    grad_score = (chance * (grad_prob - deltas.T[:, :, None])).astype(jnp.bfloat16)
    grad_value = jnp.einsum(
        "hqk,qhd->khd", chance.astype(jnp.bfloat16), grads, preferred_element_type=jnp.float32
    )
    grad_query = (
        jnp.einsum("hqk,khd->qhd", grad_score, keys, preferred_element_type=jnp.float32)
        * head_factor
    )
    grad_key = (
        jnp.einsum("hqk,qhd->khd", grad_score, queries, preferred_element_type=jnp.float32)
        * head_factor
    )
    return (outputs, grad_query, grad_key, grad_value)


def per_device(
    fine_input,
    gain_fine,
    fine_qkv,
    fine_out,
    fine_scale,
    merge_weight,
    gain_coarse,
    coarse_qkv,
    coarse_out,
    coarse_scale,
    cotangent,
):
    images, tile_rows, tile_cols, width_fine = fine_input.shape
    heads_fine = fine_scale.shape[0]
    head_size = width_fine // heads_fine
    inputs = fine_input.astype(jnp.float32)
    normed = (normalize(inputs) * gain_fine).astype(jnp.bfloat16)
    flat_fine = normed.reshape(-1, width_fine)
    queries = jnp.dot(
        flat_fine, fine_qkv[:, :width_fine], preferred_element_type=jnp.float32
    ).astype(jnp.bfloat16)
    queries = normalize(
        queries.astype(jnp.float32).reshape(images, tile_rows, tile_cols, heads_fine, head_size)
    )
    key_value = jnp.dot(
        flat_fine, fine_qkv[:, width_fine:], preferred_element_type=jnp.float32
    ).astype(jnp.bfloat16)
    key_value = key_value.reshape(images, tile_rows, tile_cols, 2 * width_fine)
    key_value = padded(key_value, (("row", 1), ("col", 2)), 3)
    key_value = key_value.reshape(images, tile_rows + 6, tile_cols + 6, 2, heads_fine, head_size)
    keys_wide = normalize(key_value[:, :, :, 0].astype(jnp.float32))
    values_wide = key_value[:, :, :, 1]
    row_place = lax.axis_index("row") * tile_rows + jnp.arange(tile_rows + 6, dtype=jnp.int32) - 3
    col_place = lax.axis_index("col") * tile_cols + jnp.arange(tile_cols + 6, dtype=jnp.int32) - 3
    row_inside = ((row_place >= 0) & (row_place < tile_rows * lax.axis_size("row"))).astype(
        jnp.float32
    )
    col_inside = ((col_place >= 0) & (col_place < tile_cols * lax.axis_size("col"))).astype(
        jnp.float32
    )
    mixed = neighbour_attention(
        queries, keys_wide, values_wide, row_inside, col_inside, fine_scale
    ).astype(jnp.bfloat16)
    fine_result = (
        inputs
        + jnp.dot(
            mixed.reshape(-1, width_fine), fine_out, preferred_element_type=jnp.float32
        ).reshape(inputs.shape)
    ).astype(jnp.bfloat16)
    half_rows = tile_rows // 2
    half_cols = tile_cols // 2
    merged = (
        fine_result.reshape(images, half_rows, 2, half_cols, 2, width_fine)
        .transpose(0, 1, 3, 2, 4, 5)
        .reshape(-1, 4 * width_fine)
    )
    width_coarse = merge_weight.shape[1]
    coarse_in = jnp.dot(merged, merge_weight, preferred_element_type=jnp.float32).astype(
        jnp.bfloat16
    )
    coarse_float = coarse_in.astype(jnp.float32).reshape(images, half_rows, half_cols, width_coarse)
    coarse_normed = (normalize(coarse_float) * gain_coarse).astype(jnp.bfloat16)
    band = lax.all_gather(coarse_normed, "col", axis=2, tiled=True)
    band_cols = band.shape[2]
    band_tokens = half_rows * band_cols
    band_flat = band.reshape(-1, width_coarse)
    heads_local = coarse_scale.shape[0]
    group_width = coarse_qkv.shape[2]
    raw = [
        jnp.dot(band_flat, coarse_qkv[index], preferred_element_type=jnp.float32).astype(
            jnp.bfloat16
        )
        for index in range(3)
    ]
    query_f = raw[0].astype(jnp.float32).reshape(images, band_tokens, heads_local, head_size)
    key_f = raw[1].astype(jnp.float32).reshape(images, band_tokens, heads_local, head_size)
    query_n = normalize(query_f).astype(jnp.bfloat16)
    key_n = normalize(key_f).astype(jnp.bfloat16)
    key_value_band = jnp.concatenate(
        [
            key_n.reshape(images, band_tokens, group_width),
            raw[2].reshape(images, band_tokens, group_width),
        ],
        axis=-1,
    )
    key_value_all = lax.all_gather(key_value_band, "row", axis=1, tiled=True)
    all_tokens = key_value_all.shape[1]
    keys_all = key_value_all[:, :, :group_width].reshape(images, all_tokens, heads_local, head_size)
    values_all = key_value_all[:, :, group_width:].reshape(
        images, all_tokens, heads_local, head_size
    )
    grad_band = lax.all_gather(cotangent, "col", axis=2, tiled=True).reshape(-1, width_coarse)
    grad_attn = jnp.dot(grad_band, coarse_out.T, preferred_element_type=jnp.float32).astype(
        jnp.bfloat16
    )
    grad_attn = grad_attn.reshape(images, band_tokens, heads_local, head_size)
    results = lax.map(
        lambda member: attend(member[0], member[1], member[2], member[3], coarse_scale),
        (query_n, keys_all, values_all, grad_attn),
    )
    attn_f, grad_qn, grad_kn, grad_v = results
    attn = attn_f.astype(jnp.bfloat16)
    attn_band = attn.reshape(-1, group_width)
    partial_out = jnp.dot(attn_band, coarse_out, preferred_element_type=jnp.float32).reshape(
        images, half_rows, band_cols, width_coarse
    )
    projected = lax.psum_scatter(
        partial_out.astype(jnp.bfloat16), "col", scatter_dimension=2, tiled=True
    ).astype(jnp.float32)
    coarse_output = (coarse_float + projected).astype(jnp.bfloat16)
    weight_term = jnp.dot(attn_band.T, grad_band, preferred_element_type=jnp.float32)
    out_grad = lax.psum_scatter(
        weight_term.astype(jnp.bfloat16), "row", scatter_dimension=1, tiled=True
    ).astype(jnp.float32)
    key_grads = jnp.concatenate(
        [
            grad_kn.reshape(images, all_tokens, group_width),
            grad_v.reshape(images, all_tokens, group_width),
        ],
        axis=-1,
    )
    key_grads = lax.psum_scatter(
        key_grads.astype(jnp.bfloat16), "row", scatter_dimension=1, tiled=True
    ).astype(jnp.float32)
    grad_kn_band = key_grads[:, :, :group_width].reshape(
        images, band_tokens, heads_local, head_size
    )
    grad_v2 = key_grads[:, :, group_width:].astype(jnp.bfloat16).reshape(-1, group_width)
    grad_q2 = norm_back(query_f, grad_qn).astype(jnp.bfloat16).reshape(-1, group_width)
    grad_k2 = norm_back(key_f, grad_kn_band).astype(jnp.bfloat16).reshape(-1, group_width)
    grads = [grad_q2, grad_k2, grad_v2]
    weight_grads = jnp.stack(
        [
            jnp.dot(band_flat.T, grads[index], preferred_element_type=jnp.float32)
            for index in range(3)
        ]
    )
    qkv_grad = lax.psum_scatter(
        weight_grads.astype(jnp.bfloat16), "row", scatter_dimension=1, tiled=True
    ).astype(jnp.float32)
    grad_normed = jnp.dot(grad_q2, coarse_qkv[0].T, preferred_element_type=jnp.float32)
    grad_normed = grad_normed + jnp.dot(
        grad_k2, coarse_qkv[1].T, preferred_element_type=jnp.float32
    )
    grad_normed = grad_normed + jnp.dot(
        grad_v2, coarse_qkv[2].T, preferred_element_type=jnp.float32
    )
    grad_normed = lax.psum_scatter(
        grad_normed.reshape(images, half_rows, band_cols, width_coarse).astype(jnp.bfloat16),
        "col",
        scatter_dimension=2,
        tiled=True,
    ).astype(jnp.float32)
    input_grad = cotangent.astype(jnp.float32) + norm_back(coarse_float, grad_normed * gain_coarse)
    return (coarse_output, input_grad, qkv_grad, out_grad)


def solution(mesh):
    return jax.shard_map(
        per_device,
        mesh=mesh,
        in_specs=(
            P(None, "row", "col", None),
            P(),
            P(),
            P(),
            P(),
            P(),
            P(),
            P(None, None, "col"),
            P("col", None),
            P("col"),
            P(None, "row", "col", None),
        ),
        out_specs=(
            P(None, "row", "col", None),
            P(None, "row", "col", None),
            P(None, "row", "col"),
            P("col", "row"),
        ),
        check_vma=False,
    )
```

profile of v0, /device:TPU:1, one launch (start us, length us, event | category | flops | bytes accessed | tf_op | source)
XLA Modules:
  0.0 632.4 jit_solution(216718003394802271)
XLA Ops:
  9.8 1.9 convolution_convert_fusion.5
  12.7 4.6 collective-permute-start
  17.5 1.9 collective-permute-start.1
  19.4 2.5 fusion.90
  26.9 2.2 constant_dynamic-update-slice_fusion.1
  29.5 3.6 collective-permute-start.2
  35.6 8.7 %collective-permute-done.2 = bf16[4,22,3,1024]{3,0,2,1:T(4,128)(2,1)S(1)} collective-permute-done((bf16[4,22,3,1024]{3,0,2,1:T(4,128)(2,1)S(1)}, bf16[4,22,3,1024]{3,0,2,1:T(4,128)(2,1)S(1)}, u32[]{:S(2)}, u32[]{:S(2)}) %collective-permute-start.2) | collective-permute-done | bytes 540704 | tf_op jit(solution)/shard_map/ppermute | solution.py:15
  44.3 4.1 collective-permute-done.3
  48.5 1.8 pad_maximum_fusion.1
  50.3 5.4 reshape.1997
  55.7 3.3 fusion.37
  59.9 4.3 convert_multiply_fusion.1
  64.2 18.1 %fusion.87 = (f32[4,16,8,8]{3,0,2,1:T(4,128)}, f32[4,16,8,8]{3,0,2,1:T(4,128)}, f32[4,16,8,8]{3,0,2,1:T(4,128)}, f32[4,16,8,8]{3,0,2,1:T(4,128)}, f32[4,16,8,8]{...) fusion(f32[4,22,14,8,64]{4,3,0,2,1:T(8,128)} %convert_multiply_, ...), kind=kLoop, calls=%fused_computation.153 | loop fusion | flops 7024640 | bytes 15958016 | tf_op jit(solution)/shard_map/reduce_sum | solution.py:46
  82.3 19.9 %fusion.89 = (f32[4,16,8,8]{3,0,2,1:T(4,128)S(1)}, f32[4,16,8,8]{3,0,2,1:T(4,128)S(1)}, f32[4,16,8,8]{3,0,2,1:T(4,128)S(1)}, f32[4,16,8,8]{3,0,2,1:T(4,128)S(1)}...) fusion(f32[4,16,8,8,64]{4,3,0,2,1:T(8,128)S(1)} %get-tuple-elem, ...), kind=kLoop, calls=%fused_computation.157 | loop fusion | flops 9363456 | bytes 20217856 | tf_op jit(solution)/shard_map/reduce_sum | solution.py:46
  102.3 12.8 %fusion.88 = (f32[4,16,8,8]{3,0,2,1:T(4,128)S(1)}, f32[4,16,8,8]{3,0,2,1:T(4,128)}, f32[4,16,8,8]{3,0,2,1:T(4,128)}, f32[4,16,8,8]{3,0,2,1:T(4,128)}, f32[4,16,8...) fusion(f32[4,16,8,8,64]{4,3,0,2,1:T(8,128)S(1)} %get-tuple-elem, ...), kind=kLoop, calls=%fused_computation.155 | loop fusion | flops 9363456 | bytes 20217856 | tf_op jit(solution)/shard_map/reduce_sum | solution.py:46
  117.6 14.3 %add_add_fusion = (f32[4,16,8,8]{3,0,2,1:T(4,128)S(1)}, f32[4,16,8,8]{3,0,2,1:T(4,128)S(1)}, f32[4,16,8,8]{3,0,2,1:T(4,128)S(1)}, f32[4,16,8,8]{3,0,2,1:T(4,128)...) fusion(f32[16,8]{1,0:T(8,128)} %get-tuple-element.375, ...), kind=kLoop, calls=%fused_computation.211 | loop fusion | flops 598016 | bytes 1647136 | tf_op jit(solution)/shard_map/add | solution.py:52
  131.9 31.4 %divide_convert_fusion = bf16[4,16,8,8,64]{4,3,0,2,1:T(8,128)(2,1)S(1)} fusion(bf16[4,22,14,8,64]{4,3,0,2,1:T(8,128)(2,1)S(1)} %slice_bitcast_fusion, f32[4,16,8,8]{3,0,2,1:T(4,128)S(1)} %get-tuple-element.272, f32[4,16,8,8]{3,0,2,1:T(4,128)} %get-tuple-element.321, f32[4,16,8,8]{3,0,2,1:T(4,128)} %get-tuple-element.320, ...), kind=kLoop, calls=%fused_computation.160 | loop fusion | flops 38797312 | bytes 27033600 | tf_op jit(solution)/shard_map/convert_element_type | solution.py:129
  165.4 3.0 multiply_reduce_fusion.5
  170.7 54.0 %all-gather.4.cloned.1.call-done = bf16[4,8,64,1024]{3,1,0,2:T(8,128)(2,1)} async-done(((bf16[4,8,4,1024]{3,1,0,2:T(8,128)(2,1)}), bf16[4,8,64,1024]{3,1,0,2:T(8,128)(2,1)}) %all-gather.4.cloned.1.call-update) | async-done | bytes 4194320 | tf_op jit(solution)/shard_map/all_gather | solution.py:149
  224.7 4.5 copy.144
  229.3 2.0 copy-done.2
  232.7 3.7 convolution_convert_fusion.3
  238.3 39.8 %all-gather.8.cloned.1.call-done = bf16[4,8,64,1024]{3,1,0,2:T(8,128)(2,1)} async-done(((bf16[4,8,4,1024]{3,1,0,2:T(8,128)(2,1)}), bf16[4,8,64,1024]{3,1,0,2:T(8,128)(2,1)}) %all-gather.8.cloned.1.call-update) | async-done | bytes 4194320 | tf_op jit(solution)/shard_map/all_gather | solution.py:178
  278.1 4.5 copy.149
  282.6 1.9 copy-done.4
  286.9 3.8 multiply_reduce_fusion.3
  291.2 20.7 %all-gather.6.cloned.1.call-done = bf16[4,4096,128]{1,2,0:T(8,128)(2,1)} async-done(((bf16[4,512,128]{1,2,0:T(8,128)(2,1)}), bf16[4,4096,128]{1,2,0:T(8,128)(2,1)}) %all-gather.6.cloned.1.call-update) | async-done | bytes 4194320 | tf_op jit(solution)/shard_map/all_gather | solution.py:172
  312.0 4.0 slice_bitcast_fusion.2
  315.9 39.7 %while.18 = (s32[]{:T(128)}, bf16[4,512,1,64]{1,3,2,0:T(8,128)(2,1)}, f32[4,512,1,64]{1,3,2,0:T(8,128)}, bf16[4,4096,1,64]{1,3,2,0:T(8,128)(2,1)}, bf16[4,4096,1...) while((s32[]{:T(128)}, ...), condition=%wide.region_58.59_spmd, body=%wide.region_55.58_spmd.sunk | while | flops 1629912064 | bytes 96292696 | solution.py:183
  321.3 1.6 multiply_convert_fusion.4
  323.8 2.1 fusion.175
  331.2 1.6 multiply_convert_fusion.4
  333.7 2.1 fusion.175
  343.6 2.1 fusion.175
  353.6 2.1 fusion.175
  355.6 1.9 fusion.40
  357.8 2.5 pad_maximum_fusion
  365.2 3.0 fusion.93
  368.3 4.5 fusion.110
  372.9 22.0 %reduce-scatter.12.cloned.1.call-done = bf16[4,512,128]{1,2,0:T(8,128)(2,1)} async-done(((bf16[4,4096,128]{1,2,0:T(8,128)(2,1)}), bf16[4,512,128]{1,2,0:T(8,128)(2,1)}) %reduce-scatter.12.cloned.1.call-update) | async-done | bytes 524304 | tf_op jit(solution)/shard_map/reduce_scatter | solution.py:208
  397.1 3.2 fusion.94
  405.0 4.7 add_convert_fusion
  409.6 4.3 copy.161
  416.1 4.3 copy.154
  420.3 7.0 %reduce-scatter.18.cloned.1.call-done = bf16[128,64]{1,0:T(8,128)(2,1)} async-done(((bf16[1024,64]{1,0:T(8,128)(2,1)}), bf16[128,64]{1,0:T(8,128)(2,1)}) %reduce-scatter.18.cloned.1.call-update) | async-done | bytes 16400
  428.8 31.2 %reduce-scatter.16.cloned.1.call-done = bf16[128,192]{1,0:T(8,128)(2,1)} async-done(((bf16[1024,192]{1,0:T(8,128)(2,1)}), bf16[128,192]{1,0:T(8,128)(2,1)}) %reduce-scatter.16.cloned.1.call-update) | async-done | bytes 49168
  461.8 79.3 %reduce-scatter.14.cloned.1.call-done = bf16[4,8,4,1024]{3,1,0,2:T(8,128)(2,1)} async-done(((bf16[4,8,64,1024]{3,1,0,2:T(8,128)(2,1)}), bf16[4,8,4,1024]{3,1,0,2:T(8,128)(2,1)}) %reduce-scatter.14.cloned.1.call-update) | async-done | bytes 262160 | tf_op jit(solution)/shard_map/reduce_scatter | solution.py:234
  542.4 79.4 %reduce-scatter.10.cloned.1.call-done = bf16[4,8,4,1024]{3,1,0,2:T(8,128)(2,1)} async-done(((bf16[4,8,64,1024]{3,1,0,2:T(8,128)(2,1)}), bf16[4,8,4,1024]{3,1,0,2:T(8,128)(2,1)}) %reduce-scatter.10.cloned.1.call-update) | async-done | bytes 262160 | tf_op jit(solution)/shard_map/reduce_scatter | solution.py:193
  (323 shorter events, 74.6 us)
Async XLA Ops:
  7.2 156.7 %copy-start = (bf16[512,512]{1,0:T(8,128)(2,1)S(1)}, bf16[512,512]{1,0:T(8,128)(2,1)}, u32[]{:S(2)}) copy-start(bf16[512,512]{1,0:T(8,128)(2,1)} %param.16) | copy-start | bytes 1572868
  7.2 217.5 %all-gather.4.cloned.1.call-start = ((), (), s32[]{:S(2)}) async-start(), calls=%async_computation.5 | async-start | bytes 4456448 | tf_op jit(solution)/shard_map/all_gather | solution.py:149
  11.7 10.2 %copy-start.19 = (bf16[512,1024]{1,0:T(8,128)(2,1)}, bf16[512,1024]{1,0:T(8,128)(2,1)S(1)}, u32[]{:S(2)}) copy-start(bf16[512,1024]{1,0:T(8,128)(2,1)S(1)} %convolution_convert_fusion.5) | copy-start | bytes 3145732
  12.7 13.2 %collective-permute-start = (bf16[4,3,8,1024]{3,0,2,1:T(4,128)(2,1)}, bf16[4,3,8,1024]{3,0,2,1:T(4,128)(2,1)}, u32[]{:S(2)}, u32[]{:S(2)}) collective-permute-start(bf16[4,3,8,1024]{3,0,2,1:T(4,128)(2,1)} %copy.209), channel_id=1, source_target_pairs={{0,16},{16,32},{32,48},{48,64},{64,80},{80,96},{96,112},{1,17},{17... | collective-permute-start | bytes 589832 | tf_op jit(solution)/shard_map/ppermute | solution.py:15
  17.5 11.6 %collective-permute-start.1 = (bf16[4,3,8,1024]{3,0,2,1:T(4,128)(2,1)S(1)}, bf16[4,3,8,1024]{3,0,2,1:T(4,128)(2,1)S(1)}, u32[]{:S(2)}, u32[]{:S(2)}) collective-permute-start(bf16[4,3,8,1024]{3,0,2,1:T(4,128)(2,1)S(1)} %copy.210), channel_id=1, source_target_pairs={{16,0},{32,16},{48,32},{64,48},{80,64},{96,80},{112,96},{17,1},{33... | collective-permute-start | bytes 589832 | tf_op jit(solution)/shard_map/ppermute | solution.py:17
  23.5 5.5 copy-start.6
  29.5 14.8 %collective-permute-start.2 = (bf16[4,22,3,1024]{3,0,2,1:T(4,128)(2,1)S(1)}, bf16[4,22,3,1024]{3,0,2,1:T(4,128)(2,1)S(1)}, u32[]{:S(2)}, u32[]{:S(2)}) collective-permute-start(bf16[4,22,3,1024]{3,0,2,1:T(4,128)(2,1)S(1)} %get-tuple-element.329), channel_id=1, source_target_pairs={{0,1},{1,2},{2,3},{3,4},{4,5},{5,6},{6,7},{7,8},{8,9},{9,10},{10,1... | collective-permute-start | bytes 1622024 | tf_op jit(solution)/shard_map/ppermute | solution.py:15
  33.1 15.3 %collective-permute-start.3 = (bf16[4,22,3,1024]{3,0,2,1:T(4,128)(2,1)S(1)}, bf16[4,22,3,1024]{3,0,2,1:T(4,128)(2,1)S(1)}, u32[]{:S(2)}, u32[]{:S(2)}) collective-permute-start(bf16[4,22,3,1024]{3,0,2,1:T(4,128)(2,1)S(1)} %get-tuple-element.330), channel_id=1, source_target_pairs={{1,0},{2,1},{3,2},{4,3},{5,4},{6,5},{7,6},{8,7},{9,8},{10,9},{11,1... | collective-permute-start | bytes 1622024 | tf_op jit(solution)/shard_map/ppermute | solution.py:17
  64.2 38.0 %slice-start = ((s8[5046272]{0:T(1024)(128)(4,1)}), s8[851968]{0:T(1024)(128)(4,1)S(1)}, s32[]{:S(2)}) async-start(s8[5046272]{0:T(1024)(128)(4,1)} %bitcast.238), calls=%async_computation.13 | async-start | bytes 1703936
  82.3 20.0 %slice-start.1 = ((s8[5046272]{0:T(1024)(128)(4,1)}), s8[4194304]{0:T(1024)(128)(4,1)S(1)}, s32[]{:S(2)}) async-start(s8[5046272]{0:T(1024)(128)(4,1)} %bitcast.238), calls=%async_computation.14 | async-start | bytes 8388608
  82.3 32.8 %slice-start.2 = ((s8[5046272]{0:T(1024)(128)(4,1)}), s8[4194304]{0:T(1024)(128)(4,1)S(1)}, s32[]{:S(2)}) async-start(s8[5046272]{0:T(1024)(128)(4,1)} %bitcast.248), calls=%async_computation.15 | async-start | bytes 8388608
  102.2 12.8 %slice-start.3 = ((s8[5046272]{0:T(1024)(128)(4,1)}), s8[851968]{0:T(1024)(128)(4,1)S(1)}, s32[]{:S(2)}) async-start(s8[5046272]{0:T(1024)(128)(4,1)} %bitcast.248), calls=%async_computation.16 | async-start | bytes 1703936
  115.2 2.2 copy-start.41
  115.3 2.2 copy-start.55
  115.3 2.2 copy-start.56
  115.3 2.2 copy-start.57
  115.3 2.2 copy-start.58
  115.3 2.2 copy-start.59
  115.3 2.2 copy-start.60
  115.3 2.2 copy-start.61
  115.3 2.2 copy-start.62
  115.3 2.2 copy-start.63
  131.9 32.0 %copy-start.14 = (bf16[4,16,8,512]{3,2,1,0:T(8,128)(2,1)S(1)}, bf16[4,16,8,512]{3,2,1,0:T(8,128)(2,1)}, u32[]{:S(2)}) copy-start(bf16[4,16,8,512]{3,2,1,0:T(8,128)(2,1)} %param.13) | copy-start | bytes 1572868
  165.3 3.4 copy-start.53
  168.5 60.7 %copy-start.10 = (f32[4,8,4,1024]{3,2,1,0:T(4,128)}, f32[4,8,4,1024]{3,2,1,0:T(4,128)S(1)}, u32[]{:S(2)}) copy-start(f32[4,8,4,1024]{3,2,1,0:T(4,128)S(1)} %reshape.2000) | copy-start | bytes 1572868
  168.7 60.5 %copy-start.49 = (f32[4,8,4]{1,0,2:T(4,128)}, f32[4,8,4]{1,0,2:T(4,128)S(1)}, u32[]{:S(2)}) copy-start(f32[4,8,4]{1,0,2:T(4,128)S(1)} %copy.142) | copy-start | bytes 1540
  169.8 108.3 %all-gather.8.cloned.1.call-start = ((), (), s32[]{:S(2)}) async-start(), calls=%async_computation.7 | async-start | bytes 4456448 | tf_op jit(solution)/shard_map/all_gather | solution.py:178
  170.7 60.6 %copy-start.20 = (bf16[3,1024,64]{1,2,0:T(8,128)(2,1)S(1)}, bf16[3,1024,64]{1,2,0:T(8,128)(2,1)}, u32[]{:S(2)}) copy-start(bf16[3,1024,64]{1,2,0:T(8,128)(2,1)} %param.20) | copy-start | bytes 1179652
  170.7 141.3 %all-gather.6.cloned.1.call-start = ((), (), s32[]{:S(2)}) async-start(), calls=%async_computation.6 | async-start | bytes 4718592 | tf_op jit(solution)/shard_map/all_gather | solution.py:172
  232.6 3.8 copy-start.8
  232.7 3.8 copy-start.51
  237.4 157.5 %reduce-scatter.12.cloned.1.call-start = ((), (), s32[]{:S(2)}) async-start(), calls=%async_computation.9 | async-start | bytes 4718592 | tf_op jit(solution)/shard_map/reduce_scatter | solution.py:208
  238.3 46.2 %copy-start.47 = (bf16[64,1024]{1,0:T(8,128)(2,1)S(1)}, bf16[64,1024]{1,0:T(8,128)(2,1)}, u32[]{:S(2)}) copy-start(bf16[64,1024]{1,0:T(8,128)(2,1)} %param.21) | copy-start | bytes 393220
  355.6 2.2 copy-start.18
  360.3 67.0 %reduce-scatter.18.cloned.1.call-start = ((), (), s32[]{:S(2)}) async-start(), calls=%async_computation.12 | async-start | bytes 294912
  361.3 2.2 copy-start.5
  368.3 26.6 %copy-start.9 = (f32[2048,64]{0,1:T(8,128)S(1)}, f32[2048,64]{0,1:T(8,128)}, u32[]{:S(2)}) copy-start(f32[2048,64]{0,1:T(8,128)} %copy-done.8) | copy-start | bytes 1572868
  368.3 26.6 %copy-start.52 = (f32[4,512]{1,0:T(4,128)S(1)}, f32[4,512]{1,0:T(4,128)}, u32[]{:S(2)}) copy-start(f32[4,512]{1,0:T(4,128)} %copy-done.51) | copy-start | bytes 24580
  372.8 87.2 %reduce-scatter.16.cloned.1.call-start = ((), (), s32[]{:S(2)}) async-start(), calls=%async_computation.11 | async-start | bytes 589824
  397.0 3.2 copy-start.22
  397.0 3.6 copy-start.3
  403.6 137.4 %reduce-scatter.14.cloned.1.call-start = ((), (), s32[]{:S(2)}) async-start(), calls=%async_computation.10 | async-start | bytes 4456448 | tf_op jit(solution)/shard_map/reduce_scatter | solution.py:234
  413.9 207.8 %reduce-scatter.10.cloned.1.call-start = ((), (), s32[]{:S(2)}) async-start(), calls=%async_computation.8 | async-start | bytes 4456448 | tf_op jit(solution)/shard_map/reduce_scatter | solution.py:193
  420.3 120.7 %copy-start.11 = (f32[4,8,4,1024]{3,2,1,0:T(4,128)S(1)}, f32[4,8,4,1024]{3,2,1,0:T(4,128)}, u32[]{:S(2)}) copy-start(f32[4,8,4,1024]{3,2,1,0:T(4,128)} %copy-done.10) | copy-start | bytes 1572868
  420.3 120.7 %copy-start.50 = (f32[4,8,4]{1,0,2:T(4,128)S(1)}, f32[4,8,4]{1,0,2:T(4,128)}, u32[]{:S(2)}) copy-start(f32[4,8,4]{1,0,2:T(4,128)} %copy-done.49) | copy-start | bytes 1540
  420.3 120.7 %copy-start.54 = (f32[1024]{0:T(1024)S(1)}, f32[1024]{0:T(1024)}, u32[]{:S(2)}) copy-start(f32[1024]{0:T(1024)} %param.19) | copy-start | bytes 12292
  420.3 201.5 %copy-start.46 = (bf16[4,8,4,1024]{3,2,1,0:T(4,128)(2,1)S(1)}, bf16[4,8,4,1024]{3,2,1,0:T(4,128)(2,1)}, u32[]{:S(2)}) copy-start(bf16[4,8,4,1024]{3,2,1,0:T(4,128)(2,1)} %param.23) | copy-start | bytes 786436
  461.1 164.2 %copy-start.1 = (bf16[512,512]{1,0:T(8,128)(2,1)S(1)}, bf16[512,512]{1,0:T(8,128)(2,1)}, u32[]{:S(2)}) copy-start(bf16[512,512]{1,0:T(8,128)(2,1)} %param.16) | copy-start | bytes 1572868
  (63 other events, 103.5 us)
Sparse Core Ops, SparseCore 0:
  169.9 54.7 all-gather.3
  226.8 51.2 all-gather.7
  279.8 32.1 all-gather.5
  360.5 34.3 reduce-scatter.11
  397.6 29.6 reduce-scatter.17
  430.3 29.7 reduce-scatter.15
  463.4 77.6 reduce-scatter.13
  544.7 76.9 reduce-scatter.9
where the time goes:
time: 639 us; the launch traced here: 632 us
  waiting for transfers between devices  346 us (54%)
  other arithmetic  122 us (19%)
  matrix products  71 us (11%)
  local copies, waits for them, and re-layouts  64.2 us (10%)
  between operations  16.2 us (3%)
  starting transfers between devices  12.5 us (2%)
    reduce_scatter x1, waiting for transfers between devices, per_device(): lax.psum_scatter(partial_out.astype(jnp.bfloat16), 'col', scatter_dimensi...  79.4 us
    reduce_scatter x1, waiting for transfers between devices, per_device(): lax.psum_scatter(grad_normed.reshape(images, half_rows, band_cols, width_...  79.3 us
    all_gather x1, waiting for transfers between devices, per_device(): band = lax.all_gather(coarse_normed, 'col', axis=2, tiled=True)  54 us
    reduce_sum x3, other arithmetic, neighbour_attention(): scores = jnp.sum(queries * keys_here, axis=-1) * head_scale  50.8 us
    all_gather x1, waiting for transfers between devices, per_device(): lax.all_gather(cotangent, 'col', axis=2, tiled=True)  39.8 us
    unnamed x10, waiting for transfers between devices  38.4 us
    convert_element_type x1, other arithmetic, per_device(): mixed = neighbour_attention(queries, keys_wide, values_wide, row_inside,...  31.4 us
    reduce_scatter x1, waiting for transfers between devices, per_device(): lax.psum_scatter(key_grads.astype(jnp.bfloat16), 'row', scatter_dimension...  22 us
  transfers between devices with their start and end apart: 12, of which 10 were waited for; matrix products, arithmetic and copies ran while one was open for 11% of the time, Pallas kernels for 0%

commit v1 on v0

--- a/solution.py
+++ b/solution.py
@@ -1,24 +1,190 @@
+import functools
+
 import jax
 import jax.numpy as jnp
+import numpy as np
 from jax import lax
+from jax.experimental import pallas as pl
+from jax.experimental.pallas import tpu as pltpu
 from jax.sharding import PartitionSpec as P
 
-
-def padded(cells, sides, width):
-    for axis, dim in sides:
-        count = lax.axis_size(axis)
-        ends = count - 1
-        head = lax.slice_in_dim(cells, 0, width, axis=dim)
-        tail = lax.slice_in_dim(cells, cells.shape[dim] - width, cells.shape[dim], axis=dim)
-        cells = jnp.concatenate(
-            [
-                lax.ppermute(tail, axis, [(i, (i + 1) % count) for i in range(ends)]),
-                cells,
-                lax.ppermute(head, axis, [((i + 1) % count, i) for i in range(ends)]),
-            ],
-            axis=dim,
+MESH = pl.DeviceIdType.MESH
+F32 = jnp.float32
+BF16 = jnp.bfloat16
+SEG = ((128, 48), (176, 48), (224, 32), (256, 32), (288, 16), (304, 16), (320, 16), (336, 16))
+WAY = ((0, 1), (0, -1), (1, 0), (-1, 0), (1, 1), (1, -1), (-1, 1), (-1, -1))
+KEYS = 384
+
+
+def dot(a, b):
+    return jnp.dot(a, b, preferred_element_type=F32)
+
+
+def dot_nt(a, b):
+    return lax.dot_general(a, b, (((1,), (1,)), ((), ())), preferred_element_type=F32)
+
+
+def fine_tables():
+    sel = np.zeros((KEYS, 128), np.float32)
+    place = np.full((8, KEYS), 10000, np.int32)
+    query = np.zeros((256, 128), np.int32)
+    for p in range(4):
+        for u in range(8):
+            for w in range(4):
+                n = p * 32 + u * 4 + w
+                i, j = 2 * u + p // 2, 2 * w + p % 2
+                sel[n, i * 8 + j] = 1
+                place[0, n], place[1, n] = i, j
+                query[n, 0] = query[n + 128, 0] = i
+                query[n, 1] = query[n + 128, 1] = j
+    for (start, _), (down, right) in zip(SEG, WAY):
+        rows = {0: range(16), 1: range(13, 16), -1: range(3)}[down]
+        cols = {0: range(8), 1: range(5, 8), -1: range(3)}[right]
+        n = start
+        for i in rows:
+            for j in cols:
+                sel[n, i * 8 + j] = 1
+                place[0, n], place[1, n] = i - 16 * down, j - 8 * right
+                n += 1
+    return sel, place, query
+
+
+def fine_kernel(
+    x_ref, sel_ref, place_ref, query_ref, gain_ref, wqkv_ref, wout_ref, scale_ref, wmerge_ref, gain2_ref,
+    in_ref, normed_ref,
+    keys_in, send, kn, vv, qn, fr, bias, send_sem, recv_sem,
+):
+    row, col = lax.axis_index("row"), lax.axis_index("col")
+    barrier = pltpu.get_barrier_semaphore()
+    peers = [(lax.rem(row + a + 8, 8), lax.rem(col + b + 16, 16)) for a, b in WAY]
+    for peer in peers:
+        pl.semaphore_signal(barrier, inc=1, device_id=peer, device_id_type=MESH)
+
+    @pl.loop(0, 4)
+    def _(img):
+        packed = dot(sel_ref[...], x_ref[img]).astype(BF16)
+        keys_in[img, 0:128, :] = packed[0:128]
+        send[img] = packed[128:352]
+        keys_in[img, 352:384, :] = packed[352:384]
+
+    pl.semaphore_wait(barrier, 8)
+    copies = []
+    for k, ((start, size), peer) in enumerate(zip(SEG, peers)):
+        copy = pltpu.make_async_remote_copy(
+            src_ref=send.at[:, start - 128 : start - 128 + size, :],
+            dst_ref=keys_in.at[:, start : start + size, :],
+            send_sem=send_sem.at[k],
+            recv_sem=recv_sem.at[k],
+            device_id=peer,
+            device_id_type=MESH,
         )
-    return cells
+        copy.start()
+        copies.append(copy)
+
+    seen = (
+        (jnp.abs(place_ref[0:1, :] - query_ref[:, 0:1]) <= 3)
+        & (jnp.abs(place_ref[1:2, :] - query_ref[:, 1:2]) <= 3)
+    )
+    gi = place_ref[0:1, :] + row * 16
+    gj = place_ref[1:2, :] + col * 8
+    inside = (gi >= 0) & (gi < 128) & (gj >= 0) & (gj < 128)
+    bias[...] = jnp.where(seen & inside, 0.0, -1e30).astype(F32)
+
+    lane = lax.broadcasted_iota(jnp.int32, (128, 128), 1)
+    sub = lax.broadcasted_iota(jnp.int32, (128, 128), 0)
+    same = jnp.where((lane < 64) == (sub < 64), 1.0 / 64, 0.0).astype(BF16)
+
+    def token_norm(tokens):
+        xf = tokens.astype(F32)
+        factor = lax.rsqrt(jnp.mean(xf * xf, axis=-1, keepdims=True) + 1e-06)
+        return (xf * factor * gain_ref[...]).astype(BF16)
+
+    def head_norm(values):
+        vf = values.astype(BF16).astype(F32)
+        sq = (vf * vf).astype(BF16)
+        parts = [dot(sq[:, k * 128 : k * 128 + 128], same) for k in range(4)]
+        return vf * lax.rsqrt(jnp.concatenate(parts, axis=1) + 1e-06)
+
+    @pl.loop(0, 4)
+    def _(img):
+        nx = token_norm(keys_in[img, 0:128, :])
+        qn[img] = (head_norm(dot(nx, wqkv_ref[:, 0:512])) * scale_ref[...]).astype(BF16)
+        kn[img, 0:128, :] = head_norm(dot(nx, wqkv_ref[:, 512:1024])).astype(BF16)
+        vv[img, 0:128, :] = dot(nx, wqkv_ref[:, 1024:1536]).astype(BF16)
+
+    for copy in copies:
+        copy.wait()
+
+    @pl.loop(0, 4)
+    def _(img):
+        nx = token_norm(keys_in[img, 128:384, :])
+        kn[img, 128:384, :] = head_norm(dot(nx, wqkv_ref[:, 512:1024])).astype(BF16)
+        vv[img, 128:384, :] = dot(nx, wqkv_ref[:, 1024:1536]).astype(BF16)
+
+    ones = jnp.ones((KEYS, 128), BF16)
+
+    @pl.loop(0, 4)
+    def _(img):
+        mixed = []
+        for pair in range(4):
+            at = slice(pair * 128, pair * 128 + 128)
+            q = qn[img, :, at]
+            zero = jnp.zeros_like(q)
+            both = jnp.concatenate([jnp.where(lane < 64, q, zero), jnp.where(lane < 64, zero, q)], axis=0)
+            powered = jnp.exp(dot_nt(both, kn[img, :, at]) + bias[...]).astype(BF16)
+            sums = dot(powered, jnp.concatenate([vv[img, :, at], ones], axis=1))
+            ratio = sums[:, 0:128] / sums[:, 128:256]
+            mixed.append(jnp.where(lane < 64, ratio[0:128], ratio[128:256]).astype(BF16))
+        mix = jnp.concatenate(mixed, axis=1)
+        fr[img] = (keys_in[img, 0:128, :].astype(F32) + dot(mix, wout_ref[...])).astype(BF16)
+
+    merged = jnp.zeros((128, 1024), F32)
+    for p in range(4):
+        part = jnp.concatenate([fr[img, p * 32 : p * 32 + 32, :] for img in range(4)], axis=0)
+        merged = merged + dot(part, wmerge_ref[p * 512 : p * 512 + 512, :])
+    inner = merged.astype(BF16)
+    in_ref[...] = inner
+    xf = inner.astype(F32)
+    factor = lax.rsqrt(jnp.mean(xf * xf, axis=-1, keepdims=True) + 1e-06)
+    normed_ref[...] = (xf * factor * gain2_ref[...]).astype(BF16)
+
+
+def fine_level(x, gain, wqkv, wout, scale, wmerge, gain2):
+    sel, place, query = fine_tables()
+    vmem = pl.BlockSpec(memory_space=pltpu.VMEM)
+    return pl.pallas_call(
+        fine_kernel,
+        out_shape=(jax.ShapeDtypeStruct((128, 1024), BF16),) * 2,
+        in_specs=[vmem] * 10,
+        out_specs=(vmem,) * 2,
+        scratch_shapes=[
+            pltpu.VMEM((4, KEYS, 512), BF16),
+            pltpu.VMEM((4, 224, 512), BF16),
+            pltpu.VMEM((4, KEYS, 512), BF16),
+            pltpu.VMEM((4, KEYS, 512), BF16),
+            pltpu.VMEM((4, 128, 512), BF16),
+            pltpu.VMEM((4, 128, 512), BF16),
+            pltpu.VMEM((256, KEYS), F32),
+            pltpu.SemaphoreType.DMA((8,)),
+            pltpu.SemaphoreType.DMA((8,)),
+        ],
+        compiler_params=pltpu.CompilerParams(
+            collective_id=0, has_side_effects=True, vmem_limit_bytes=48 * 1024 * 1024
+        ),
+        cost_estimate=pl.CostEstimate(flops=6_000_000_000, bytes_accessed=8_000_000, transcendentals=2_000_000),
+        name="fine_level",
+    )(
+        x.reshape(4, 128, 512),
+        jnp.asarray(sel, BF16),
+        jnp.asarray(place),
+        jnp.asarray(query),
+        gain.reshape(1, 512),
+        wqkv,
+        wout,
+        jnp.repeat(scale / 64, 64).reshape(1, 512),
+        wmerge,
+        gain2.reshape(1, 1024),
+    )
 
 
 def normalize(values):
@@ -29,29 +195,6 @@
     factor = lax.rsqrt(jnp.mean(values * values, axis=-1, keepdims=True) + 1e-06)
     unit = values * factor
     return factor * (upstream - unit * jnp.mean(upstream * unit, axis=-1, keepdims=True))
-
-
-def neighbour_attention(queries, keys_wide, values_wide, row_inside, col_inside, scales):
-    rows = queries.shape[1]
-    cols = queries.shape[2]
-    head_scale = scales / queries.shape[-1]
-    totals = jnp.zeros(queries.shape[:4], jnp.float32)
-    weighted = jnp.zeros(queries.shape, jnp.float32)
-    for row_off in range(7):
-        for col_off in range(7):
-            keys_here = keys_wide[:, row_off : row_off + rows, col_off : col_off + cols]
-            values_here = values_wide[:, row_off : row_off + rows, col_off : col_off + cols].astype(
-                jnp.float32
-            )
-            scores = jnp.sum(queries * keys_here, axis=-1) * head_scale
-            inside = (
-                row_inside[row_off : row_off + rows][:, None]
-                * col_inside[col_off : col_off + cols][None, :]
-            )
-            powered = jnp.exp(scores) * inside[None, :, :, None]
-            totals = totals + powered
-            weighted = weighted + powered[..., None] * values_here
-    return weighted / totals[..., None]
 
 
 def attend(queries, keys, values, grads, scales):
@@ -97,55 +240,14 @@
     cotangent,
 ):
     images, tile_rows, tile_cols, width_fine = fine_input.shape
-    heads_fine = fine_scale.shape[0]
-    head_size = width_fine // heads_fine
-    inputs = fine_input.astype(jnp.float32)
-    normed = (normalize(inputs) * gain_fine).astype(jnp.bfloat16)
-    flat_fine = normed.reshape(-1, width_fine)
-    queries = jnp.dot(
-        flat_fine, fine_qkv[:, :width_fine], preferred_element_type=jnp.float32
-    ).astype(jnp.bfloat16)
-    queries = normalize(
-        queries.astype(jnp.float32).reshape(images, tile_rows, tile_cols, heads_fine, head_size)
-    )
-    key_value = jnp.dot(
-        flat_fine, fine_qkv[:, width_fine:], preferred_element_type=jnp.float32
-    ).astype(jnp.bfloat16)
-    key_value = key_value.reshape(images, tile_rows, tile_cols, 2 * width_fine)
-    key_value = padded(key_value, (("row", 1), ("col", 2)), 3)
-    key_value = key_value.reshape(images, tile_rows + 6, tile_cols + 6, 2, heads_fine, head_size)
-    keys_wide = normalize(key_value[:, :, :, 0].astype(jnp.float32))
-    values_wide = key_value[:, :, :, 1]
-    row_place = lax.axis_index("row") * tile_rows + jnp.arange(tile_rows + 6, dtype=jnp.int32) - 3
-    col_place = lax.axis_index("col") * tile_cols + jnp.arange(tile_cols + 6, dtype=jnp.int32) - 3
-    row_inside = ((row_place >= 0) & (row_place < tile_rows * lax.axis_size("row"))).astype(
-        jnp.float32
-    )
-    col_inside = ((col_place >= 0) & (col_place < tile_cols * lax.axis_size("col"))).astype(
-        jnp.float32
-    )
-    mixed = neighbour_attention(
-        queries, keys_wide, values_wide, row_inside, col_inside, fine_scale
-    ).astype(jnp.bfloat16)
-    fine_result = (
-        inputs
-        + jnp.dot(
-            mixed.reshape(-1, width_fine), fine_out, preferred_element_type=jnp.float32
-        ).reshape(inputs.shape)
-    ).astype(jnp.bfloat16)
-    half_rows = tile_rows // 2
-    half_cols = tile_cols // 2
-    merged = (
-        fine_result.reshape(images, half_rows, 2, half_cols, 2, width_fine)
-        .transpose(0, 1, 3, 2, 4, 5)
-        .reshape(-1, 4 * width_fine)
-    )
+    head_size = 64
+    half_rows, half_cols = tile_rows // 2, tile_cols // 2
     width_coarse = merge_weight.shape[1]
-    coarse_in = jnp.dot(merged, merge_weight, preferred_element_type=jnp.float32).astype(
-        jnp.bfloat16
+    coarse_in, coarse_normed = fine_level(
+        fine_input, gain_fine, fine_qkv, fine_out, fine_scale, merge_weight, gain_coarse
     )
     coarse_float = coarse_in.astype(jnp.float32).reshape(images, half_rows, half_cols, width_coarse)
-    coarse_normed = (normalize(coarse_float) * gain_coarse).astype(jnp.bfloat16)
+    coarse_normed = coarse_normed.reshape(images, half_rows, half_cols, width_coarse)
     band = lax.all_gather(coarse_normed, "col", axis=2, tiled=True)
     band_cols = band.shape[2]
     band_tokens = half_rows * band_cols

time: 639 us -> 514 us (0.80)
  other arithmetic: 122 us -> 11.7 us
  Pallas kernels: 0 us -> 27.4 us
  waiting for transfers between devices: 346 us -> 331 us
  starting transfers between devices: 12.5 us -> 1.18 us
  local copies, waits for them, and re-layouts: 64.2 us -> 55.6 us
  matrix products: 71 us -> 62.9 us
    reduce_sum x6 -> x1, other arithmetic: 56 us -> 0.13 us  [norm_back(): jnp.mean(values * values, axis=-1, keepdims=True) + 1e-06]
    convert_element_type x5 -> x0, other arithmetic: 33.6 us -> none  [the longest x1 31.4 us: per_device(): mixed = neighbour_attention(queries, keys_wide, values_wide, row_inside,...]
    pallas_call x0 -> x1, Pallas kernels: none -> 27.4 us  [fine_level(): pl.pallas_call(fine_kernel, out_shape=(jax.ShapeDtypeStruct((128, 1024),...]
    add x1 -> x0, other arithmetic: 14.3 us -> none  [neighbour_attention(): totals = totals + powered]
    ppermute x4 -> x0, waiting for transfers between devices: 12.8 us -> none  [the longest x2 8.69 us: padded(): lax.ppermute(tail, axis, [(i, (i + 1) % count) for i in range(ends)])]
    ppermute x4 -> x0, starting transfers between devices: 11.5 us -> none  [the longest x2 8.16 us: padded(): lax.ppermute(tail, axis, [(i, (i + 1) % count) for i in range(ends)])]
    dot_general x4 -> x0, matrix products: 7.89 us -> none  [the longest x1 2.99 us: per_device(): jnp.dot(merged, merge_weight, preferred_element_type=jnp.float32)]
    reshape x5 -> x2, local copies, waits for them, and re-layouts: 8.03 us -> 0.89 us  [per_device(): coarse_normed.reshape(images, half_rows, half_cols, width_coarse)]
  transfers between devices with their start and end apart: 12 -> 8, of which waited for: 10 -> 8; matrix products, arithmetic and copies ran while one was open for 11% -> 12% of each run, Pallas kernels for 0% -> 0%
where the time goes in v1:
time: 514 us; the launch traced here: 506 us
  waiting for transfers between devices  331 us (64%)
  matrix products  62.9 us (12%)
  local copies, waits for them, and re-layouts  55.6 us (11%)
  Pallas kernels  27.4 us (5%)
  between operations  15.5 us (3%)
  other arithmetic  11.7 us (2%)
    reduce_scatter x1, waiting for transfers between devices, per_device(): lax.psum_scatter(grad_normed.reshape(images, half_rows, band_cols, width_...  79.5 us
    reduce_scatter x1, waiting for transfers between devices, per_device(): lax.psum_scatter(partial_out.astype(jnp.bfloat16), 'col', scatter_dimensi...  79.4 us
    all_gather x1, waiting for transfers between devices, per_device(): band = lax.all_gather(coarse_normed, 'col', axis=2, tiled=True)  50.3 us
    unnamed x10, waiting for transfers between devices  38.1 us
    all_gather x1, waiting for transfers between devices, per_device(): lax.all_gather(cotangent, 'col', axis=2, tiled=True)  35.5 us
    pallas_call x1, Pallas kernels, fine_level(): pl.pallas_call(fine_kernel, out_shape=(jax.ShapeDtypeStruct((128, 1024),...  27.4 us
    all_gather x1, waiting for transfers between devices, per_device(): key_value_all = lax.all_gather(key_value_band, 'row', axis=1, tiled=True)  25.6 us
    reduce_scatter x1, waiting for transfers between devices, per_device(): lax.psum_scatter(key_grads.astype(jnp.bfloat16), 'row', scatter_dimension...  22.7 us
  transfers between devices with their start and end apart: 8, of which 8 were waited for; matrix products, arithmetic and copies ran while one was open for 12% of the time, Pallas kernels for 0%

profile of v1, /device:TPU:1, one launch (start us, length us, event | category | flops | bytes accessed | tf_op | source)
XLA Modules:
  0.0 505.6 jit_solution(14118195434672995356)
XLA Ops:
  8.8 1.4 copy-done.3
  15.4 27.4 %fine_level.1 = (bf16[128,1024]{1,0:T(8,128)(2,1)S(1)}, bf16[128,1024]{1,0:T(8,128)(2,1)S(1)}) custom-call(bf16[4,128,512]{2,1,0:T(8,128)(2,1)S(1)} %bitcast.211, bf16[384,128]{1,0:T(8,128)(2,1)S(1)} %copy-done.8, s32[8,384]{1,0:T(8,128)S(1)} %copy-done.9, s32[256,128]{1,0:T(8,128)S(1)} %copy-done.7, f32[1,512]{1,0:T(1,128)S(1)} %bitcast.212, ...), custom_call_target="tpu_custom_call" | custom-call | flops 6000000000 | bytes 8000000 | tf_op jit(solution)/shard_map/fine_level/pallas_call | solution.py:155
  44.7 50.3 %all-gather.4.cloned.1.call-done = bf16[4,8,64,1024]{3,1,0,2:T(8,128)(2,1)} async-done(((bf16[4,8,4,1024]{3,1,0,2:T(8,128)(2,1)}), bf16[4,8,64,1024]{3,1,0,2:T(8,128)(2,1)}) %all-gather.4.cloned.1.call-update) | async-done | bytes 4194320 | tf_op jit(solution)/shard_map/all_gather | solution.py:251
  95.0 4.5 copy.62
  99.5 2.0 copy-done.10
  101.5 1.4 multiply_reduce_fusion.4
  103.0 3.7 convolution_convert_fusion.3
  108.9 3.6 multiply_reduce_fusion.3
  112.9 35.5 %all-gather.8.cloned.1.call-done = bf16[4,8,64,1024]{3,1,0,2:T(8,128)(2,1)} async-done(((bf16[4,8,4,1024]{3,1,0,2:T(8,128)(2,1)}), bf16[4,8,64,1024]{3,1,0,2:T(8,128)(2,1)}) %all-gather.8.cloned.1.call-update) | async-done | bytes 4194320 | tf_op jit(solution)/shard_map/all_gather | solution.py:280
  148.4 4.5 copy.67
  152.9 1.9 copy-done.12
  154.9 1.4 convolution_convert_fusion.1
  156.7 25.6 %all-gather.6.cloned.1.call-done = bf16[4,4096,128]{1,2,0:T(8,128)(2,1)} async-done(((bf16[4,512,128]{1,2,0:T(8,128)(2,1)}), bf16[4,4096,128]{1,2,0:T(8,128)(2,1)}) %all-gather.6.cloned.1.call-update) | async-done | bytes 4194320 | tf_op jit(solution)/shard_map/all_gather | solution.py:274
  182.3 3.9 slice_bitcast_fusion
  186.2 42.5 %while.18 = (s32[]{:T(128)}, bf16[4,512,1,64]{1,3,2,0:T(8,128)(2,1)}, f32[4,512,1,64]{1,3,2,0:T(8,128)}, bf16[4,4096,1,64]{1,3,2,0:T(8,128)(2,1)}, bf16[4,4096,1...) while((s32[]{:T(128)}, ...), condition=%wide.region_5.6_spmd, body=%wide.region_2.5_spmd.sunk | while | flops 1629912064 | bytes 95244088 | solution.py:285
  186.2 1.4 fusion.105
  190.1 1.4 bitcast_dynamic-update-slice_fusion.2
  192.2 1.6 multiply_convert_fusion.3
  194.8 2.1 fusion.107
  196.8 1.4 fusion.105
  200.7 1.4 bitcast_dynamic-update-slice_fusion.2
  202.9 1.6 multiply_convert_fusion.3
  205.4 2.1 fusion.107
  207.4 1.4 fusion.105
  211.3 1.4 bitcast_dynamic-update-slice_fusion.2
  213.5 1.6 multiply_convert_fusion.3
  216.0 2.1 fusion.107
  218.1 1.4 fusion.105
  222.0 1.4 bitcast_dynamic-update-slice_fusion.2
  224.1 1.6 multiply_convert_fusion.3
  226.6 2.1 fusion.107
  228.7 1.9 fusion.39
  230.9 2.4 pad_maximum_fusion
  237.5 3.0 fusion.40
  240.6 4.6 fusion.50
  245.2 22.7 %reduce-scatter.12.cloned.1.call-done = bf16[4,512,128]{1,2,0:T(8,128)(2,1)} async-done(((bf16[4,4096,128]{1,2,0:T(8,128)(2,1)}), bf16[4,512,128]{1,2,0:T(8,128)(2,1)}) %reduce-scatter.12.cloned.1.call-update) | async-done | bytes 524304 | tf_op jit(solution)/shard_map/reduce_scatter | solution.py:310
  269.2 1.3 fusion.48
  270.5 3.0 fusion.41
  275.2 1.4 reshape.329
  278.0 4.7 add_convert_fusion
  282.6 4.3 copy.80
  288.7 4.4 copy.72
  293.6 6.8 %reduce-scatter.18.cloned.1.call-done = bf16[128,64]{1,0:T(8,128)(2,1)} async-done(((bf16[1024,64]{1,0:T(8,128)(2,1)}), bf16[128,64]{1,0:T(8,128)(2,1)}) %reduce-scatter.18.cloned.1.call-update) | async-done | bytes 16400
  301.9 31.2 %reduce-scatter.16.cloned.1.call-done = bf16[128,192]{1,0:T(8,128)(2,1)} async-done(((bf16[1024,192]{1,0:T(8,128)(2,1)}), bf16[128,192]{1,0:T(8,128)(2,1)}) %reduce-scatter.16.cloned.1.call-update) | async-done | bytes 49168
  334.7 79.5 %reduce-scatter.14.cloned.1.call-done = bf16[4,8,4,1024]{3,1,0,2:T(8,128)(2,1)} async-done(((bf16[4,8,64,1024]{3,1,0,2:T(8,128)(2,1)}), bf16[4,8,4,1024]{3,1,0,2:T(8,128)(2,1)}) %reduce-scatter.14.cloned.1.call-update) | async-done | bytes 262160 | tf_op jit(solution)/shard_map/reduce_scatter | solution.py:336
  414.2 1.4 multiply_reduce_fusion
  415.6 79.4 %reduce-scatter.10.cloned.1.call-done = bf16[4,8,4,1024]{3,1,0,2:T(8,128)(2,1)} async-done(((bf16[4,8,64,1024]{3,1,0,2:T(8,128)(2,1)}), bf16[4,8,4,1024]{3,1,0,2:T(8,128)(2,1)}) %reduce-scatter.10.cloned.1.call-update) | async-done | bytes 262160 | tf_op jit(solution)/shard_map/reduce_scatter | solution.py:295
  495.0 1.5 multiply_add_fusion
  (187 shorter events, 43.3 us)
Async XLA Ops:
  7.2 147.7 %copy-start = (bf16[64,1024]{1,0:T(8,128)(2,1)S(1)}, bf16[64,1024]{1,0:T(8,128)(2,1)}, u32[]{:S(2)}) copy-start(bf16[64,1024]{1,0:T(8,128)(2,1)} %param.24) | copy-start | bytes 393220
  7.2 87.8 %all-gather.4.cloned.1.call-start = ((), (), s32[]{:S(2)}) async-start(), calls=%async_computation.5 | async-start | bytes 4456448 | tf_op jit(solution)/shard_map/all_gather | solution.py:251
  8.8 1.4 copy-start.3
  15.4 28.3 %copy-start.29 = (bf16[4,8,4,1024]{3,2,1,0:T(4,128)(2,1)S(1)}, bf16[4,8,4,1024]{3,2,1,0:T(4,128)(2,1)}, u32[]{:S(2)}) copy-start(bf16[4,8,4,1024]{3,2,1,0:T(4,128)(2,1)} %param.26) | copy-start | bytes 786436
  43.7 104.7 %all-gather.8.cloned.1.call-start = ((), (), s32[]{:S(2)}) async-start(), calls=%async_computation.7 | async-start | bytes 4456448 | tf_op jit(solution)/shard_map/all_gather | solution.py:280
  44.6 56.9 %copy-start.23 = (bf16[3,1024,64]{1,2,0:T(8,128)(2,1)S(1)}, bf16[3,1024,64]{1,2,0:T(8,128)(2,1)}, u32[]{:S(2)}) copy-start(bf16[3,1024,64]{1,2,0:T(8,128)(2,1)} %param.23) | copy-start | bytes 1179652
  44.6 137.7 %all-gather.6.cloned.1.call-start = ((), (), s32[]{:S(2)}) async-start(), calls=%async_computation.6 | async-start | bytes 4718592 | tf_op jit(solution)/shard_map/all_gather | solution.py:274
  99.5 2.0 copy-start.10
  102.9 4.8 copy-start.15
  102.9 4.7 copy-start.31
  107.7 160.2 %reduce-scatter.12.cloned.1.call-start = ((), (), s32[]{:S(2)}) async-start(), calls=%async_computation.9 | async-start | bytes 4718592 | tf_op jit(solution)/shard_map/reduce_scatter | solution.py:310
  152.9 1.9 copy-start.12
  186.2 1.6 copy-start.20
  187.8 2.3 copy-start.14
  187.8 2.3 copy-start.26
  188.8 1.3 copy-start.21
  192.2 1.7 copy-start.17
  194.7 2.1 copy-start.18
  196.8 1.6 copy-start.20
  198.4 2.3 copy-start.14
  198.4 2.3 copy-start.26
  199.4 1.3 copy-start.21
  202.9 1.7 copy-start.17
  205.4 2.1 copy-start.18
  207.4 1.6 copy-start.20
  209.0 2.3 copy-start.14
  209.0 2.3 copy-start.26
  213.5 1.7 copy-start.17
  216.0 2.1 copy-start.18
  218.1 1.6 copy-start.20
  219.7 2.3 copy-start.14
  219.7 2.3 copy-start.26
  224.1 1.7 copy-start.17
  226.6 2.1 copy-start.18
  228.7 2.2 copy-start.22
  233.4 1.7 copy-start.28
  233.4 67.0 %reduce-scatter.18.cloned.1.call-start = ((), (), s32[]{:S(2)}) async-start(), calls=%async_computation.12 | async-start | bytes 294912
  233.6 2.2 copy-start.13
  235.9 4.7 copy-start.24
  240.6 27.3 %copy-start.16 = (f32[2048,64]{0,1:T(8,128)S(1)}, f32[2048,64]{0,1:T(8,128)}, u32[]{:S(2)}) copy-start(f32[2048,64]{0,1:T(8,128)} %copy-done.15) | copy-start | bytes 1572868
  240.6 27.3 %copy-start.32 = (f32[4,512]{1,0:T(4,128)S(1)}, f32[4,512]{1,0:T(4,128)}, u32[]{:S(2)}) copy-start(f32[4,512]{1,0:T(4,128)} %copy-done.31) | copy-start | bytes 24580
  245.2 87.8 %reduce-scatter.16.cloned.1.call-start = ((), (), s32[]{:S(2)}) async-start(), calls=%async_computation.11 | async-start | bytes 589824
  267.9 5.6 %copy-start.25 = (bf16[4,512,128]{1,2,0:T(8,128)(2,1)S(1)}, bf16[4,512,128]{1,2,0:T(8,128)(2,1)}, u32[]{:S(2)}) copy-start(bf16[4,512,128]{1,2,0:T(8,128)(2,1)} %reduce-scatter.12.cloned.1.call-done) | copy-start | bytes 1572868
  267.9 5.7 %copy-start.11 = (bf16[4,8,64,1024]{3,2,1,0:T(8,128)(2,1)S(1)}, bf16[4,8,64,1024]{3,2,1,0:T(8,128)(2,1)}, u32[]{:S(2)}) copy-start(bf16[4,8,64,1024]{3,2,1,0:T(8,128)(2,1)} %copy-done.10) | copy-start | bytes 12582916
  276.6 137.6 %reduce-scatter.14.cloned.1.call-start = ((), (), s32[]{:S(2)}) async-start(), calls=%async_computation.10 | async-start | bytes 4456448 | tf_op jit(solution)/shard_map/reduce_scatter | solution.py:336
  286.9 208.1 %reduce-scatter.10.cloned.1.call-start = ((), (), s32[]{:S(2)}) async-start(), calls=%async_computation.8 | async-start | bytes 4456448 | tf_op jit(solution)/shard_map/reduce_scatter | solution.py:295
  293.0 121.2 %copy-start.2 = (f32[1024]{0:T(1024)S(1)}, f32[1024]{0:T(1024)}, u32[]{:S(2)}) copy-start(f32[1024]{0:T(1024)} %param.22) | copy-start | bytes 12292
  293.0 201.9 %copy-start.30 = (bf16[4,8,4,1024]{3,2,1,0:T(4,128)(2,1)S(1)}, bf16[4,8,4,1024]{3,2,1,0:T(4,128)(2,1)}, u32[]{:S(2)}) copy-start(bf16[4,8,4,1024]{3,2,1,0:T(4,128)(2,1)} %param.26) | copy-start | bytes 786436
  (14 other events, 12.5 us)
Sparse Core Ops, SparseCore 0:
  43.8 51.1 all-gather.3
  97.1 51.2 all-gather.7
  150.1 32.1 all-gather.5
  233.5 34.3 reduce-scatter.11
  270.7 29.6 reduce-scatter.17
  303.3 29.6 reduce-scatter.15
  336.4 77.7 reduce-scatter.13
  417.9 77.0 reduce-scatter.9

commit v2 on v1

v2 whole, which is shorter than its diff:
```python
import jax
import jax.numpy as jnp
import numpy as np
from jax import lax
from jax.experimental import pallas as pl
from jax.experimental.pallas import tpu as pltpu
from jax.sharding import PartitionSpec as P

MESH = pl.DeviceIdType.MESH
F32 = jnp.float32
BF16 = jnp.bfloat16
SEG = ((128, 48), (176, 48), (224, 32), (256, 32), (288, 16), (304, 16), (320, 16), (336, 16))
WAY = ((0, 1), (0, -1), (1, 0), (-1, 0), (1, 1), (1, -1), (-1, 1), (-1, -1))
KEYS = 384
RING = (1, 3, 2)
BLOCK = 512
CHUNK = 1024
LOG2E = 1.4426950408889634
LN2 = 0.6931471805599453


def dot(a, b):
    return jnp.dot(a, b, preferred_element_type=F32)


def dot_nt(a, b):
    return lax.dot_general(a, b, (((1,), (1,)), ((), ())), preferred_element_type=F32)


def start_copy(source, target, send_sem, recv_sem, device):
    copy = pltpu.make_async_remote_copy(
        src_ref=source, dst_ref=target, send_sem=send_sem, recv_sem=recv_sem, device_id=device, device_id_type=MESH
    )
    copy.start()
    return copy


def swap_peers(x, y, z, core):
    peers = []
    for d in range(1, 16):
        px, py = lax.rem(x + d // 4, 4), lax.rem(y + d % 4, 4)
        peers.append((px, py, (py * 2 + core, px * 4 + z)))
    return peers


def fine_tables():
    sel = np.zeros((KEYS, 128), np.float32)
    place = np.full((8, KEYS), 10000, np.int32)
    query = np.zeros((256, 128), np.int32)
    for p in range(4):
        for u in range(8):
            for w in range(4):
                n = p * 32 + u * 4 + w
                i, j = 2 * u + p // 2, 2 * w + p % 2
                sel[n, i * 8 + j] = 1
                place[0, n], place[1, n] = i, j
                query[n, 0] = query[n + 128, 0] = i
                query[n, 1] = query[n + 128, 1] = j
    for (start, _), (down, right) in zip(SEG, WAY):
        rows = {0: range(16), 1: range(13, 16), -1: range(3)}[down]
        cols = {0: range(8), 1: range(5, 8), -1: range(3)}[right]
        n = start
        for i in rows:
            for j in cols:
                sel[n, i * 8 + j] = 1
                place[0, n], place[1, n] = i - 16 * down, j - 8 * right
                n += 1
    return sel, place, query


def fine_kernel(
    x_ref, sel_ref, place_ref, query_ref, gain_ref, wqkv_ref, wout_ref, scale_ref, wmerge_ref, gain2_ref,
    cot_ref, wpack_ref, scale2_ref,
    in_ref, ng, cg, wg, tr, qg, kv,
    keys_in, send, kn, vv, qn, fr, bias, ts,
    send_sem, recv_sem, w_s, w_r, f_s, f_r, c_s, c_r, n_s, n_r, a_s, a_r, k_s, k_r,
):
    row, col = lax.axis_index("row"), lax.axis_index("col")
    y, core, x, z = lax.div(row, 2), lax.rem(row, 2), lax.div(col, 4), lax.rem(col, 4)
    barrier = pltpu.get_barrier_semaphore()
    peers = [(lax.rem(row + a + 8, 8), lax.rem(col + b + 16, 16)) for a, b in WAY]
    z_peers = [(row, x * 4 + lax.rem(z + off, 4)) for off in RING]
    x_peers = [(row, lax.rem(x + off, 4) * 4 + z) for off in RING]
    twin = (y * 2 + 1 - core, col)
    swap = swap_peers(x, y, z, core)
    for peer in peers + z_peers + x_peers + [twin] + [p for _, _, p in swap]:
        pl.semaphore_signal(barrier, inc=1, device_id=peer, device_id_type=MESH)

    wg[x] = wpack_ref[...]
    cg[z] = cot_ref[...]

    @pl.loop(0, 4)
    def _(img):
        packed = dot(sel_ref[...], x_ref[img]).astype(BF16)
        keys_in[img, 0:128, :] = packed[0:128]
        send[img] = packed[128:352]
        keys_in[img, 352:384, :] = packed[352:384]

    pl.semaphore_wait(barrier, 30)
    copies = []
    for k, ((start, size), peer) in enumerate(zip(SEG, peers)):
        copy = pltpu.make_async_remote_copy(
            src_ref=send.at[:, start - 128 : start - 128 + size, :],
            dst_ref=keys_in.at[:, start : start + size, :],
            send_sem=send_sem.at[k],
            recv_sem=recv_sem.at[k],
            device_id=peer,
            device_id_type=MESH,
        )
        copy.start()
        copies.append(copy)

    half = pl.ds(pl.multiple_of(core * 512, 512), 512)
    w_copies = [
        start_copy(wpack_ref.at[half, :], wg.at[x, half, :], w_s.at[k], w_r.at[k], x_peers[k]) for k in range(3)
    ]

    seen = (
        (jnp.abs(place_ref[0:1, :] - query_ref[:, 0:1]) <= 3)
        & (jnp.abs(place_ref[1:2, :] - query_ref[:, 1:2]) <= 3)
    )
    gi = place_ref[0:1, :] + row * 16
    gj = place_ref[1:2, :] + col * 8
    inside = (gi >= 0) & (gi < 128) & (gj >= 0) & (gj < 128)
    bias[...] = jnp.where(seen & inside, 0.0, -1e30).astype(F32)

    lane = lax.broadcasted_iota(jnp.int32, (128, 128), 1)
    sub = lax.broadcasted_iota(jnp.int32, (128, 128), 0)
    same = jnp.where((lane < 64) == (sub < 64), 1.0 / 64, 0.0).astype(BF16)

    def token_norm(tokens):
        xf = tokens.astype(F32)
        factor = lax.rsqrt(jnp.mean(xf * xf, axis=-1, keepdims=True) + 1e-06)
        return (xf * factor * gain_ref[...]).astype(BF16)

    def head_norm(values):
        vf = values.astype(BF16).astype(F32)
        sq = (vf * vf).astype(BF16)
        parts = [dot(sq[:, k * 128 : k * 128 + 128], same) for k in range(4)]
        return vf * lax.rsqrt(jnp.concatenate(parts, axis=1) + 1e-06)

    @pl.loop(0, 4)
    def _(img):
        nx = token_norm(keys_in[img, 0:128, :])
        qn[img] = (head_norm(dot(nx, wqkv_ref[:, 0:512])) * scale_ref[...]).astype(BF16)
        kn[img, 0:128, :] = head_norm(dot(nx, wqkv_ref[:, 512:1024])).astype(BF16)
        vv[img, 0:128, :] = dot(nx, wqkv_ref[:, 1024:1536]).astype(BF16)

    for copy in copies:
        copy.wait()
    c_copies = [start_copy(cot_ref, cg.at[z], c_s.at[k], c_r.at[k], z_peers[k]) for k in range(3)]

    @pl.loop(0, 4)
    def _(img):
        nx = token_norm(keys_in[img, 128:384, :])
        kn[img, 128:384, :] = head_norm(dot(nx, wqkv_ref[:, 512:1024])).astype(BF16)
        vv[img, 128:384, :] = dot(nx, wqkv_ref[:, 1024:1536]).astype(BF16)

    ones = jnp.ones((KEYS, 128), BF16)

    @pl.loop(0, 4)
    def _(img):
        mixed = []
        for pair in range(4):
            at = slice(pair * 128, pair * 128 + 128)
            q = qn[img, :, at]
            zero = jnp.zeros_like(q)
            both = jnp.concatenate([jnp.where(lane < 64, q, zero), jnp.where(lane < 64, zero, q)], axis=0)
            powered = jnp.exp(dot_nt(both, kn[img, :, at]) + bias[...]).astype(BF16)
            sums = dot(powered, jnp.concatenate([vv[img, :, at], ones], axis=1))
            ratio = sums[:, 0:128] / sums[:, 128:256]
            mixed.append(jnp.where(lane < 64, ratio[0:128], ratio[128:256]).astype(BF16))
        mix = jnp.concatenate(mixed, axis=1)
        fr[img] = (keys_in[img, 0:128, :].astype(F32) + dot(mix, wout_ref[...])).astype(BF16)

    f_copies = []
    for k, off in enumerate(RING):
        w_copies[k].wait()
        block = wg.at[lax.rem(x - off + 4, 4), half, :]
        f_copies.append(start_copy(block, block, f_s.at[k], f_r.at[k], twin))

    merged = jnp.zeros((128, 1024), F32)
    for p in range(4):
        part = jnp.concatenate([fr[img, p * 32 : p * 32 + 32, :] for img in range(4)], axis=0)
        merged = merged + dot(part, wmerge_ref[p * 512 : p * 512 + 512, :])
    inner = merged.astype(BF16)
    in_ref[...] = inner
    xf = inner.astype(F32)
    factor = lax.rsqrt(jnp.mean(xf * xf, axis=-1, keepdims=True) + 1e-06)
    ng[z] = (xf * factor * gain2_ref[...]).astype(BF16)
    n_copies = [start_copy(ng.at[z], ng.at[z], n_s.at[k], n_r.at[k], z_peers[k]) for k in range(3)]
    for copy in f_copies:
        copy.wait()

    a_copies = []
    for step in range(4):
        if step == 0:
            zi = z
        else:
            zi = lax.rem(z - RING[step - 1] + 4, 4)
            c_copies[step - 1].wait()
            n_copies[step - 1].wait()
        normed, grads = ng[zi], cg[zi]
        for h in range(4):
            first = dot(normed, wg[h])
            second = dot(grads, wg[h, :, 128:256])
            ts[h, zi, :, 0:128] = first[:, 0:128].astype(BF16)
            ts[h, zi, :, 128:256] = jnp.where(lane < 64, first[:, 128:256], second).astype(BF16)
        for d, (px, py, peer) in enumerate(swap):
            rows = pl.ds(pl.multiple_of(py * 32, 32), 32)
            a_copies.append(
                start_copy(ts.at[px, zi, rows, :], tr.at[x * 4 + y, zi], a_s.at[d, step], a_r.at[d, step], peer)
            )
        tr[x * 4 + y, zi] = ts[x, zi, pl.ds(pl.multiple_of(y * 32, 32), 32), :]

    low = jnp.where(sub < 64, 1.0 / 64, 0.0).astype(BF16)
    for d in range(16):
        if d > 0:
            for step in range(4):
                a_copies[step * 15 + d - 1].wait()
        dx, dy = d // 4, d % 4
        slot = lax.rem(x - dx + 4, 4) * 4 + lax.rem(y - dy + 4, 4)
        raw = tr[slot].reshape(128, 256).astype(F32)
        k_f, q_f = raw[:, 0:128], raw[:, 128:256]
        k_n = k_f * lax.rsqrt(dot((k_f * k_f).astype(BF16), low) + 1e-06)
        q_n = q_f * lax.rsqrt(dot((q_f * q_f).astype(BF16), low) + 1e-06) * scale2_ref[...]
        at = pl.ds(pl.multiple_of(slot * 128, 128), 128)
        kv[0, at, :] = jnp.where(lane < 64, k_n, k_f).astype(BF16)
        qg[at, :] = jnp.where(lane < 64, q_n, q_f).astype(BF16)
    start_copy(kv.at[0], kv.at[1], k_s, k_r, twin).wait()


def front(x, gain, wqkv, wout, scale, wmerge, gain2, cot, wpack, scale2):
    sel, place, query = fine_tables()
    vmem = pl.BlockSpec(memory_space=pltpu.VMEM)
    dma = pltpu.SemaphoreType.DMA
    return pl.pallas_call(
        fine_kernel,
        out_shape=(
            jax.ShapeDtypeStruct((128, 1024), BF16),
            jax.ShapeDtypeStruct((4, 128, 1024), BF16),
            jax.ShapeDtypeStruct((4, 128, 1024), BF16),
            jax.ShapeDtypeStruct((4, 1024, 256), BF16),
            jax.ShapeDtypeStruct((16, 4, 32, 256), BF16),
            jax.ShapeDtypeStruct((2048, 128), BF16),
            jax.ShapeDtypeStruct((2, 2048, 128), BF16),
        ),
        in_specs=[vmem] * 13,
        out_specs=(vmem,) * 7,
        scratch_shapes=[
            pltpu.VMEM((4, KEYS, 512), BF16),
            pltpu.VMEM((4, 224, 512), BF16),
            pltpu.VMEM((4, KEYS, 512), BF16),
            pltpu.VMEM((4, KEYS, 512), BF16),
            pltpu.VMEM((4, 128, 512), BF16),
            pltpu.VMEM((4, 128, 512), BF16),
            pltpu.VMEM((256, KEYS), F32),
            pltpu.VMEM((4, 4, 128, 256), BF16),
            dma((8,)), dma((8,)),
            dma((3,)), dma((3,)), dma((3,)), dma((3,)), dma((3,)), dma((3,)), dma((3,)), dma((3,)),
            dma((15, 4)), dma((15, 4)), dma(()), dma(()),
        ],
        compiler_params=pltpu.CompilerParams(
            collective_id=0, has_side_effects=True, vmem_limit_bytes=50 * 1024 * 1024
        ),
        cost_estimate=pl.CostEstimate(flops=8_000_000_000, bytes_accessed=16_000_000, transcendentals=2_000_000),
        name="front",
    )(
        x.reshape(4, 128, 512),
        jnp.asarray(sel, BF16),
        jnp.asarray(place),
        jnp.asarray(query),
        gain.reshape(1, 512),
        wqkv,
        wout,
        jnp.repeat(scale / 64, 64).reshape(1, 512),
        wmerge,
        gain2.reshape(1, 1024),
        cot,
        wpack,
        scale2,
    )


def attention_kernel(qg_ref, kv_ref, back_ref, gqa_ref, gkv_ref, powers, ones_v, sums):
    step = pl.program_id(0)
    lane = lax.broadcasted_iota(jnp.int32, (BLOCK, 128), 1)

    @pl.when(step == 0)
    def _():
        kv = kv_ref[...]
        lanes = lax.broadcasted_iota(jnp.int32, kv.shape, 1)
        ones_v[...] = jnp.where(lanes < 64, jnp.ones_like(kv), kv)
        sums[...] = jnp.zeros_like(sums)

    tile = qg_ref[...]
    zero = jnp.zeros_like(tile)
    q = jnp.where(lane < 64, tile, zero)
    total = jnp.zeros((BLOCK, 128), F32)
    for c in range(4096 // CHUNK):
        at = slice(c * CHUNK, c * CHUNK + CHUNK)
        powered = jnp.exp2(dot_nt(q, kv_ref[at, :])).astype(BF16)
        powers[:, at] = powered
        total = total + dot(powered, ones_v[at, :])
    turned = pltpu.roll(total, 64, 1)
    upper = lane >= 64
    inverse = 1.0 / jnp.where(upper, turned, total)
    outputs = total * inverse
    g = tile.astype(F32)
    delta = jnp.sum(jnp.where(upper, g * outputs, 0.0), axis=1, keepdims=True) * inverse
    high = delta.astype(BF16).astype(F32)
    rest = jnp.where(lane == 0, -high, jnp.where(lane == 1, high - delta, 0.0))
    scaled = jnp.where(upper, g * inverse, rest)
    g_aug = scaled.astype(BF16)
    g_turn = scaled.T[64:128].astype(BF16)
    q_turn = g.T[0:64].astype(BF16)
    grad_q = jnp.zeros((BLOCK, 128), F32)
    for c in range(4096 // CHUNK):
        at = slice(c * CHUNK, c * CHUNK + CHUNK)
        powered = powers[:, at]
        grad_s = (powered.astype(F32) * dot_nt(g_aug, ones_v[at, :])).astype(BF16)
        grad_q = grad_q + dot(grad_s, kv_ref[at, :])
        sums[64:128, at] += dot(g_turn, powered)
        sums[0:64, at] += dot(q_turn, grad_s)
    gqa_ref[...] = jnp.where(upper, outputs, grad_q * back_ref[...])

    @pl.when(step == 2048 // BLOCK - 1)
    def _():
        for c in range(8):
            part = sums[:, c * 512 : c * 512 + 512].T
            lanes = lax.broadcasted_iota(jnp.int32, part.shape, 1)
            gkv_ref[c * 512 : c * 512 + 512, :] = jnp.where(lanes < 64, part * LN2, part)


def attention(qg, kv, back):
    whole = pl.BlockSpec((4096, 128), lambda i: (0, 0))
    part = pl.BlockSpec((BLOCK, 128), lambda i: (i, 0))
    return pl.pallas_call(
        attention_kernel,
        grid=(2048 // BLOCK,),
        out_shape=(jax.ShapeDtypeStruct((2048, 128), F32), jax.ShapeDtypeStruct((4096, 128), F32)),
        in_specs=[part, whole, pl.BlockSpec((1, 128), lambda i: (0, 0))],
        out_specs=(part, whole),
        scratch_shapes=[
            pltpu.VMEM((BLOCK, 4096), BF16),
            pltpu.VMEM((4096, 128), BF16),
            pltpu.VMEM((128, 4096), F32),
        ],
        compiler_params=pltpu.CompilerParams(vmem_limit_bytes=50 * 1024 * 1024),
        cost_estimate=pl.CostEstimate(flops=20_000_000_000, bytes_accessed=8_000_000, transcendentals=8_000_000),
        name="attention",
    )(qg, kv, back)


def back_kernel(
    gkv_ref, gqa_ref, raw_ref, wg_ref, ng_ref, cg_ref, in_ref, cot_ref, gain_ref,
    out_ref, grad_ref, dw_ref, do_ref,
    other, r, rr, ps, pr, ws, wr,
    k_s, k_r, a_s, a_r, p_s, p_r, d_s, d_r,
):
    row, col = lax.axis_index("row"), lax.axis_index("col")
    y, core, x, z = lax.div(row, 2), lax.rem(row, 2), lax.div(col, 4), lax.rem(col, 4)
    barrier = pltpu.get_barrier_semaphore()
    z_peers = [(row, x * 4 + lax.rem(z + off, 4)) for off in RING]
    twin = (y * 2 + 1 - core, col)
    swap = swap_peers(x, y, z, core)
    plane = [
        (dx, dr, lax.rem(x + dx, 4), lax.rem(row + dr, 8))
        for dx in (2, 1, 3, 0)
        for dr in range(8)
    ]
    others = [(pr_, px * 4 + z) for dx, dr, px, pr_ in plane if dx + dr > 0]
    for peer in z_peers + [twin] + [p for _, _, p in swap] + others:
        pl.semaphore_signal(barrier, inc=1, device_id=peer, device_id_type=MESH)
    pl.semaphore_wait(barrier, 50)
    start_copy(gkv_ref.at[1], other, k_s, k_r, twin).wait()

    lane = lax.broadcasted_iota(jnp.int32, (128, 128), 1)
    sub = lax.broadcasted_iota(jnp.int32, (128, 128), 0)
    low = jnp.where(sub < 64, 1.0 / 64, 0.0).astype(BF16)

    def head_back(values, upstream):
        factor = lax.rsqrt(dot((values * values).astype(BF16), low) + 1e-06)
        unit = values * factor
        grad = factor * (upstream - unit * dot((upstream * unit).astype(BF16), low))
        return jnp.where(lane < 64, grad, upstream).astype(BF16)

    def prepare(slot):
        at = pl.ds(pl.multiple_of(slot * 128, 128), 128)
        raw = raw_ref[slot].reshape(128, 256).astype(F32)
        r[slot, :, :, 0:128] = head_back(raw[:, 0:128], gkv_ref[0, at, :] + other[at, :]).reshape(4, 32, 128)
        r[slot, :, :, 128:256] = head_back(raw[:, 128:256], gqa_ref[at, :]).reshape(4, 32, 128)

    mine = pl.ds(pl.multiple_of(y * 32, 32), 32)
    a_copies = []
    for d, (px, py, peer) in enumerate(swap):
        prepare(px * 4 + py)
        a_copies.append(
            start_copy(r.at[px * 4 + py], rr.at[x, :, mine, :], a_s.at[d], a_r.at[d], peer)
        )
    prepare(x * 4 + y)
    rr[x, :, mine, :] = r[x * 4 + y]
    for copy in a_copies:
        copy.wait()

    wide = lax.broadcasted_iota(jnp.int32, (128, 256), 1)

    def partial(zi):
        grad = jnp.zeros((128, 1024), F32)
        term = jnp.zeros((128, 1024), F32)
        for h in range(4):
            part = rr[h, zi]
            zero = jnp.zeros_like(part)
            grad = grad + dot_nt(jnp.where(wide < 192, part, zero), wg_ref[h])
            last = part[:, 128:256]
            term = term + dot_nt(jnp.where(lane >= 64, last, jnp.zeros_like(last)), wg_ref[h, :, 128:256])
        return grad, term

    p_copies = []
    for k in (2, 0, 1):
        zi = lax.rem(z + RING[k], 4)
        grad, term = partial(zi)
        ps[k, 0] = grad.astype(BF16)
        ps[k, 1] = term.astype(BF16)
        p_copies.append(start_copy(ps.at[k], pr.at[k], p_s.at[k], p_r.at[k], z_peers[k]))

    normed = ng_ref[...].reshape(512, 1024)
    cots = cg_ref[...].reshape(512, 1024)
    d_copies = []
    for k in range(4):
        h = plane[k * 8][2]
        turned = rr[h].reshape(512, 256).astype(F32).T.astype(BF16)
        ws[h, 0:192, :] = dot(turned[0:192], normed).astype(BF16)
        ws[h, 192:256, :] = dot(turned[192:256], cots).astype(BF16)
        for dx, dr, px, prow in plane[k * 8 : k * 8 + 8]:
            piece = ws.at[px, :, pl.ds(pl.multiple_of(prow * 128, 128), 128)]
            if dx + dr > 0:
                n = dx * 8 + dr
                d_copies.append(
                    start_copy(piece, wr.at[x * 8 + row], d_s.at[n], d_r.at[n], (prow, px * 4 + z))
                )
    wr[x * 8 + row] = ws[x, :, pl.ds(pl.multiple_of(row * 128, 128), 128)]

    grad, term = partial(z)
    for copy in p_copies:
        copy.wait()
    for k in range(3):
        grad = grad + pr[k, 0].astype(F32)
        term = term + pr[k, 1].astype(F32)
    values = in_ref[...].astype(F32)
    out_ref[...] = (values + term).astype(BF16)
    factor = lax.rsqrt(jnp.mean(values * values, axis=-1, keepdims=True) + 1e-06)
    unit = values * factor
    upstream = grad * gain_ref[...]
    grad_ref[...] = cot_ref[...].astype(F32) + factor * (
        upstream - unit * jnp.mean(upstream * unit, axis=-1, keepdims=True)
    )

    for copy in d_copies:
        copy.wait()
    total = jnp.zeros((256, 128), F32)
    for n in range(32):
        total = total + wr[n].astype(F32)
    do_ref[...] = total[192:256]
    turned = total.T
    dw_ref[0] = turned[:, 128:192]
    dw_ref[1] = turned[:, 0:64]
    dw_ref[2] = turned[:, 64:128]


def back(gkv, gqa, raw, wg, ng, cg, inner, cot, gain):
    vmem = pl.BlockSpec(memory_space=pltpu.VMEM)
    dma = pltpu.SemaphoreType.DMA
    return pl.pallas_call(
        back_kernel,
        out_shape=(
            jax.ShapeDtypeStruct((128, 1024), BF16),
            jax.ShapeDtypeStruct((128, 1024), F32),
            jax.ShapeDtypeStruct((3, 128, 64), F32),
            jax.ShapeDtypeStruct((64, 128), F32),
        ),
        in_specs=[vmem] * 9,
        out_specs=(vmem,) * 4,
        scratch_shapes=[
            pltpu.VMEM((2048, 128), F32),
            pltpu.VMEM((16, 4, 32, 256), BF16),
            pltpu.VMEM((4, 4, 128, 256), BF16),
            pltpu.VMEM((3, 2, 128, 1024), BF16),
            pltpu.VMEM((3, 2, 128, 1024), BF16),
            pltpu.VMEM((4, 256, 1024), BF16),
            pltpu.VMEM((32, 256, 128), BF16),
            dma(()), dma(()), dma((15,)), dma((15,)), dma((3,)), dma((3,)), dma((32,)), dma((32,)),
        ],
        compiler_params=pltpu.CompilerParams(
            collective_id=1, has_side_effects=True, vmem_limit_bytes=50 * 1024 * 1024
        ),
        cost_estimate=pl.CostEstimate(flops=8_000_000_000, bytes_accessed=16_000_000, transcendentals=1_000_000),
        name="back",
    )(gkv, gqa, raw, wg, ng, cg, inner, cot, gain)


def per_device(
    fine_input,
    gain_fine,
    fine_qkv,
    fine_out,
    fine_scale,
    merge_weight,
    gain_coarse,
    coarse_qkv,
    coarse_out,
    coarse_scale,
    cotangent,
):
    cot = cotangent.reshape(128, 1024)
    wpack = jnp.concatenate([coarse_qkv[1], coarse_qkv[2], coarse_qkv[0], coarse_out.T], axis=1)
    back_scale = jnp.broadcast_to(coarse_scale.reshape(1, 1) / 64, (1, 128))
    inner, ng, cg, wg, raw, qg, kv = front(
        fine_input, gain_fine, fine_qkv, fine_out, fine_scale, merge_weight, gain_coarse,
        cot, wpack, back_scale * LOG2E,
    )
    gqa, gkv = attention(qg, kv.reshape(4096, 128), back_scale)
    output, grad, qkv_grad, out_grad = back(
        gkv.reshape(2, 2048, 128), gqa, raw, wg, ng, cg, inner, cot, gain_coarse.reshape(1, 1024)
    )
    return (output.reshape(4, 8, 4, 1024), grad.reshape(4, 8, 4, 1024), qkv_grad, out_grad)


def solution(mesh):
    return jax.shard_map(
        per_device,
        mesh=mesh,
        in_specs=(
            P(None, "row", "col", None),
            P(),
            P(),
            P(),
            P(),
            P(),
            P(),
            P(None, None, "col"),
            P("col", None),
            P("col"),
            P(None, "row", "col", None),
        ),
        out_specs=(
            P(None, "row", "col", None),
            P(None, "row", "col", None),
            P(None, "row", "col"),
            P("col", "row"),
        ),
        check_vma=False,
    )
```

time: 514 us -> 170 us (0.33); the launches traced: 506 us -> 170 us
  waiting for transfers between devices: 331 us -> 0 us
  Pallas kernels: 27.4 us -> 158 us
  matrix products: 62.9 us -> 0 us
  local copies, waits for them, and re-layouts: 55.6 us -> 9.31 us
  between operations: 15.5 us -> 1.47 us
  other arithmetic: 11.7 us -> 1.02 us
    reduce_scatter x3 -> x0, waiting for transfers between devices: 182 us -> none  [the longest x1 79.5 us: per_device(): lax.psum_scatter(grad_normed.reshape(images, half_rows, band_cols, width_...]
    pallas_call x1 -> x3, Pallas kernels: 27.4 us -> 158 us  [the longest x1 67.6 us: front(): pl.pallas_call(fine_kernel, out_shape=(jax.ShapeDtypeStruct((128, 1024),...]
    all_gather x3 -> x0, waiting for transfers between devices: 111 us -> none  [the longest x1 50.3 us: per_device(): band = lax.all_gather(coarse_normed, 'col', axis=2, tiled=True)]
    dot_general x36 -> x0, matrix products: 62.9 us -> none  [the longest x3 8.73 us: per_device(): jnp.dot(band_flat, coarse_qkv[index], preferred_element_type=jnp.float32)]
    unnamed x10 -> x0, waiting for transfers between devices: 38.1 us -> none
    unnamed x64 -> x26, local copies, waits for them, and re-layouts: 20.6 us -> 5.33 us
    while x58 -> x0, local copies, waits for them, and re-layouts: 12.8 us -> none
    all_gather x2 -> x0, local copies, waits for them, and re-layouts: 9.03 us -> none  [the longest x1 4.52 us: per_device(): band = lax.all_gather(coarse_normed, 'col', axis=2, tiled=True)]
  transfers between devices with their start and end apart: 8 -> 0, of which waited for: 8 -> 0; matrix products, arithmetic and copies ran while one was open for 12% -> 0% of each run, Pallas kernels for 0% -> 0%
where the time goes in v2:
time: 170 us
  Pallas kernels  158 us (93%)
  local copies, waits for them, and re-layouts  9.31 us (5%)
    pallas_call x1, Pallas kernels, front(): pl.pallas_call(fine_kernel, out_shape=(jax.ShapeDtypeStruct((128, 1024),...  67.6 us
    pallas_call x1, Pallas kernels, back(): pl.pallas_call(back_kernel, out_shape=(jax.ShapeDtypeStruct((128, 1024),...  58.5 us
    pallas_call x1, Pallas kernels, attention(): pl.pallas_call(attention_kernel, grid=(2048 // BLOCK,), out_shape=(jax.Sh...  32.3 us
    unnamed x26, local copies, waits for them, and re-layouts  5.33 us

profile of v2, /device:TPU:1, one launch (start us, length us, event | category | flops | bytes accessed | tf_op | source)
XLA Modules:
  0.0 170.2 jit_solution(5842162589245086897)
XLA Ops:
  1.3 0.7 broadcast_multiply_fusion
  2.0 0.1 broadcast_in_dim.12
  2.0 0.1 reshape_reshape.3.scale_ref
  2.1 1.0 reshape.50.cot_ref
  3.1 0.0 copy-start
  3.1 0.0 copy-start.1
  3.2 0.0 copy-start.2
  3.2 0.0 copy-start.3
  3.2 0.0 copy-start.5
  3.2 0.0 copy-start.6
  3.2 0.0 copy-start.7
  3.2 1.2 copy.21
  4.4 1.1 fusion
  5.4 0.2 copy.23
  5.6 0.2 copy.24
  5.8 0.2 copy.25
  6.0 0.4 pad_maximum_fusion.wpack_ref
  6.4 0.0 copy-done
  6.4 0.0 copy-done.1
  6.4 0.0 copy-done.2
  6.4 0.0 copy-done.3
  6.4 0.0 copy-done.5
  6.4 0.0 copy-done.6
  6.4 0.0 copy-done.7
  6.4 67.6 %front.1 = (bf16[128,1024]{1,0:T(8,128)(2,1)S(1)}, bf16[4,128,1024]{2,1,0:T(8,128)(2,1)S(1)}, bf16[4,128,1024]{2,1,0:T(8,128)(2,1)}, bf16[4,1024,256]{2,1,0:T(8,...) custom-call(bf16[4,128,512]{2,1,0:T(8,128)(2,1)S(1)} %bitcast.11, ...), custom_call_target="tpu_custom_call" | custom-call | flops 8000000000 | bytes 16000000 | tf_op jit(solution)/shard_map/front/pallas_call | solution.py:237
  74.0 0.0 copy-start.8
  74.0 1.0 copy-done.8
  75.0 0.0 copy-start.4
  75.0 1.2 copy-done.4
  76.2 0.0 copy-start.9
  76.2 32.3 %attention.1 = (f32[2048,128]{1,0:T(8,128)S(1)}, f32[4096,128]{1,0:T(8,128)}) custom-call(bf16[2048,128]{1,0:T(8,128)(2,1)S(1)} %get-tuple-element.17.qg_ref, bf16[4096,128]{1,0:T(8,128)(2,1)S(1)} %bitcast.15, f32[1,128]{1,0:T(1,128)S(1)} %broadcast_in_dim.15.back_ref), custom_call_target="tpu_custom_call" | custom-call | flops 20000000000 | bytes 8000000 | tf_op jit(solution)/shard_map/attention/pallas_call | solution.py:338
  108.5 0.0 copy-done.9
  108.5 58.5 %back.1 = (bf16[128,1024]{1,0:T(8,128)(2,1)S(1)}, f32[128,1024]{1,0:T(8,128)S(1)}, f32[3,128,64]{2,1,0:T(8,128)S(1)}, f32[64,128]{1,0:T(8,128)S(1)}) custom-call(f32[2,2048,128]{2,1,0:T(8,128)} %bitcast.20, f32[2048,128]{1,0:T(8,128)S(1)} %get-tuple-element.20.gqa_ref, bf16[16,4,32,256]{3,2,1,0:T(8,128)(2,1)S(1)} %copy-done.9, ...), custom_call_target="tpu_custom_call" | custom-call | flops 8000000000 | bytes 16000000 | tf_op jit(solution)/shard_map/back/pallas_call | solution.py:474
  167.0 0.8 reshape.53
  167.8 0.8 copy.22
  168.6 0.9 reshape.54
  169.5 0.6 copy.28
  (2 shorter events, 0.0 us)
Async XLA Ops:
  3.1 3.2 %copy-start = (bf16[4,16,8,512]{3,2,1,0:T(8,128)(2,1)S(1)}, bf16[4,16,8,512]{3,2,1,0:T(8,128)(2,1)}, u32[]{:S(2)}) copy-start(bf16[4,16,8,512]{3,2,1,0:T(8,128)(2,1)} %param.14) | copy-start | bytes 1572868
  3.1 3.2 %copy-start.1 = (bf16[512,512]{1,0:T(8,128)(2,1)S(1)}, bf16[512,512]{1,0:T(8,128)(2,1)}, u32[]{:S(2)}) copy-start(bf16[512,512]{1,0:T(8,128)(2,1)} %wout_ref.1) | copy-start | bytes 1572868
  3.2 3.2 %copy-start.2 = (f32[1024]{0:T(1024)S(1)}, f32[1024]{0:T(1024)}, u32[]{:S(2)}) copy-start(f32[1024]{0:T(1024)} %param.20) | copy-start | bytes 12292
  3.2 3.2 %copy-start.3 = (f32[512]{0:T(512)S(1)}, f32[512]{0:T(512)}, u32[]{:S(2)}) copy-start(f32[512]{0:T(512)} %param.15) | copy-start | bytes 6148
  3.2 3.2 %copy-start.5 = (s32[256,128]{1,0:T(8,128)S(1)}, s32[256,128]{1,0:T(8,128)}, u32[]{:S(2)}) copy-start(s32[256,128]{1,0:T(8,128)} %constant.21.clone.query_ref) | copy-start | bytes 393220
  3.2 3.2 %copy-start.6 = (bf16[384,128]{1,0:T(8,128)(2,1)S(1)}, bf16[384,128]{1,0:T(8,128)(2,1)}, u32[]{:S(2)}) copy-start(bf16[384,128]{1,0:T(8,128)(2,1)} %constant.19.clone.sel_ref) | copy-start | bytes 294916
  3.2 3.2 %copy-start.7 = (s32[8,384]{1,0:T(8,128)S(1)}, s32[8,384]{1,0:T(8,128)}, u32[]{:S(2)}) copy-start(s32[8,384]{1,0:T(8,128)} %constant.20.clone.place_ref) | copy-start | bytes 36868
  74.0 1.0 copy-start.8
  75.0 1.2 copy-start.4
  76.2 32.3 %copy-start.9 = (bf16[16,4,32,256]{3,2,1,0:T(8,128)(2,1)S(1)}, bf16[16,4,32,256]{3,2,1,0:T(8,128)(2,1)}, u32[]{:S(2)}) copy-start(bf16[16,4,32,256]{3,2,1,0:T(8,128)(2,1)} %get-tuple-element.21.raw_ref) | copy-start | bytes 3145732

commit v3 on v2

v3 whole, which is shorter than its diff:
```python
import jax
import jax.numpy as jnp
import numpy as np
from jax import lax
from jax.experimental import pallas as pl
from jax.experimental.pallas import tpu as pltpu
from jax.sharding import PartitionSpec as P

MESH = pl.DeviceIdType.MESH
F32 = jnp.float32
BF16 = jnp.bfloat16
SEG = ((128, 48), (176, 48), (224, 32), (256, 32), (288, 16), (304, 16), (320, 16), (336, 16))
WAY = ((0, 1), (0, -1), (1, 0), (-1, 0), (1, 1), (1, -1), (-1, 1), (-1, -1))
KEYS = 384
RING = (1, 3, 2)
BLOCK = 512
CHUNK = 1024
LOG2E = 1.4426950408889634
LN2 = 0.6931471805599453


def dot(a, b):
    return jnp.dot(a, b, preferred_element_type=F32)


def dot_nt(a, b):
    return lax.dot_general(a, b, (((1,), (1,)), ((), ())), preferred_element_type=F32)


def start_copy(source, target, send_sem, recv_sem, device):
    copy = pltpu.make_async_remote_copy(
        src_ref=source, dst_ref=target, send_sem=send_sem, recv_sem=recv_sem, device_id=device, device_id_type=MESH
    )
    copy.start()
    return copy


def swap_peers(x, y, z, core):
    peers = []
    for d in range(1, 16):
        px, py = lax.rem(x + d // 4, 4), lax.rem(y + d % 4, 4)
        peers.append((px, py, (py * 2 + core, px * 4 + z)))
    return peers


def fine_tables():
    sel = np.zeros((KEYS, 128), np.float32)
    place = np.full((8, KEYS), 10000, np.int32)
    query = np.zeros((256, 128), np.int32)
    for p in range(4):
        for u in range(8):
            for w in range(4):
                n = p * 32 + u * 4 + w
                i, j = 2 * u + p // 2, 2 * w + p % 2
                sel[n, i * 8 + j] = 1
                place[0, n], place[1, n] = i, j
                query[n, 0] = query[n + 128, 0] = i
                query[n, 1] = query[n + 128, 1] = j
    for (start, _), (down, right) in zip(SEG, WAY):
        rows = {0: range(16), 1: range(13, 16), -1: range(3)}[down]
        cols = {0: range(8), 1: range(5, 8), -1: range(3)}[right]
        n = start
        for i in rows:
            for j in cols:
                sel[n, i * 8 + j] = 1
                place[0, n], place[1, n] = i - 16 * down, j - 8 * right
                n += 1
    return sel, place, query


def kernel(
    x_ref, sel_ref, place_ref, query_ref, gain_ref, wqkv_ref, wout_ref, scale_ref, wmerge_ref, gain2_ref,
    cot_ref, wpack_ref, scale2_ref,
    back_ref,
    out_ref, grad_ref, dw_ref, do_ref,
    inner_ref, ng, cg, wg, tr, qg, kv,
    keys_in, send, kn, vv, qn, fr, bias, ts,
    powers, ones_v, sums, r0, r1, rr0, rr1, gsend, grecv, ps, pr, ws, wt, wsum, wr,
    send_sem, recv_sem, w_s, w_r, f_s, f_r, c_s, c_r, n_s, n_r, a_s, a_r, k_s, k_r,
    g_s, g_r, q_s, q_r, b_s, b_r, p_s, p_r, t_s, t_r, d_s, d_r,
):
    row, col = lax.axis_index("row"), lax.axis_index("col")
    y, core, x, z = lax.div(row, 2), lax.rem(row, 2), lax.div(col, 4), lax.rem(col, 4)
    barrier = pltpu.get_barrier_semaphore()
    peers = [(lax.rem(row + a + 8, 8), lax.rem(col + b + 16, 16)) for a, b in WAY]
    z_peers = [(row, x * 4 + lax.rem(z + off, 4)) for off in RING]
    x_peers = [(row, lax.rem(x + off, 4) * 4 + z) for off in RING]
    twin = (y * 2 + 1 - core, col)
    swap = swap_peers(x, y, z, core)
    for peer in peers + z_peers + x_peers + [twin] + [p for _, _, p in swap]:
        pl.semaphore_signal(barrier, inc=1, device_id=peer, device_id_type=MESH)

    wg[x] = wpack_ref[...]
    cg[z] = cot_ref[...]

    @pl.loop(0, 4)
    def _(img):
        packed = dot(sel_ref[...], x_ref[img]).astype(BF16)
        keys_in[img, 0:128, :] = packed[0:128]
        send[img] = packed[128:352]
        keys_in[img, 352:384, :] = packed[352:384]

    pl.semaphore_wait(barrier, 30)
    copies = []
    for k, ((start, size), peer) in enumerate(zip(SEG, peers)):
        copy = pltpu.make_async_remote_copy(
            src_ref=send.at[:, start - 128 : start - 128 + size, :],
            dst_ref=keys_in.at[:, start : start + size, :],
            send_sem=send_sem.at[k],
            recv_sem=recv_sem.at[k],
            device_id=peer,
            device_id_type=MESH,
        )
        copy.start()
        copies.append(copy)

    half = pl.ds(pl.multiple_of(core * 512, 512), 512)
    w_copies = [
        start_copy(wpack_ref.at[half, :], wg.at[x, half, :], w_s.at[k], w_r.at[k], x_peers[k]) for k in range(3)
    ]

    seen = (
        (jnp.abs(place_ref[0:1, :] - query_ref[:, 0:1]) <= 3)
        & (jnp.abs(place_ref[1:2, :] - query_ref[:, 1:2]) <= 3)
    )
    gi = place_ref[0:1, :] + row * 16
    gj = place_ref[1:2, :] + col * 8
    inside = (gi >= 0) & (gi < 128) & (gj >= 0) & (gj < 128)
    bias[...] = jnp.where(seen & inside, 0.0, -1e30).astype(F32)

    lane = lax.broadcasted_iota(jnp.int32, (128, 128), 1)
    sub = lax.broadcasted_iota(jnp.int32, (128, 128), 0)
    same = jnp.where((lane < 64) == (sub < 64), 1.0 / 64, 0.0).astype(BF16)

    def token_norm(tokens):
        xf = tokens.astype(F32)
        factor = lax.rsqrt(jnp.mean(xf * xf, axis=-1, keepdims=True) + 1e-06)
        return (xf * factor * gain_ref[...]).astype(BF16)

    def head_norm(values):
        vf = values.astype(BF16).astype(F32)
        sq = (vf * vf).astype(BF16)
        parts = [dot(sq[:, k * 128 : k * 128 + 128], same) for k in range(4)]
        return vf * lax.rsqrt(jnp.concatenate(parts, axis=1) + 1e-06)

    @pl.loop(0, 4)
    def _(img):
        nx = token_norm(keys_in[img, 0:128, :])
        qn[img] = (head_norm(dot(nx, wqkv_ref[:, 0:512])) * scale_ref[...]).astype(BF16)
        kn[img, 0:128, :] = head_norm(dot(nx, wqkv_ref[:, 512:1024])).astype(BF16)
        vv[img, 0:128, :] = dot(nx, wqkv_ref[:, 1024:1536]).astype(BF16)

    for copy in copies:
        copy.wait()
    c_copies = [start_copy(cot_ref, cg.at[z], c_s.at[k], c_r.at[k], z_peers[k]) for k in range(3)]

    @pl.loop(0, 4)
    def _(img):
        nx = token_norm(keys_in[img, 128:384, :])
        kn[img, 128:384, :] = head_norm(dot(nx, wqkv_ref[:, 512:1024])).astype(BF16)
        vv[img, 128:384, :] = dot(nx, wqkv_ref[:, 1024:1536]).astype(BF16)

    ones = jnp.ones((KEYS, 128), BF16)

    @pl.loop(0, 4)
    def _(img):
        mixed = []
        for pair in range(4):
            at = slice(pair * 128, pair * 128 + 128)
            q = qn[img, :, at]
            zero = jnp.zeros_like(q)
            both = jnp.concatenate([jnp.where(lane < 64, q, zero), jnp.where(lane < 64, zero, q)], axis=0)
            powered = jnp.exp(dot_nt(both, kn[img, :, at]) + bias[...]).astype(BF16)
            sums = dot(powered, jnp.concatenate([vv[img, :, at], ones], axis=1))
            ratio = sums[:, 0:128] / sums[:, 128:256]
            mixed.append(jnp.where(lane < 64, ratio[0:128], ratio[128:256]).astype(BF16))
        mix = jnp.concatenate(mixed, axis=1)
        fr[img] = (keys_in[img, 0:128, :].astype(F32) + dot(mix, wout_ref[...])).astype(BF16)

    f_copies = []
    for k, off in enumerate(RING):
        w_copies[k].wait()
        block = wg.at[lax.rem(x - off + 4, 4), half, :]
        f_copies.append(start_copy(block, block, f_s.at[k], f_r.at[k], twin))

    merged = jnp.zeros((128, 1024), F32)
    for p in range(4):
        part = jnp.concatenate([fr[img, p * 32 : p * 32 + 32, :] for img in range(4)], axis=0)
        merged = merged + dot(part, wmerge_ref[p * 512 : p * 512 + 512, :])
    inner = merged.astype(BF16)
    inner_ref[...] = inner
    xf = inner.astype(F32)
    factor = lax.rsqrt(jnp.mean(xf * xf, axis=-1, keepdims=True) + 1e-06)
    ng[z] = (xf * factor * gain2_ref[...]).astype(BF16)
    up, down = z_peers[0], z_peers[1]
    above, below, far = lax.rem(z + 1, 4), lax.rem(z + 3, 4), lax.rem(z + 2, 4)
    from_below = start_copy(ng.at[z], ng.at[z], n_s.at[0], n_r.at[0], up)
    from_above = start_copy(ng.at[z], ng.at[z], n_s.at[1], n_r.at[1], down)
    for copy in f_copies + c_copies:
        copy.wait()

    a_copies = []
    far_copies = []
    for step, zi in enumerate((z, below, above, far)):
        if step == 1:
            from_below.wait()
            half_block = ng.at[below, 0:64, :]
            far_copies.append(start_copy(half_block, half_block, n_s.at[2], n_r.at[2], up))
            from_above.wait()
            half_block = ng.at[above, 64:128, :]
            far_copies.append(start_copy(half_block, half_block, n_s.at[3], n_r.at[3], down))
        if step == 3:
            for copy in far_copies:
                copy.wait()
        normed, grads = ng[zi], cg[zi]
        for h in range(4):
            first = dot(normed, wg[h])
            second = dot(grads, wg[h, :, 128:256])
            ts[h, zi, :, 0:128] = first[:, 0:128].astype(BF16)
            ts[h, zi, :, 128:256] = jnp.where(lane < 64, first[:, 128:256], second).astype(BF16)
        for d, (px, py, peer) in enumerate(swap):
            rows = pl.ds(pl.multiple_of(py * 32, 32), 32)
            a_copies.append(
                start_copy(ts.at[px, zi, rows, :], tr.at[x * 4 + y, zi], a_s.at[d, step], a_r.at[d, step], peer)
            )
        tr[x * 4 + y, zi] = ts[x, zi, pl.ds(pl.multiple_of(y * 32, 32), 32), :]

    low = jnp.where(sub < 64, 1.0 / 64, 0.0).astype(BF16)
    for d in range(16):
        if d > 0:
            for step in range(4):
                a_copies[step * 15 + d - 1].wait()
        dx, dy = d // 4, d % 4
        slot = lax.rem(x - dx + 4, 4) * 4 + lax.rem(y - dy + 4, 4)
        raw = tr[slot].reshape(128, 256).astype(F32)
        k_f, q_f = raw[:, 0:128], raw[:, 128:256]
        k_n = k_f * lax.rsqrt(dot((k_f * k_f).astype(BF16), low) + 1e-06)
        q_n = q_f * lax.rsqrt(dot((q_f * q_f).astype(BF16), low) + 1e-06) * scale2_ref[...]
        at = pl.ds(pl.multiple_of(slot * 128, 128), 128)
        kv[0, at, :] = jnp.where(lane < 64, k_n, k_f).astype(BF16)
        qg[at, :] = jnp.where(lane < 64, q_n, q_f).astype(BF16)
    start_copy(kv.at[0], kv.at[1], k_s, k_r, twin).wait()

    for part in range(2):
        ones_v[part] = jnp.where(
            lax.broadcasted_iota(jnp.int32, (2048, 128), 1) < 64, jnp.ones((2048, 128), BF16), kv[part]
        )
    sums[...] = jnp.zeros_like(sums)

    def head_back(values, upstream):
        factor = lax.rsqrt(dot((values * values).astype(BF16), low) + 1e-06)
        unit = values * factor
        grad = factor * (upstream - unit * dot((upstream * unit).astype(BF16), low))
        return jnp.where(lane < 64, grad, upstream).astype(BF16)

    tall = lax.broadcasted_iota(jnp.int32, (BLOCK, 128), 1)
    upper = tall >= 64
    mine = pl.ds(pl.multiple_of(y * 32, 32), 32)
    chunks = [(c // 2, slice(c % 2 * CHUNK, c % 2 * CHUNK + CHUNK), slice(c * CHUNK, c * CHUNK + CHUNK)) for c in range(4)]

    def q_copy(i, dy):
        px, py = lax.rem(x + i + 1, 4), lax.rem(y + dy, 4)
        n = lax.rem(i + 1, 4) * 4 + dy
        return pltpu.make_async_remote_copy(
            src_ref=r1.at[px * 4 + py], dst_ref=rr1.at[x, :, mine, :],
            send_sem=q_s.at[n], recv_sem=q_r.at[n],
            device_id=(py * 2 + core, px * 4 + z), device_id_type=MESH,
        )

    @pl.loop(0, 4)
    def _(i):
        block = lax.rem(x + i + 1, 4)
        tile = qg[pl.ds(pl.multiple_of(block * BLOCK, BLOCK), BLOCK), :]
        q = jnp.where(upper, jnp.zeros_like(tile), tile)
        total = jnp.zeros((BLOCK, 128), F32)
        for part, at, wide_at in chunks:
            powered = jnp.exp2(dot_nt(q, kv[part, at, :])).astype(BF16)
            powers[:, wide_at] = powered
            total = total + dot(powered, ones_v[part, at, :])
        turned = pltpu.roll(total, 64, 1)
        inverse = 1.0 / jnp.where(upper, turned, total)
        outputs = total * inverse
        g = tile.astype(F32)
        delta = jnp.sum(jnp.where(upper, g * outputs, 0.0), axis=1, keepdims=True) * inverse
        high = delta.astype(BF16).astype(F32)
        rest = jnp.where(tall == 0, -high, jnp.where(tall == 1, high - delta, 0.0))
        scaled = jnp.where(upper, g * inverse, rest)
        g_aug = scaled.astype(BF16)
        g_turn = scaled.T[64:128].astype(BF16)
        q_turn = g.T[0:64].astype(BF16)
        grad_q = jnp.zeros((BLOCK, 128), F32)
        for part, at, wide_at in chunks:
            powered = powers[:, wide_at]
            grad_s = (powered.astype(F32) * dot_nt(g_aug, ones_v[part, at, :])).astype(BF16)
            grad_q = grad_q + dot(grad_s, kv[part, at, :])
            sums[64:128, wide_at] += dot(g_turn, powered)
            sums[0:64, wide_at] += dot(q_turn, grad_s)
        both = jnp.where(upper, outputs, grad_q * back_ref[...])
        for py in range(4):
            raw = tr[block * 4 + py, :, :, 128:256].reshape(128, 128).astype(F32)
            r1[block * 4 + py] = head_back(raw, both[py * 128 : py * 128 + 128]).reshape(4, 32, 128)
        for dy in range(1, 4):
            q_copy(i, dy).start()

        @pl.when(i < 3)
        def _():
            q_copy(i, 0).start()

    gsend[...] = sums[:, 2048:4096].astype(BF16)
    g_copy = start_copy(gsend, grecv, g_s, g_r, twin)

    rr1[x, :, mine, :] = r1[x * 4 + y]
    for i in range(4):
        for dy in range(4):
            if i < 3 or dy > 0:
                q_copy(i, dy).wait()

    def out_part(zi):
        term = jnp.zeros((128, 1024), F32)
        for h in range(4):
            last = rr1[h, zi]
            term = term + dot_nt(jnp.where(lane >= 64, last, jnp.zeros_like(last)), wg[h, :, 128:256])
        return term

    def grad_part(zi):
        grad = jnp.zeros((128, 1024), F32)
        for h in range(4):
            last = rr1[h, zi]
            both = jnp.concatenate([rr0[h, zi], jnp.where(lane < 64, last, jnp.zeros_like(last))], axis=1)
            grad = grad + dot_nt(both, wg[h])
        return grad

    p_copies = []

    def send_part(kind, k, value):
        ps[kind, k] = value.astype(BF16)
        n = kind * 3 + k
        p_copies.append(start_copy(ps.at[kind, k], pr.at[kind, k], p_s.at[n], p_r.at[n], z_peers[k]))

    def weight_part(part):
        normed = ng[...].reshape(512, 1024)
        cots = cg[...].reshape(512, 1024)
        for h in range(4):
            if part == 0:
                turned = rr0[h].reshape(512, 128).astype(F32).T.astype(BF16)
                value = dot(turned, normed)
            else:
                turned = rr1[h].reshape(512, 128).astype(F32).T.astype(BF16)
                value = jnp.concatenate([dot(turned[0:64], normed), dot(turned[64:128], cots)], axis=0)
            for band in range(8):
                ws[part, band % 2, h, band // 2] = value[:, band * 128 : band * 128 + 128].astype(BF16)
        return start_copy(ws.at[part, 1 - core], wt.at[part], t_s.at[part], t_r.at[part], twin)

    def weight_send(part, copy):
        copy.wait()
        for h in range(4):
            for py in range(4):
                wsum[part, h, py] = (ws[part, core, h, py].astype(F32) + wt[part, h, py].astype(F32)).astype(BF16)
        copies = []
        for d, (px, py, peer) in enumerate(swap):
            n = part * 15 + d
            copies.append(
                start_copy(wsum.at[part, px, py], wr.at[part, x * 4 + y], d_s.at[n], d_r.at[n], peer)
            )
        wr[part, x * 4 + y] = wsum[part, x, y]
        return copies

    for k in (2, 0, 1):
        send_part(0, k, out_part(lax.rem(z + RING[k], 4)))

    g_copy.wait()

    def prepare(slot):
        at = pl.ds(pl.multiple_of(slot * 128, 128), 128)
        upstream = (sums[:, at] + grecv[:, at].astype(F32)).T
        upstream = jnp.where(lane < 64, upstream * LN2, upstream)
        raw = tr[slot, :, :, 0:128].reshape(128, 128).astype(F32)
        r0[slot] = head_back(raw, upstream).reshape(4, 32, 128)

    b_copies = []
    for d, (px, py, peer) in enumerate(swap):
        prepare(px * 4 + py)
        b_copies.append(start_copy(r0.at[px * 4 + py], rr0.at[x, :, mine, :], b_s.at[d], b_r.at[d], peer))
    prepare(x * 4 + y)
    rr0[x, :, mine, :] = r0[x * 4 + y]

    term = out_part(z)
    w_copy = weight_part(1)
    for copy in b_copies:
        copy.wait()
    d_copies = weight_send(1, w_copy)
    for k in (2, 0, 1):
        send_part(1, k, grad_part(lax.rem(z + RING[k], 4)))
    w_copy = weight_part(0)
    grad = grad_part(z)
    d_copies += weight_send(0, w_copy)

    for copy in p_copies:
        copy.wait()
    for k in range(3):
        term = term + pr[0, k].astype(F32)
        grad = grad + pr[1, k].astype(F32)
    values = inner_ref[...].astype(F32)
    out_ref[...] = (values + term).astype(BF16)
    factor = lax.rsqrt(jnp.mean(values * values, axis=-1, keepdims=True) + 1e-06)
    unit = values * factor
    upstream = grad * gain2_ref[...]
    grad_ref[...] = cot_ref[...].astype(F32) + factor * (
        upstream - unit * jnp.mean(upstream * unit, axis=-1, keepdims=True)
    )

    for copy in d_copies:
        copy.wait()
    total = jnp.zeros((128, 128), F32)
    for n in range(16):
        total = total + wr[1, n].astype(F32)
    do_ref[...] = total[64:128]
    dw_ref[0] = total.T[:, 0:64]
    total = jnp.zeros((128, 128), F32)
    for n in range(16):
        total = total + wr[0, n].astype(F32)
    turned = total.T
    dw_ref[1] = turned[:, 0:64]
    dw_ref[2] = turned[:, 64:128]


def per_device(
    fine_input,
    gain_fine,
    fine_qkv,
    fine_out,
    fine_scale,
    merge_weight,
    gain_coarse,
    coarse_qkv,
    coarse_out,
    coarse_scale,
    cotangent,
):
    cot = cotangent.reshape(128, 1024)
    wpack = jnp.concatenate([coarse_qkv[1], coarse_qkv[2], coarse_qkv[0], coarse_out.T], axis=1)
    back_scale = jnp.broadcast_to(coarse_scale.reshape(1, 1) / 64, (1, 128))
    sel, place, query = fine_tables()
    vmem = pl.BlockSpec(memory_space=pltpu.VMEM)
    dma = pltpu.SemaphoreType.DMA
    output, grad, qkv_grad, out_grad = pl.pallas_call(
        kernel,
        out_shape=(
            jax.ShapeDtypeStruct((128, 1024), BF16),
            jax.ShapeDtypeStruct((128, 1024), F32),
            jax.ShapeDtypeStruct((3, 128, 64), F32),
            jax.ShapeDtypeStruct((64, 128), F32),
        ),
        in_specs=[vmem] * 14,
        out_specs=(vmem,) * 4,
        scratch_shapes=[
            pltpu.VMEM((128, 1024), BF16),
            pltpu.VMEM((4, 128, 1024), BF16),
            pltpu.VMEM((4, 128, 1024), BF16),
            pltpu.VMEM((4, 1024, 256), BF16),
            pltpu.VMEM((16, 4, 32, 256), BF16),
            pltpu.VMEM((2048, 128), BF16),
            pltpu.VMEM((2, 2048, 128), BF16),
            pltpu.VMEM((4, KEYS, 512), BF16),
            pltpu.VMEM((4, 224, 512), BF16),
            pltpu.VMEM((4, KEYS, 512), BF16),
            pltpu.VMEM((4, KEYS, 512), BF16),
            pltpu.VMEM((4, 128, 512), BF16),
            pltpu.VMEM((4, 128, 512), BF16),
            pltpu.VMEM((256, KEYS), F32),
            pltpu.VMEM((4, 4, 128, 256), BF16),
            pltpu.VMEM((BLOCK, 4096), BF16),
            pltpu.VMEM((2, 2048, 128), BF16),
            pltpu.VMEM((128, 4096), F32),
            pltpu.VMEM((16, 4, 32, 128), BF16),
            pltpu.VMEM((16, 4, 32, 128), BF16),
            pltpu.VMEM((4, 4, 128, 128), BF16),
            pltpu.VMEM((4, 4, 128, 128), BF16),
            pltpu.VMEM((128, 2048), BF16),
            pltpu.VMEM((128, 2048), BF16),
            pltpu.VMEM((2, 3, 128, 1024), BF16),
            pltpu.VMEM((2, 3, 128, 1024), BF16),
            pltpu.VMEM((2, 2, 4, 4, 128, 128), BF16),
            pltpu.VMEM((2, 4, 4, 128, 128), BF16),
            pltpu.VMEM((2, 4, 4, 128, 128), BF16),
            pltpu.VMEM((2, 16, 128, 128), BF16),
            dma((8,)), dma((8,)),
            dma((3,)), dma((3,)), dma((3,)), dma((3,)), dma((3,)), dma((3,)), dma((4,)), dma((4,)),
            dma((15, 4)), dma((15, 4)), dma(()), dma(()),
            dma(()), dma(()), dma((16,)), dma((16,)), dma((15,)), dma((15,)), dma((6,)), dma((6,)),
            dma((2,)), dma((2,)), dma((30,)), dma((30,)),
        ],
        compiler_params=pltpu.CompilerParams(
            collective_id=0, has_side_effects=True, vmem_limit_bytes=58 * 1024 * 1024
        ),
        cost_estimate=pl.CostEstimate(flops=36_000_000_000, bytes_accessed=16_000_000, transcendentals=12_000_000),
        name="step",
    )(
        fine_input.reshape(4, 128, 512),
        jnp.asarray(sel, BF16),
        jnp.asarray(place),
        jnp.asarray(query),
        gain_fine.reshape(1, 512),
        fine_qkv,
        fine_out,
        jnp.repeat(fine_scale / 64, 64).reshape(1, 512),
        merge_weight,
        gain_coarse.reshape(1, 1024),
        cot,
        wpack,
        back_scale * LOG2E,
        back_scale,
    )
    return (output.reshape(4, 8, 4, 1024), grad.reshape(4, 8, 4, 1024), qkv_grad, out_grad)


def solution(mesh):
    return jax.shard_map(
        per_device,
        mesh=mesh,
        in_specs=(
            P(None, "row", "col", None),
            P(),
            P(),
            P(),
            P(),
            P(),
            P(),
            P(None, None, "col"),
            P("col", None),
            P("col"),
            P(None, "row", "col", None),
        ),
        out_specs=(
            P(None, "row", "col", None),
            P(None, "row", "col", None),
            P(None, "row", "col"),
            P("col", "row"),
        ),
        check_vma=False,
    )
```

time: 170 us -> 139 us (0.82)
  Pallas kernels: 158 us -> 124 us
  local copies, waits for them, and re-layouts: 9.31 us -> 12.9 us
    pallas_call x3 -> x1, Pallas kernels: 158 us -> 124 us  [per_device(): pl.pallas_call(kernel, out_shape=(jax.ShapeDtypeStruct((128, 1024), BF16)...]
    unnamed x26 -> x8, local copies, waits for them, and re-layouts: 5.33 us -> 4.65 us
where the time goes in v3:
time: 139 us
  Pallas kernels  124 us (89%)
  local copies, waits for them, and re-layouts  12.9 us (9%)
    pallas_call x1, Pallas kernels, per_device(): pl.pallas_call(kernel, out_shape=(jax.ShapeDtypeStruct((128, 1024), BF16)...  124 us
    unnamed x8, local copies, waits for them, and re-layouts  4.65 us

profile of v3, /device:TPU:1, one launch (start us, length us, event | category | flops | bytes accessed | tf_op | source)
XLA Modules:
  0.0 139.1 jit_solution(3945323462549144421)
XLA Ops:
  0.6 0.0 copy-start
  0.6 1.1 fusion
  1.7 0.2 copy.23
  1.9 0.2 copy.24
  2.1 0.2 copy.25
  2.2 1.1 copy.21
  3.3 1.1 pad_maximum_fusion.wpack_ref
  5.1 0.5 broadcast_in_dim.13.scale2_ref
  5.6 0.5 broadcast_in_dim.15.back_ref
  6.1 1.7 %reshape.43.cot_ref = bf16[128,1024]{1,0:T(8,128)(2,1)} reshape(bf16[4,8,4,1024]{3,2,1,0:T(4,128)(2,1)} %param.24) | data formatting | bytes 524288 | tf_op jit(solution)/shard_map/reshape | solution.py:440
  7.9 0.0 copy-done
  7.9 0.1 broadcast_in_dim.12
  7.9 0.7 reshape_reshape.3.scale_ref
  8.6 123.7 %step.1 = (bf16[128,1024]{1,0:T(8,128)(2,1)}, f32[128,1024]{1,0:T(8,128)}, f32[3,128,64]{2,1,0:T(8,128)}, f32[64,128]{1,0:T(8,128)}) custom-call(bf16[4,128,512]{2,1,0:T(8,128)(2,1)} %bitcast.13, bf16[384,128]{1,0:T(8,128)(2,1)} %constant.19.clone.sel_ref, s32[8,384]{1,0:T(8,128)} %constant.20.clone.place_ref, s32[256,128]{1,0:T(8,128)} %constant.21.clone.query_ref, ...), custom_call_target="tpu_custom_call" | custom-call | flops 35999997952 | bytes 16000000 | tf_op jit(solution)/shard_map/step/pallas_call | solution.py:446
  132.3 2.0 %reshape.45 = f32[4,8,4,1024]{3,2,1,0:T(4,128)} reshape(f32[128,1024]{1,0:T(8,128)} %get-tuple-element.9) | data formatting | bytes 1048576 | tf_op jit(solution)/shard_map/reshape | solution.py:514
  134.3 1.8 %reshape.44 = bf16[4,8,4,1024]{3,2,1,0:T(4,128)(2,1)} reshape(bf16[128,1024]{1,0:T(8,128)(2,1)} %get-tuple-element.8) | data formatting | bytes 524288 | tf_op jit(solution)/shard_map/reshape | solution.py:514
  136.1 1.7 %copy.22 = f32[3,128,64]{1,2,0:T(8,128)} copy(f32[3,128,64]{2,1,0:T(8,128)} %get-tuple-element.14) | data formatting | bytes 196608
  137.7 1.4 copy.28
  (1 shorter events, 0.0 us)
Async XLA Ops:
  0.6 7.2 %copy-start = (f32[8]{0:T(128)S(1)}, f32[8]{0:T(128)}, u32[]{:S(2)}) copy-start(f32[8]{0:T(128)} %param.18) | copy-start | bytes 100

commit v4 on v3

--- a/solution.py
+++ b/solution.py
@@ -14,7 +14,6 @@
 KEYS = 384
 RING = (1, 3, 2)
 BLOCK = 512
-CHUNK = 1024
 LOG2E = 1.4426950408889634
 LN2 = 0.6931471805599453
 
@@ -69,15 +68,15 @@
 
 
 def kernel(
-    x_ref, sel_ref, place_ref, query_ref, gain_ref, wqkv_ref, wout_ref, scale_ref, wmerge_ref, gain2_ref,
-    cot_ref, wpack_ref, scale2_ref,
-    back_ref,
+    x_ref, sel_ref, place_ref, query_ref, gain_ref, wqkv_hbm, wout_hbm, scale_ref, wmerge_hbm, gain2_ref,
+    cot_ref, heads_ref, proj_ref, scale2_ref,
     out_ref, grad_ref, dw_ref, do_ref,
     inner_ref, ng, cg, wg, tr, qg, kv,
     keys_in, send, kn, vv, qn, fr, bias, ts,
-    powers, ones_v, sums, r0, r1, rr0, rr1, gsend, grecv, ps, pr, ws, wt, wsum, wr,
+    powers, ones_v, kvt, vt, g_aug, g_turn, q_turn, gq_turn,
+    r0, r1, rq, rr0, rr1, rrq, gsend, grecv, ps, pr, ws, wt, wsum, wr,
     send_sem, recv_sem, w_s, w_r, f_s, f_r, c_s, c_r, n_s, n_r, a_s, a_r, k_s, k_r,
-    g_s, g_r, q_s, q_r, b_s, b_r, p_s, p_r, t_s, t_r, d_s, d_r,
+    g_s, g_r, q_s, q_r, b_s, b_r, e_s, e_r, p_s, p_r, t_s, t_r, d_s, d_r, l_s,
 ):
     row, col = lax.axis_index("row"), lax.axis_index("col")
     y, core, x, z = lax.div(row, 2), lax.rem(row, 2), lax.div(col, 4), lax.rem(col, 4)
@@ -90,8 +89,25 @@
     for peer in peers + z_peers + x_peers + [twin] + [p for _, _, p in swap]:
         pl.semaphore_signal(barrier, inc=1, device_id=peer, device_id_type=MESH)
 
-    wg[x] = wpack_ref[...]
-    cg[z] = cot_ref[...]
+    wqkv_ref = powers.at[0:512, 1024:2560]
+    wout_ref = powers.at[512:1024, 1024:1536]
+    wmerge_ref = powers.at[:, 0:1024]
+    loads = [
+        pltpu.make_async_copy(wqkv_hbm, wqkv_ref, l_s.at[0]),
+        pltpu.make_async_copy(wout_hbm, wout_ref, l_s.at[1]),
+        pltpu.make_async_copy(wmerge_hbm, wmerge_ref, l_s.at[2]),
+    ]
+    for load in loads:
+        load.start()
+    wg[x] = jnp.concatenate(
+        [heads_ref[1], heads_ref[2], heads_ref[0], proj_ref[...].astype(F32).T.astype(BF16)], axis=1
+    )
+    cg[z] = cot_ref[...].reshape(128, 1024)
+    back = scale2_ref[...] * (1.0 / 64)
+    head_of = lax.shift_right_logical(lax.broadcasted_iota(jnp.int32, (1, 512), 1), 6)
+    fine_scale = jnp.zeros((1, 512), F32)
+    for h in range(8):
+        fine_scale = jnp.where(head_of == h, scale_ref[0:1, h : h + 1] * (1.0 / 64), fine_scale)
 
     @pl.loop(0, 4)
     def _(img):
@@ -116,7 +132,7 @@
 
     half = pl.ds(pl.multiple_of(core * 512, 512), 512)
     w_copies = [
-        start_copy(wpack_ref.at[half, :], wg.at[x, half, :], w_s.at[k], w_r.at[k], x_peers[k]) for k in range(3)
+        start_copy(wg.at[x, half, :], wg.at[x, half, :], w_s.at[k], w_r.at[k], x_peers[k]) for k in range(3)
     ]
 
     seen = (
@@ -143,16 +159,18 @@
         parts = [dot(sq[:, k * 128 : k * 128 + 128], same) for k in range(4)]
         return vf * lax.rsqrt(jnp.concatenate(parts, axis=1) + 1e-06)
 
+    loads[0].wait()
+
     @pl.loop(0, 4)
     def _(img):
         nx = token_norm(keys_in[img, 0:128, :])
-        qn[img] = (head_norm(dot(nx, wqkv_ref[:, 0:512])) * scale_ref[...]).astype(BF16)
+        qn[img] = (head_norm(dot(nx, wqkv_ref[:, 0:512])) * fine_scale).astype(BF16)
         kn[img, 0:128, :] = head_norm(dot(nx, wqkv_ref[:, 512:1024])).astype(BF16)
         vv[img, 0:128, :] = dot(nx, wqkv_ref[:, 1024:1536]).astype(BF16)
 
     for copy in copies:
         copy.wait()
-    c_copies = [start_copy(cot_ref, cg.at[z], c_s.at[k], c_r.at[k], z_peers[k]) for k in range(3)]
+    c_copies = [start_copy(cg.at[z], cg.at[z], c_s.at[k], c_r.at[k], z_peers[k]) for k in range(3)]
 
     @pl.loop(0, 4)
     def _(img):
@@ -161,6 +179,8 @@
         vv[img, 128:384, :] = dot(nx, wqkv_ref[:, 1024:1536]).astype(BF16)
 
     ones = jnp.ones((KEYS, 128), BF16)
+    loads[1].wait()
+    loads[2].wait()
 
     @pl.loop(0, 4)
     def _(img):
@@ -235,99 +255,117 @@
         raw = tr[slot].reshape(128, 256).astype(F32)
         k_f, q_f = raw[:, 0:128], raw[:, 128:256]
         k_n = k_f * lax.rsqrt(dot((k_f * k_f).astype(BF16), low) + 1e-06)
-        q_n = q_f * lax.rsqrt(dot((q_f * q_f).astype(BF16), low) + 1e-06) * scale2_ref[...]
+        q_n = q_f * lax.rsqrt(dot((q_f * q_f).astype(BF16), low) + 1e-06) * (back * LOG2E)
         at = pl.ds(pl.multiple_of(slot * 128, 128), 128)
-        kv[0, at, :] = jnp.where(lane < 64, k_n, k_f).astype(BF16)
+        kv[at, :] = jnp.where(lane < 64, k_n, k_f).astype(BF16)
         qg[at, :] = jnp.where(lane < 64, q_n, q_f).astype(BF16)
-    start_copy(kv.at[0], kv.at[1], k_s, k_r, twin).wait()
-
-    for part in range(2):
-        ones_v[part] = jnp.where(
-            lax.broadcasted_iota(jnp.int32, (2048, 128), 1) < 64, jnp.ones((2048, 128), BF16), kv[part]
-        )
-    sums[...] = jnp.zeros_like(sums)
-
-    def head_back(values, upstream):
-        factor = lax.rsqrt(dot((values * values).astype(BF16), low) + 1e-06)
+    k_copy = start_copy(kv.at[0:2048, :], kv.at[2048:4096, :], k_s, k_r, twin)
+
+    def key_side(c):
+        at = slice(c * 512, c * 512 + 512)
+        tile = kv[at, :]
+        ones_v[at, :] = jnp.where(lax.broadcasted_iota(jnp.int32, (512, 128), 1) < 64, jnp.ones_like(tile), tile)
+        turned = tile.astype(F32).T.astype(BF16)
+        kvt[:, at] = turned[0:64]
+        vt[0:64, at] = turned[64:128]
+
+    vt[64:80, :] = jnp.ones((16, 4096), BF16)
+    for c in range(4):
+        key_side(c)
+    k_copy.wait()
+    for c in range(4, 8):
+        key_side(c)
+
+    def head_back(values, upstream, means):
+        factor = lax.rsqrt(dot((values * values).astype(BF16), means) + 1e-06)
         unit = values * factor
-        grad = factor * (upstream - unit * dot((upstream * unit).astype(BF16), low))
-        return jnp.where(lane < 64, grad, upstream).astype(BF16)
+        return factor * (upstream - unit * dot((upstream * unit).astype(BF16), means))
 
     tall = lax.broadcasted_iota(jnp.int32, (BLOCK, 128), 1)
-    upper = tall >= 64
+    sub64 = lax.broadcasted_iota(jnp.int32, (64, BLOCK), 0)
     mine = pl.ds(pl.multiple_of(y * 32, 32), 32)
-    chunks = [(c // 2, slice(c % 2 * CHUNK, c % 2 * CHUNK + CHUNK), slice(c * CHUNK, c * CHUNK + CHUNK)) for c in range(4)]
-
-    def q_copy(i, dy):
+
+    def block_copy(source, target, send, recv, i, dy):
         px, py = lax.rem(x + i + 1, 4), lax.rem(y + dy, 4)
         n = lax.rem(i + 1, 4) * 4 + dy
         return pltpu.make_async_remote_copy(
-            src_ref=r1.at[px * 4 + py], dst_ref=rr1.at[x, :, mine, :],
-            send_sem=q_s.at[n], recv_sem=q_r.at[n],
+            src_ref=source.at[px * 4 + py], dst_ref=target.at[x, :, mine, :],
+            send_sem=send.at[n], recv_sem=recv.at[n],
             device_id=(py * 2 + core, px * 4 + z), device_id_type=MESH,
         )
 
+    def block_start(source, target, send, recv, i):
+        for dy in range(1, 4):
+            block_copy(source, target, send, recv, i, dy).start()
+
+        @pl.when(i < 3)
+        def _():
+            block_copy(source, target, send, recv, i, 0).start()
+
+    def block_finish(source, target, send, recv):
+        target[x, :, mine, :] = source[x * 4 + y]
+        for i in range(4):
+            for dy in range(4):
+                if i < 3 or dy > 0:
+                    block_copy(source, target, send, recv, i, dy).wait()
+
     @pl.loop(0, 4)
     def _(i):
         block = lax.rem(x + i + 1, 4)
-        tile = qg[pl.ds(pl.multiple_of(block * BLOCK, BLOCK), BLOCK), :]
-        q = jnp.where(upper, jnp.zeros_like(tile), tile)
-        total = jnp.zeros((BLOCK, 128), F32)
-        for part, at, wide_at in chunks:
-            powered = jnp.exp2(dot_nt(q, kv[part, at, :])).astype(BF16)
-            powers[:, wide_at] = powered
-            total = total + dot(powered, ones_v[part, at, :])
-        turned = pltpu.roll(total, 64, 1)
-        inverse = 1.0 / jnp.where(upper, turned, total)
-        outputs = total * inverse
-        g = tile.astype(F32)
-        delta = jnp.sum(jnp.where(upper, g * outputs, 0.0), axis=1, keepdims=True) * inverse
+        rows = pl.ds(pl.multiple_of(block * BLOCK, BLOCK), BLOCK)
+        tile = qg[rows, :]
+        q = jnp.where(tall < 64, tile, jnp.zeros_like(tile))
+        for c in range(8):
+            at = slice(c * 512, c * 512 + 512)
+            powers[rows, at] = jnp.exp2(dot_nt(q, kv[at, :])).astype(BF16)
+        total = dot_nt(vt[...], powers[rows, :])
+        turned = tile.astype(F32).T
+        inverse = 1.0 / total[64:65]
+        outputs = total[0:64] * inverse
+        g = turned[64:128]
+        delta = jnp.sum(g * outputs, axis=0, keepdims=True) * inverse
         high = delta.astype(BF16).astype(F32)
-        rest = jnp.where(tall == 0, -high, jnp.where(tall == 1, high - delta, 0.0))
-        scaled = jnp.where(upper, g * inverse, rest)
-        g_aug = scaled.astype(BF16)
-        g_turn = scaled.T[64:128].astype(BF16)
-        q_turn = g.T[0:64].astype(BF16)
-        grad_q = jnp.zeros((BLOCK, 128), F32)
-        for part, at, wide_at in chunks:
-            powered = powers[:, wide_at]
-            grad_s = (powered.astype(F32) * dot_nt(g_aug, ones_v[part, at, :])).astype(BF16)
-            grad_q = grad_q + dot(grad_s, kv[part, at, :])
-            sums[64:128, wide_at] += dot(g_turn, powered)
-            sums[0:64, wide_at] += dot(q_turn, grad_s)
-        both = jnp.where(upper, outputs, grad_q * back_ref[...])
+        rest = jnp.where(sub64 == 0, -high, jnp.where(sub64 == 1, high - delta, 0.0))
+        scaled = g * inverse
+        g_turn[:, rows] = scaled.astype(BF16)
+        q_turn[:, rows] = turned[0:64].astype(BF16)
+        g_aug[rows, :] = jnp.concatenate([rest, scaled], axis=0).T.astype(BF16)
+        attn = jnp.concatenate([jnp.zeros_like(outputs), outputs], axis=0).T.astype(BF16)
         for py in range(4):
-            raw = tr[block * 4 + py, :, :, 128:256].reshape(128, 128).astype(F32)
-            r1[block * 4 + py] = head_back(raw, both[py * 128 : py * 128 + 128]).reshape(4, 32, 128)
-        for dy in range(1, 4):
-            q_copy(i, dy).start()
-
-        @pl.when(i < 3)
-        def _():
-            q_copy(i, 0).start()
-
-    gsend[...] = sums[:, 2048:4096].astype(BF16)
+            r1[block * 4 + py] = attn[py * 128 : py * 128 + 128].reshape(4, 32, 128)
+        block_start(r1, rr1, q_s, q_r, i)
+
+    gq_turn[...] = jnp.zeros_like(gq_turn)
+
+    def key_block(at):
+        powered = powers[:, at]
+        value_part = dot(g_turn[...], powered)
+        powers[:, at] = (powered.astype(F32) * dot_nt(g_aug[...], ones_v[at, :])).astype(BF16)
+        grad_s = powers[:, at]
+        key_part = dot(q_turn[...], grad_s)
+        gq_turn[...] += dot_nt(kvt[:, at], grad_s)
+        return jnp.concatenate([key_part * LN2, value_part], axis=0)
+
+    @pl.loop(0, 4)
+    def _(i):
+        at = pl.ds(pl.multiple_of(i * 512, 512), 512)
+        gsend[:, at] = key_block(pl.ds(pl.multiple_of(2048 + i * 512, 512), 512)).astype(BF16)
+
     g_copy = start_copy(gsend, grecv, g_s, g_r, twin)
-
-    rr1[x, :, mine, :] = r1[x * 4 + y]
-    for i in range(4):
-        for dy in range(4):
-            if i < 3 or dy > 0:
-                q_copy(i, dy).wait()
+    block_finish(r1, rr1, q_s, q_r)
 
     def out_part(zi):
         term = jnp.zeros((128, 1024), F32)
         for h in range(4):
-            last = rr1[h, zi]
-            term = term + dot_nt(jnp.where(lane >= 64, last, jnp.zeros_like(last)), wg[h, :, 128:256])
+            term = term + dot_nt(rr1[h, zi], wg[h, :, 128:256])
         return term
 
     def grad_part(zi):
         grad = jnp.zeros((128, 1024), F32)
         for h in range(4):
-            last = rr1[h, zi]
-            both = jnp.concatenate([rr0[h, zi], jnp.where(lane < 64, last, jnp.zeros_like(last))], axis=1)
-            grad = grad + dot_nt(both, wg[h])
+            packed = rrq[h, lax.rem(zi, 2)].astype(F32)
+            last = jnp.where(lane < 64, jnp.where(zi < 2, packed, pltpu.roll(packed, 64, 1)), 0.0).astype(BF16)
+            grad = grad + dot_nt(jnp.concatenate([rr0[h, zi], last], axis=1), wg[h])
         return grad
 
     p_copies = []
@@ -345,8 +383,10 @@
                 turned = rr0[h].reshape(512, 128).astype(F32).T.astype(BF16)
                 value = dot(turned, normed)
             else:
-                turned = rr1[h].reshape(512, 128).astype(F32).T.astype(BF16)
-                value = jnp.concatenate([dot(turned[0:64], normed), dot(turned[64:128], cots)], axis=0)
+                turned = rr1[h].reshape(512, 128).astype(F32).T.astype(BF16)[64:128]
+                even, odd = rrq[h, 0].astype(F32).T, rrq[h, 1].astype(F32).T
+                grad_q = jnp.concatenate([even[0:64], odd[0:64], even[64:128], odd[64:128]], axis=1).astype(BF16)
+                value = jnp.concatenate([dot(grad_q, normed), dot(turned, cots)], axis=0)
             for band in range(8):
                 ws[part, band % 2, h, band // 2] = value[:, band * 128 : band * 128 + 128].astype(BF16)
         return start_copy(ws.at[part, 1 - core], wt.at[part], t_s.at[part], t_r.at[part], twin)
@@ -368,32 +408,49 @@
     for k in (2, 0, 1):
         send_part(0, k, out_part(lax.rem(z + RING[k], 4)))
 
-    g_copy.wait()
-
-    def prepare(slot):
-        at = pl.ds(pl.multiple_of(slot * 128, 128), 128)
-        upstream = (sums[:, at] + grecv[:, at].astype(F32)).T
-        upstream = jnp.where(lane < 64, upstream * LN2, upstream)
-        raw = tr[slot, :, :, 0:128].reshape(128, 128).astype(F32)
-        r0[slot] = head_back(raw, upstream).reshape(4, 32, 128)
-
-    b_copies = []
-    for d, (px, py, peer) in enumerate(swap):
-        prepare(px * 4 + py)
-        b_copies.append(start_copy(r0.at[px * 4 + py], rr0.at[x, :, mine, :], b_s.at[d], b_r.at[d], peer))
-    prepare(x * 4 + y)
-    rr0[x, :, mine, :] = r0[x * 4 + y]
-
+    @pl.loop(0, 4)
+    def _(i):
+        block = lax.rem(x + i + 1, 4)
+        at = pl.ds(pl.multiple_of(block * 512, 512), 512)
+        own = key_block(at)
+
+        @pl.when(i == 0)
+        def _():
+            pltpu.make_async_remote_copy(
+                src_ref=gsend, dst_ref=grecv, send_sem=g_s, recv_sem=g_r, device_id=twin, device_id_type=MESH
+            ).wait()
+
+        upstream = (own + grecv[:, at].astype(F32)).T
+        for py in range(4):
+            raw = tr[block * 4 + py, :, :, 0:128].reshape(128, 128).astype(F32)
+            part = upstream[py * 128 : py * 128 + 128]
+            r0[block * 4 + py] = (
+                jnp.where(lane < 64, head_back(raw, part, low), part).astype(BF16).reshape(4, 32, 128)
+            )
+        block_start(r0, rr0, b_s, b_r, i)
+
+    @pl.loop(0, 4)
+    def _(i):
+        block = lax.rem(x + i + 1, 4)
+        for py in range(4):
+            slot = block * 4 + py
+            part = gq_turn[:, pl.ds(pl.multiple_of(slot * 128, 128), 128)] * back
+            packed = jnp.concatenate([part[:, 0:64], part[:, 64:128]], axis=0).T
+            raw = tr[slot, :, :, 128:256].reshape(128, 128).astype(F32)
+            raw = jnp.where(lane[0:64] < 64, raw[0:64], pltpu.roll(raw[64:128], 64, 1))
+            rq[slot] = head_back(raw, packed, same).astype(BF16).reshape(2, 32, 128)
+        block_start(rq, rrq, e_s, e_r, i)
+
+    block_finish(r0, rr0, b_s, b_r)
+    w_copy = weight_part(0)
     term = out_part(z)
-    w_copy = weight_part(1)
-    for copy in b_copies:
-        copy.wait()
-    d_copies = weight_send(1, w_copy)
+    block_finish(rq, rrq, e_s, e_r)
     for k in (2, 0, 1):
         send_part(1, k, grad_part(lax.rem(z + RING[k], 4)))
-    w_copy = weight_part(0)
+    d_copies = weight_send(0, w_copy)
+    w_copy = weight_part(1)
     grad = grad_part(z)
-    d_copies += weight_send(0, w_copy)
+    d_copies += weight_send(1, w_copy)
 
     for copy in p_copies:
         copy.wait()
@@ -401,13 +458,14 @@
         term = term + pr[0, k].astype(F32)
         grad = grad + pr[1, k].astype(F32)
     values = inner_ref[...].astype(F32)
-    out_ref[...] = (values + term).astype(BF16)
+    out_ref[...] = (values + term).astype(BF16).reshape(32, 4, 1024)
     factor = lax.rsqrt(jnp.mean(values * values, axis=-1, keepdims=True) + 1e-06)
     unit = values * factor
     upstream = grad * gain2_ref[...]
-    grad_ref[...] = cot_ref[...].astype(F32) + factor * (
+    grad = cg[z].astype(F32) + factor * (
         upstream - unit * jnp.mean(upstream * unit, axis=-1, keepdims=True)
     )
+    grad_ref[...] = grad.reshape(32, 4, 1024)
 
     for copy in d_copies:
         copy.wait()
@@ -437,21 +495,19 @@
     coarse_scale,
     cotangent,
 ):
-    cot = cotangent.reshape(128, 1024)
-    wpack = jnp.concatenate([coarse_qkv[1], coarse_qkv[2], coarse_qkv[0], coarse_out.T], axis=1)
-    back_scale = jnp.broadcast_to(coarse_scale.reshape(1, 1) / 64, (1, 128))
     sel, place, query = fine_tables()
     vmem = pl.BlockSpec(memory_space=pltpu.VMEM)
+    hbm = pl.BlockSpec(memory_space=pl.ANY)
     dma = pltpu.SemaphoreType.DMA
     output, grad, qkv_grad, out_grad = pl.pallas_call(
         kernel,
         out_shape=(
-            jax.ShapeDtypeStruct((128, 1024), BF16),
-            jax.ShapeDtypeStruct((128, 1024), F32),
+            jax.ShapeDtypeStruct((32, 4, 1024), BF16),
+            jax.ShapeDtypeStruct((32, 4, 1024), F32),
             jax.ShapeDtypeStruct((3, 128, 64), F32),
             jax.ShapeDtypeStruct((64, 128), F32),
         ),
-        in_specs=[vmem] * 14,
+        in_specs=[vmem] * 5 + [hbm, hbm, vmem, hbm] + [vmem] * 5,
         out_specs=(vmem,) * 4,
         scratch_shapes=[
             pltpu.VMEM((128, 1024), BF16),
@@ -460,7 +516,7 @@
             pltpu.VMEM((4, 1024, 256), BF16),
             pltpu.VMEM((16, 4, 32, 256), BF16),
             pltpu.VMEM((2048, 128), BF16),
-            pltpu.VMEM((2, 2048, 128), BF16),
+            pltpu.VMEM((4096, 128), BF16),
             pltpu.VMEM((4, KEYS, 512), BF16),
             pltpu.VMEM((4, 224, 512), BF16),
             pltpu.VMEM((4, KEYS, 512), BF16),
@@ -469,13 +525,20 @@
             pltpu.VMEM((4, 128, 512), BF16),
             pltpu.VMEM((256, KEYS), F32),
             pltpu.VMEM((4, 4, 128, 256), BF16),
-            pltpu.VMEM((BLOCK, 4096), BF16),
-            pltpu.VMEM((2, 2048, 128), BF16),
-            pltpu.VMEM((128, 4096), F32),
+            pltpu.VMEM((2048, 4096), BF16),
+            pltpu.VMEM((4096, 128), BF16),
+            pltpu.VMEM((64, 4096), BF16),
+            pltpu.VMEM((80, 4096), BF16),
+            pltpu.VMEM((2048, 128), BF16),
+            pltpu.VMEM((64, 2048), BF16),
+            pltpu.VMEM((64, 2048), BF16),
+            pltpu.VMEM((64, 2048), F32),
             pltpu.VMEM((16, 4, 32, 128), BF16),
             pltpu.VMEM((16, 4, 32, 128), BF16),
+            pltpu.VMEM((16, 2, 32, 128), BF16),
             pltpu.VMEM((4, 4, 128, 128), BF16),
             pltpu.VMEM((4, 4, 128, 128), BF16),
+            pltpu.VMEM((4, 2, 128, 128), BF16),
             pltpu.VMEM((128, 2048), BF16),
             pltpu.VMEM((128, 2048), BF16),
             pltpu.VMEM((2, 3, 128, 1024), BF16),
@@ -487,11 +550,11 @@
             dma((8,)), dma((8,)),
             dma((3,)), dma((3,)), dma((3,)), dma((3,)), dma((3,)), dma((3,)), dma((4,)), dma((4,)),
             dma((15, 4)), dma((15, 4)), dma(()), dma(()),
-            dma(()), dma(()), dma((16,)), dma((16,)), dma((15,)), dma((15,)), dma((6,)), dma((6,)),
-            dma((2,)), dma((2,)), dma((30,)), dma((30,)),
+            dma(()), dma(()), dma((16,)), dma((16,)), dma((16,)), dma((16,)), dma((16,)), dma((16,)), dma((6,)), dma((6,)),
+            dma((2,)), dma((2,)), dma((30,)), dma((30,)), dma((3,)),
         ],
         compiler_params=pltpu.CompilerParams(
-            collective_id=0, has_side_effects=True, vmem_limit_bytes=58 * 1024 * 1024
+            collective_id=0, has_side_effects=True, vmem_limit_bytes=60 * 1024 * 1024
         ),
         cost_estimate=pl.CostEstimate(flops=36_000_000_000, bytes_accessed=16_000_000, transcendentals=12_000_000),
         name="step",
@@ -503,13 +566,13 @@
         gain_fine.reshape(1, 512),
         fine_qkv,
         fine_out,
-        jnp.repeat(fine_scale / 64, 64).reshape(1, 512),
+        fine_scale.reshape(1, 8),
         merge_weight,
         gain_coarse.reshape(1, 1024),
-        cot,
-        wpack,
-        back_scale * LOG2E,
-        back_scale,
+        cotangent.reshape(32, 4, 1024),
+        coarse_qkv,
+        coarse_out,
+        coarse_scale.reshape(1, 1),
     )
     return (output.reshape(4, 8, 4, 1024), grad.reshape(4, 8, 4, 1024), qkv_grad, out_grad)
 

time: 139 us -> 125 us (0.90)
  Pallas kernels: 124 us -> 114 us
  local copies, waits for them, and re-layouts: 12.9 us -> 8.83 us
    pallas_call x1, Pallas kernels: 124 us -> 114 us  [per_device(): pl.pallas_call(kernel, out_shape=(jax.ShapeDtypeStruct((32, 4, 1024), BF1...]
    reshape x3 -> x0, local copies, waits for them, and re-layouts: 5.45 us -> none  [the longest x1 1.98 us: per_device(): grad.reshape(4, 8, 4, 1024)]
    unnamed x8 -> x5, local copies, waits for them, and re-layouts: 4.65 us -> 8.83 us
where the time goes in v4:
time: 125 us; the launch traced here: 124 us
  Pallas kernels  114 us (91%)
  local copies, waits for them, and re-layouts  8.83 us (7%)
  between operations  1.29 us (1%)
    pallas_call x1, Pallas kernels, per_device(): pl.pallas_call(kernel, out_shape=(jax.ShapeDtypeStruct((32, 4, 1024), BF1...  114 us
    unnamed x5, local copies, waits for them, and re-layouts  8.83 us

profile of v4, /device:TPU:1, one launch (start us, length us, event | category | flops | bytes accessed | tf_op | source)
XLA Modules:
  0.0 124.1 jit_solution(12099383142069684539)
XLA Ops:
  1.3 2.2 %copy.18.heads_ref = bf16[3,1024,64]{2,1,0:T(8,128)(2,1)} copy(bf16[3,1024,64]{1,2,0:T(8,128)(2,1)} %param.21) | data formatting | bytes 786432 | tf_op args[7]
  3.4 114.0 %step.1 = (bf16[32,4,1024]{2,1,0:T(4,128)(2,1)}, f32[32,4,1024]{2,1,0:T(4,128)}, f32[3,128,64]{2,1,0:T(8,128)}, f32[64,128]{1,0:T(8,128)}) custom-call(bf16[4,128,512]{2,1,0:T(8,128)(2,1)} %bitcast.11, bf16[384,128]{1,0:T(8,128)(2,1)} %constant.6.clone.sel_ref, s32[8,384]{1,0:T(8,128)} %constant.7.clone.place_ref, s32[256,128]{1,0:T(8,128)} %constant.8.clone.query_ref, ...), custom_call_target="tpu_custom_call" | custom-call | flops 35999997952 | bytes 16000000 | tf_op jit(solution)/shard_map/step/pallas_call | solution.py:502
  117.4 1.7 %copy.19 = f32[3,128,64]{1,2,0:T(8,128)} copy(f32[3,128,64]{2,1,0:T(8,128)} %get-tuple-element.14) | data formatting | bytes 196608
  119.1 1.7 %copy.24 = bf16[4,8,4,1024]{3,2,1,0:T(4,128)(2,1)} copy(bf16[4,8,4,1024]{3,2,1,0:T(4,128)(2,1)} %bitcast.10) | data formatting | bytes 524288
  120.8 1.9 %copy.25 = f32[4,8,4,1024]{3,2,1,0:T(4,128)} copy(f32[4,8,4,1024]{3,2,1,0:T(4,128)} %bitcast.9) | data formatting | bytes 1048576
  122.7 1.4 %copy.26 = f32[64,128]{1,0:T(8,128)} copy(f32[64,128]{1,0:T(8,128)} %get-tuple-element.23) | data formatting | bytes 65536

commit v5 on v4

v5 whole, which is shorter than its diff:
```python
import jax
import jax.numpy as jnp
import numpy as np
from jax import lax
from jax.experimental import pallas as pl
from jax.experimental.pallas import tpu as pltpu
from jax.sharding import PartitionSpec as P

MESH = pl.DeviceIdType.MESH
F32 = jnp.float32
BF16 = jnp.bfloat16
SEG = ((128, 48), (176, 48), (224, 32), (256, 32), (288, 16), (304, 16), (320, 16), (336, 16))
WAY = ((0, 1), (0, -1), (1, 0), (-1, 0), (1, 1), (1, -1), (-1, 1), (-1, -1))
KEYS = 384
RING = (1, 3, 2)
BLOCK = 512
KEY, VALUE, QUERY, ATTN = range(4)
LOG2E = 1.4426950408889634
LN2 = 0.6931471805599453


def dot(a, b):
    return jnp.dot(a, b, preferred_element_type=F32)


def dot_nt(a, b):
    return lax.dot_general(a, b, (((1,), (1,)), ((), ())), preferred_element_type=F32)


def start_copy(source, target, send_sem, recv_sem, device):
    copy = pltpu.make_async_remote_copy(
        src_ref=source, dst_ref=target, send_sem=send_sem, recv_sem=recv_sem, device_id=device, device_id_type=MESH
    )
    copy.start()
    return copy


def swap_peers(x, y, z, core):
    peers = []
    for d in range(1, 16):
        px, py = lax.rem(x + d // 4, 4), lax.rem(y + d % 4, 4)
        peers.append((px, py, (py * 2 + core, px * 4 + z)))
    return peers


def fine_tables():
    sel = np.zeros((KEYS, 128), np.float32)
    place = np.full((8, KEYS), 10000, np.int32)
    query = np.zeros((256, 128), np.int32)
    for p in range(4):
        for u in range(8):
            for w in range(4):
                n = p * 32 + u * 4 + w
                i, j = 2 * u + p // 2, 2 * w + p % 2
                sel[n, i * 8 + j] = 1
                place[0, n], place[1, n] = i, j
                query[n, 0] = query[n + 128, 0] = i
                query[n, 1] = query[n + 128, 1] = j
    for (start, _), (down, right) in zip(SEG, WAY):
        rows = {0: range(16), 1: range(13, 16), -1: range(3)}[down]
        cols = {0: range(8), 1: range(5, 8), -1: range(3)}[right]
        n = start
        for i in rows:
            for j in cols:
                sel[n, i * 8 + j] = 1
                place[0, n], place[1, n] = i - 16 * down, j - 8 * right
                n += 1
    return sel, place, query


def kernel(
    x_ref, sel_ref, place_ref, query_ref, gain_ref, wqkv_hbm, wout_hbm, scale_ref, wmerge_hbm, gain2_ref,
    cot_ref, heads_ref, proj_ref, scale2_ref,
    out_ref, grad_ref, dw_ref, do_ref,
    inner_ref, ng, cg, wg, tr, gr, qg, kv,
    keys_in, send, kn, vv, qn, fr, bias, tk, tq, gs,
    powers, ones_v, kvt, vt, g_aug, g_turn, q_turn, gq_turn, outs_turn, inv, own_v,
    r, rr, gsend, grecv, ps, pr, ws, wt, wsum, wr,
    send_sem, recv_sem, w_s, w_r, f_s, f_r, c_s, c_r, n_s, n_r, a_s, a_r, k_s, k_r,
    x_s, x_r, g_s, g_r, b_s, b_r, p_s, p_r, t_s, t_r, d_s, d_r, l_s,
):
    row, col = lax.axis_index("row"), lax.axis_index("col")
    y, core, x, z = lax.div(row, 2), lax.rem(row, 2), lax.div(col, 4), lax.rem(col, 4)
    barrier = pltpu.get_barrier_semaphore()
    peers = [(lax.rem(row + a + 8, 8), lax.rem(col + b + 16, 16)) for a, b in WAY]
    z_peers = [(row, x * 4 + lax.rem(z + off, 4)) for off in RING]
    x_peers = [(row, lax.rem(x + off, 4) * 4 + z) for off in RING]
    twin = (y * 2 + 1 - core, col)
    swap = swap_peers(x, y, z, core)
    for peer in peers + z_peers + x_peers + [twin] + [p for _, _, p in swap]:
        pl.semaphore_signal(barrier, inc=1, device_id=peer, device_id_type=MESH)

    wqkv_ref = powers.at[0:512, 1024:2560]
    wout_ref = powers.at[512:1024, 1024:1536]
    wmerge_ref = powers.at[:, 0:1024]
    loads = [
        pltpu.make_async_copy(wqkv_hbm, wqkv_ref, l_s.at[0]),
        pltpu.make_async_copy(wout_hbm, wout_ref, l_s.at[1]),
        pltpu.make_async_copy(wmerge_hbm, wmerge_ref, l_s.at[2]),
    ]
    for load in loads:
        load.start()
    own_kv = pl.ds(pl.multiple_of(x * 128, 128), 128)
    own_qo = pl.ds(pl.multiple_of(512 + x * 128, 128), 128)
    wg[:, own_kv] = jnp.concatenate([heads_ref[1], heads_ref[2]], axis=0).astype(F32).T.astype(BF16)
    wg[:, own_qo] = jnp.concatenate([heads_ref[0], proj_ref[...]], axis=0).astype(F32).T.astype(BF16)
    cg[0] = cot_ref[...].reshape(128, 1024)
    back = scale2_ref[...] * (1.0 / 64)
    head_of = lax.shift_right_logical(lax.broadcasted_iota(jnp.int32, (1, 512), 1), 6)
    fine_scale = jnp.zeros((1, 512), F32)
    for h in range(8):
        fine_scale = jnp.where(head_of == h, scale_ref[0:1, h : h + 1] * (1.0 / 64), fine_scale)

    @pl.loop(0, 4)
    def _(img):
        packed = dot(sel_ref[...], x_ref[img]).astype(BF16)
        keys_in[img, 0:128, :] = packed[0:128]
        send[img] = packed[128:352]
        keys_in[img, 352:384, :] = packed[352:384]

    pl.semaphore_wait(barrier, 30)
    copies = []
    for k, ((start, size), peer) in enumerate(zip(SEG, peers)):
        copy = pltpu.make_async_remote_copy(
            src_ref=send.at[:, start - 128 : start - 128 + size, :],
            dst_ref=keys_in.at[:, start : start + size, :],
            send_sem=send_sem.at[k],
            recv_sem=recv_sem.at[k],
            device_id=peer,
            device_id_type=MESH,
        )
        copy.start()
        copies.append(copy)

    seen = (
        (jnp.abs(place_ref[0:1, :] - query_ref[:, 0:1]) <= 3)
        & (jnp.abs(place_ref[1:2, :] - query_ref[:, 1:2]) <= 3)
    )
    gi = place_ref[0:1, :] + row * 16
    gj = place_ref[1:2, :] + col * 8
    inside = (gi >= 0) & (gi < 128) & (gj >= 0) & (gj < 128)
    bias[...] = jnp.where(seen & inside, 0.0, -1e30).astype(F32)

    lane = lax.broadcasted_iota(jnp.int32, (128, 128), 1)
    sub = lax.broadcasted_iota(jnp.int32, (128, 128), 0)
    same = jnp.where((lane < 64) == (sub < 64), 1.0 / 64, 0.0).astype(BF16)

    def token_norm(tokens):
        xf = tokens.astype(F32)
        factor = lax.rsqrt(jnp.mean(xf * xf, axis=-1, keepdims=True) + 1e-06)
        return (xf * factor * gain_ref[...]).astype(BF16)

    def head_norm(values):
        vf = values.astype(BF16).astype(F32)
        sq = (vf * vf).astype(BF16)
        parts = [dot(sq[:, k * 128 : k * 128 + 128], same) for k in range(4)]
        return vf * lax.rsqrt(jnp.concatenate(parts, axis=1) + 1e-06)

    loads[0].wait()

    @pl.loop(0, 4)
    def _(img):
        nx = token_norm(keys_in[img, 0:128, :])
        qn[img] = (head_norm(dot(nx, wqkv_ref[:, 0:512])) * fine_scale).astype(BF16)
        kn[img, 0:128, :] = head_norm(dot(nx, wqkv_ref[:, 512:1024])).astype(BF16)
        vv[img, 0:128, :] = dot(nx, wqkv_ref[:, 1024:1536]).astype(BF16)

    for copy in copies:
        copy.wait()
    half = pl.ds(pl.multiple_of(core * 512, 512), 512)
    quarters = [pl.ds(pl.multiple_of(core * 512 + n * 256, 256), 256) for n in range(2)]

    def head_copies(block, rows, sems, peer, target):
        copies = []
        for n in range(2):
            piece = wg.at[rows, pl.ds(pl.multiple_of(n * 512 + block * 128, 128), 128)]
            copies.append(start_copy(piece, piece, sems[0].at[target, n], sems[1].at[target, n], peer))
        return copies

    w_copies = [head_copies(x, half, (w_s, w_r), x_peers[k], k) for k in range(2)]

    @pl.loop(0, 4)
    def _(img):
        nx = token_norm(keys_in[img, 128:384, :])
        kn[img, 128:384, :] = head_norm(dot(nx, wqkv_ref[:, 512:1024])).astype(BF16)
        vv[img, 128:384, :] = dot(nx, wqkv_ref[:, 1024:1536]).astype(BF16)

    ones = jnp.ones((KEYS, 128), BF16)
    loads[1].wait()
    loads[2].wait()

    @pl.loop(0, 4)
    def _(img):
        mixed = []
        for pair in range(4):
            at = slice(pair * 128, pair * 128 + 128)
            q = qn[img, :, at]
            zero = jnp.zeros_like(q)
            both = jnp.concatenate([jnp.where(lane < 64, q, zero), jnp.where(lane < 64, zero, q)], axis=0)
            powered = jnp.exp(dot_nt(both, kn[img, :, at]) + bias[...]).astype(BF16)
            sums = dot(powered, jnp.concatenate([vv[img, :, at], ones], axis=1))
            ratio = sums[:, 0:128] / sums[:, 128:256]
            mixed.append(jnp.where(lane < 64, ratio[0:128], ratio[128:256]).astype(BF16))
        mix = jnp.concatenate(mixed, axis=1)
        fr[img] = (keys_in[img, 0:128, :].astype(F32) + dot(mix, wout_ref[...])).astype(BF16)

    left, right, across = lax.rem(x + 3, 4), lax.rem(x + 1, 4), lax.rem(x + 2, 4)
    w_far = []
    f_copies = []
    for k, (block, peer) in enumerate(((left, x_peers[0]), (right, x_peers[1]))):
        for copy in w_copies[k]:
            copy.wait()
        w_far += head_copies(block, quarters[k], (w_s, w_r), peer, 2 + k)
        f_copies += head_copies(block, half, (f_s, f_r), twin, k)

    merged = jnp.zeros((128, 1024), F32)
    for p in range(4):
        part = jnp.concatenate([fr[img, p * 32 : p * 32 + 32, :] for img in range(4)], axis=0)
        merged = merged + dot(part, wmerge_ref[p * 512 : p * 512 + 512, :])
    inner = merged.astype(BF16)
    inner_ref[...] = inner
    xf = inner.astype(F32)
    factor = lax.rsqrt(jnp.mean(xf * xf, axis=-1, keepdims=True) + 1e-06)
    ng[0] = (xf * factor * gain2_ref[...]).astype(BF16)
    up, down = z_peers[0], z_peers[1]
    from_below = start_copy(ng.at[0], ng.at[1], n_s.at[0], n_r.at[0], up)
    from_above = start_copy(ng.at[0], ng.at[2], n_s.at[1], n_r.at[1], down)
    for copy in w_far:
        copy.wait()
    f_copies += head_copies(across, half, (f_s, f_r), twin, 2)
    for copy in f_copies:
        copy.wait()

    mine = pl.ds(pl.multiple_of(y * 32, 32), 32)
    here = x * 4 + y
    a_copies = []
    far_copies = []

    def project(j):
        value = dot(ng[j], wg[...]).astype(BF16)
        for h in range(4):
            tk[h, j] = value[:, h * 128 : h * 128 + 128]
            tq[h, j] = value[:, 512 + h * 128 : 640 + h * 128]

    def spread(source, target, pieces, sems):
        copies = []
        for d, (px, py, peer) in enumerate(swap):
            rows = pl.ds(pl.multiple_of(py * 32, 32), 32)
            copies.append(
                start_copy(
                    source.at[px, pieces, rows, :], target.at[here, pieces], sems[0].at[d], sems[1].at[d], peer
                )
            )
        target[here, pieces] = source[x, pieces, mine, :]
        return copies

    def swap_halves(values):
        return pltpu.roll(values, 64, 1)

    project(0)
    a_copies.append(spread(tk, tr, slice(0, 1), (a_s.at[0], a_r.at[0])))
    from_below.wait()
    far_copies.append(
        start_copy(ng.at[1, 0:64, :], ng.at[3, 0:64, :], n_s.at[2], n_r.at[2], up)
    )
    from_above.wait()
    far_copies.append(
        start_copy(ng.at[2, 64:128, :], ng.at[3, 64:128, :], n_s.at[3], n_r.at[3], down)
    )
    c_copies = [
        start_copy(cg.at[0], cg.at[1 + k], c_s.at[k], c_r.at[k], z_peers[k]) for k in range(2)
    ]
    project(1)
    project(2)
    a_copies.append(spread(tk, tr, slice(1, 3), (a_s.at[1], a_r.at[1])))
    for copy in far_copies:
        copy.wait()
    project(3)
    for h in range(4):
        for n in range(2):
            high = swap_halves(tq[h, n + 2].astype(F32))
            tk[h, 4 + n] = jnp.where(lane < 64, tq[h, n].astype(F32), high).astype(BF16)
    a_copies.append(spread(tk, tr, slice(3, 6), (a_s.at[2], a_r.at[2])))
    c_far = []
    for k, peer in enumerate((up, down)):
        c_copies[k].wait()
        rows = slice(k * 64, k * 64 + 64)
        c_far.append(
            start_copy(cg.at[1 + k, rows, :], cg.at[3, rows, :], c_s.at[2 + k], c_r.at[2 + k], peer)
        )

    low = jnp.where(sub < 64, 1.0 / 64, 0.0).astype(BF16)
    lane64 = lane[0:64]
    for d in range(16):
        if d > 0:
            for copies in a_copies:
                copies[d - 1].wait()
        dx, dy = d // 4, d % 4
        slot = lax.rem(x - dx + 4, 4) * 4 + lax.rem(y - dy + 4, 4)
        at = pl.ds(pl.multiple_of(slot * 128, 128), 128)
        k_f = tr[slot, 0:4].reshape(128, 128).astype(F32)
        k_n = k_f * lax.rsqrt(dot((k_f * k_f).astype(BF16), low) + 1e-06)
        kv[at, :] = jnp.where(lane < 64, k_n, k_f).astype(BF16)
        q_f = tr[slot, 4:6].reshape(64, 128).astype(F32)
        q_n = q_f * lax.rsqrt(dot((q_f * q_f).astype(BF16), same) + 1e-06) * (back * LOG2E)
        q_n = jnp.concatenate([q_n, swap_halves(q_n)], axis=0)
        qg[at, :] = jnp.where(lane < 64, q_n, 0.0).astype(BF16)
    k_copy = start_copy(kv.at[0:2048, :], kv.at[2048:4096, :], k_s, k_r, twin)

    for copy in c_far:
        copy.wait()
    for n in range(2):
        first = dot(cg[n], wg[:, 512:1024])
        second = dot(cg[n + 2], wg[:, 512:1024])
        for h in range(4):
            at = slice(h * 128, h * 128 + 128)
            gs[h, n] = jnp.where(lane < 64, swap_halves(first[:, at]), second[:, at]).astype(BF16)
    grad_copies = spread(gs, gr, slice(0, 2), (x_s, x_r))

    def key_side(c):
        at = slice(c * 512, c * 512 + 512)
        tile = kv[at, :]
        ones_v[at, :] = jnp.where(lax.broadcasted_iota(jnp.int32, (512, 128), 1) < 64, jnp.ones_like(tile), tile)
        turned = tile.astype(F32).T.astype(BF16)
        kvt[:, at] = turned[0:64]
        vt[0:64, at] = turned[64:128]

    vt[64:80, :] = jnp.ones((16, 4096), BF16)
    for c in range(4):
        key_side(c)
    k_copy.wait()
    for c in range(4, 8):
        key_side(c)

    def head_back(values, upstream):
        factor = lax.rsqrt(dot((values * values).astype(BF16), same) + 1e-06)
        unit = values * factor
        return factor * (upstream - unit * dot((upstream * unit).astype(BF16), same))

    def pack(turned):
        return jnp.concatenate([turned[:, 0:64], turned[:, 64:128]], axis=0).T

    def block_copy(kind, i, dy):
        px, py = lax.rem(x + i + 1, 4), lax.rem(y + dy, 4)
        n = lax.rem(i + 1, 4) * 4 + dy
        return pltpu.make_async_remote_copy(
            src_ref=r.at[kind, px * 4 + py], dst_ref=rr.at[kind, x, :, mine, :],
            send_sem=b_s.at[kind, n], recv_sem=b_r.at[kind, n],
            device_id=(py * 2 + core, px * 4 + z), device_id_type=MESH,
        )

    def block_start(kind, i):
        for dy in range(1, 4):
            block_copy(kind, i, dy).start()

        @pl.when(i < 3)
        def _():
            block_copy(kind, i, 0).start()

    def block_finish(kind):
        rr[kind, x, :, mine, :] = r[kind, here]
        for i in range(4):
            for dy in range(4):
                if i < 3 or dy > 0:
                    block_copy(kind, i, dy).wait()

    @pl.loop(0, 4)
    def _(i):
        block = lax.rem(x + i + 1, 4)
        rows = pl.ds(pl.multiple_of(block * BLOCK, BLOCK), BLOCK)
        q = qg[rows, :]
        for c in range(8):
            at = slice(c * 512, c * 512 + 512)
            powers[rows, at] = jnp.exp2(dot_nt(q, kv[at, :])).astype(BF16)
        total = dot_nt(vt[...], powers[rows, :])
        inverse = 1.0 / total[64:65]
        outputs = total[0:64] * inverse
        inv[0:1, rows] = inverse
        outs_turn[:, rows] = outputs
        q_turn[:, rows] = q.astype(F32).T[0:64].astype(BF16)
        for py in range(4):
            r[ATTN, block * 4 + py] = pack(outputs[:, py * 128 : py * 128 + 128]).astype(BF16).reshape(2, 32, 128)
        block_start(ATTN, i)

    for copy in grad_copies:
        copy.wait()
    sub64 = lax.broadcasted_iota(jnp.int32, (64, BLOCK), 0)

    @pl.loop(0, 4)
    def _(b):
        rows = pl.ds(pl.multiple_of(b * BLOCK, BLOCK), BLOCK)
        parts = []
        for n in range(4):
            turned = gr[b * 4 + n].reshape(64, 128).astype(F32).T
            parts += [turned[0:64], turned[64:128]]
        g = jnp.concatenate(parts, axis=1)
        inverse = inv[0:1, rows]
        delta = jnp.sum(g * outs_turn[:, rows], axis=0, keepdims=True) * inverse
        high = delta.astype(BF16).astype(F32)
        rest = jnp.where(sub64 == 0, -high, jnp.where(sub64 == 1, high - delta, 0.0))
        scaled = g * inverse
        g_turn[:, rows] = scaled.astype(BF16)
        g_aug[rows, :] = jnp.concatenate([rest, scaled], axis=0).T.astype(BF16)

    for c in range(4):
        at = slice(c * 512, c * 512 + 512)
        gsend[1, :, at] = dot(g_turn[...], powers[:, 2048 + c * 512 : 2560 + c * 512]).astype(BF16)
    twin_v = start_copy(gsend.at[1], grecv.at[1], g_s.at[1], g_r.at[1], twin)
    for c in range(4):
        at = slice(c * 512, c * 512 + 512)
        own_v[:, at] = dot(g_turn[...], powers[:, at])
    gq_turn[...] = jnp.zeros_like(gq_turn)

    def pick(kind, h, j, high):
        packed = rr[kind, h, j % 2].astype(F32)
        return packed if (j >= 2) == high else swap_halves(packed)

    def out_part(j):
        parts = [jnp.where(lane < 64, 0.0, pick(ATTN, h, j, True)).astype(BF16) for h in range(4)]
        return dot_nt(jnp.concatenate(parts, axis=1), wg[:, 512:1024])

    def grad_part(j):
        parts = [jnp.where(lane < 64, pick(KEY, h, j, False), pick(VALUE, h, j, True)) for h in range(4)]
        parts += [jnp.where(lane < 64, pick(QUERY, h, j, False), 0.0) for h in range(4)]
        return dot_nt(jnp.concatenate([part.astype(BF16) for part in parts], axis=1), wg[...])

    p_copies = []

    def send_part(kind, k, value):
        ps[kind, k] = value.astype(BF16)
        n = kind * 3 + k
        p_copies.append(start_copy(ps.at[kind, k], pr.at[kind, k], p_s.at[n], p_r.at[n], z_peers[k]))

    def weight_part(kind):
        tokens = (cg if kind == ATTN else ng)[...].reshape(512, 1024)
        parts = []
        for h in range(4):
            even, odd = rr[kind, h, 0].astype(F32).T, rr[kind, h, 1].astype(F32).T
            parts.append(jnp.concatenate([even[0:64], odd[0:64], even[64:128], odd[64:128]], axis=1).astype(BF16))
        value = dot(jnp.concatenate(parts, axis=0), tokens).astype(BF16)
        for h in range(4):
            for band in range(8):
                ws[kind, band % 2, h, band // 2] = value[h * 64 : h * 64 + 64, band * 128 : band * 128 + 128]
        return start_copy(ws.at[kind, 1 - core], wt.at[kind], t_s.at[kind], t_r.at[kind], twin)

    d_copies = []

    def weight_send(kind, copy):
        copy.wait()
        for h in range(4):
            for py in range(4):
                total = ws[kind, core, h, py].astype(F32) + wt[kind, h, py].astype(F32)
                wsum[kind, h, py] = total.astype(BF16)
        for d, (px, py, peer) in enumerate(swap):
            d_copies.append(
                start_copy(
                    wsum.at[kind, px, py], wr.at[kind, here], d_s.at[kind, d], d_r.at[kind, d], peer
                )
            )
        wr[kind, here] = wsum[kind, x, y]

    block_finish(ATTN)
    for k, j in ((2, 3), (0, 2), (1, 1)):
        send_part(0, k, out_part(j))
    t_attn = weight_part(ATTN)
    twin_v.wait()

    @pl.loop(0, 4)
    def _(i):
        block = lax.rem(x + i + 1, 4)
        for py in range(4):
            slot = block * 4 + py
            at = pl.ds(pl.multiple_of(slot * 128, 128), 128)
            part = own_v[:, at] + grecv[1, :, at].astype(F32)
            r[VALUE, slot] = pack(part).astype(BF16).reshape(2, 32, 128)
        block_start(VALUE, i)

    def key_block(at):
        powers[:, at] = (powers[:, at].astype(F32) * dot_nt(g_aug[...], ones_v[at, :])).astype(BF16)
        grad_s = powers[:, at]
        gq_turn[...] += dot_nt(kvt[:, at], grad_s)
        return dot(q_turn[...], grad_s) * LN2

    @pl.loop(0, 4)
    def _(i):
        at = pl.ds(pl.multiple_of(i * 512, 512), 512)
        gsend[0, :, at] = key_block(pl.ds(pl.multiple_of(2048 + i * 512, 512), 512)).astype(BF16)

    start_copy(gsend.at[0], grecv.at[0], g_s.at[0], g_r.at[0], twin)
    weight_send(ATTN, t_attn)
    block_finish(VALUE)
    t_value = weight_part(VALUE)

    @pl.loop(0, 4)
    def _(i):
        block = lax.rem(x + i + 1, 4)
        at = pl.ds(pl.multiple_of(block * 512, 512), 512)
        own = key_block(at)

        @pl.when(i == 0)
        def _():
            pltpu.make_async_remote_copy(
                src_ref=gsend.at[0], dst_ref=grecv.at[0], send_sem=g_s.at[0], recv_sem=g_r.at[0],
                device_id=twin, device_id_type=MESH,
            ).wait()

        upstream = own + grecv[0, :, at].astype(F32)
        for py in range(4):
            raw = tr[block * 4 + py, 0:4].reshape(128, 128).astype(F32)
            raw = jnp.where(lane64 < 64, raw[0:64], swap_halves(raw[64:128]))
            part = pack(upstream[:, py * 128 : py * 128 + 128])
            r[KEY, block * 4 + py] = head_back(raw, part).astype(BF16).reshape(2, 32, 128)
        block_start(KEY, i)

    @pl.loop(0, 4)
    def _(i):
        block = lax.rem(x + i + 1, 4)
        for py in range(4):
            slot = block * 4 + py
            part = pack(gq_turn[:, pl.ds(pl.multiple_of(slot * 128, 128), 128)] * back)
            raw = tr[slot, 4:6].reshape(64, 128).astype(F32)
            r[QUERY, slot] = head_back(raw, part).astype(BF16).reshape(2, 32, 128)
        block_start(QUERY, i)

    weight_send(VALUE, t_value)
    block_finish(KEY)
    t_key = weight_part(KEY)
    term = out_part(0)
    block_finish(QUERY)
    for k, j in ((2, 3), (0, 2), (1, 1)):
        send_part(1, k, grad_part(j))
    t_query = weight_part(QUERY)
    weight_send(KEY, t_key)
    grad = grad_part(0)
    weight_send(QUERY, t_query)

    for copy in p_copies:
        copy.wait()
    for k in range(3):
        term = term + pr[0, k].astype(F32)
        grad = grad + pr[1, k].astype(F32)
    values = inner_ref[...].astype(F32)
    out_ref[...] = (values + term).astype(BF16).reshape(32, 4, 1024)
    factor = lax.rsqrt(jnp.mean(values * values, axis=-1, keepdims=True) + 1e-06)
    unit = values * factor
    upstream = grad * gain2_ref[...]
    grad = cg[0].astype(F32) + factor * (
        upstream - unit * jnp.mean(upstream * unit, axis=-1, keepdims=True)
    )
    grad_ref[...] = grad.reshape(32, 4, 1024)

    for copy in d_copies:
        copy.wait()
    for kind in range(4):
        total = jnp.zeros((64, 128), F32)
        for n in range(16):
            total = total + wr[kind, n].astype(F32)
        if kind == ATTN:
            do_ref[...] = total
        else:
            dw_ref[(1, 2, 0)[kind]] = total


def store_kernel(a_ref, b_ref, c_ref, d_ref, a_out, b_out, c_out, d_out):
    a_out[...] = a_ref[...]
    b_out[...] = b_ref[...]
    c_out[...] = c_ref[...]
    d_out[...] = d_ref[...]


def per_device(
    fine_input,
    gain_fine,
    fine_qkv,
    fine_out,
    fine_scale,
    merge_weight,
    gain_coarse,
    coarse_qkv,
    coarse_out,
    coarse_scale,
    cotangent,
):
    sel, place, query = fine_tables()
    vmem = pl.BlockSpec(memory_space=pltpu.VMEM)
    hbm = pl.BlockSpec(memory_space=pl.ANY)
    dma = pltpu.SemaphoreType.DMA
    results = pl.pallas_call(
        kernel,
        out_shape=(
            jax.ShapeDtypeStruct((32, 4, 1024), BF16),
            jax.ShapeDtypeStruct((32, 4, 1024), F32),
            jax.ShapeDtypeStruct((3, 64, 128), F32),
            jax.ShapeDtypeStruct((64, 128), F32),
        ),
        in_specs=[vmem] * 5 + [hbm, hbm, vmem, hbm] + [vmem] * 5,
        out_specs=(vmem,) * 4,
        scratch_shapes=[
            pltpu.VMEM((128, 1024), BF16),
            pltpu.VMEM((4, 128, 1024), BF16),
            pltpu.VMEM((4, 128, 1024), BF16),
            pltpu.VMEM((1024, 1024), BF16),
            pltpu.VMEM((16, 6, 32, 128), BF16),
            pltpu.VMEM((16, 2, 32, 128), BF16),
            pltpu.VMEM((2048, 128), BF16),
            pltpu.VMEM((4096, 128), BF16),
            pltpu.VMEM((4, KEYS, 512), BF16),
            pltpu.VMEM((4, 224, 512), BF16),
            pltpu.VMEM((4, KEYS, 512), BF16),
            pltpu.VMEM((4, KEYS, 512), BF16),
            pltpu.VMEM((4, 128, 512), BF16),
            pltpu.VMEM((4, 128, 512), BF16),
            pltpu.VMEM((256, KEYS), F32),
            pltpu.VMEM((4, 6, 128, 128), BF16),
            pltpu.VMEM((4, 4, 128, 128), BF16),
            pltpu.VMEM((4, 2, 128, 128), BF16),
            pltpu.VMEM((2048, 4096), BF16),
            pltpu.VMEM((4096, 128), BF16),
            pltpu.VMEM((64, 4096), BF16),
            pltpu.VMEM((80, 4096), BF16),
            pltpu.VMEM((2048, 128), BF16),
            pltpu.VMEM((64, 2048), BF16),
            pltpu.VMEM((64, 2048), BF16),
            pltpu.VMEM((64, 2048), F32),
            pltpu.VMEM((64, 2048), F32),
            pltpu.VMEM((8, 2048), F32),
            pltpu.VMEM((64, 2048), F32),
            pltpu.VMEM((4, 16, 2, 32, 128), BF16),
            pltpu.VMEM((4, 4, 2, 128, 128), BF16),
            pltpu.VMEM((2, 64, 2048), BF16),
            pltpu.VMEM((2, 64, 2048), BF16),
            pltpu.VMEM((2, 3, 128, 1024), BF16),
            pltpu.VMEM((2, 3, 128, 1024), BF16),
            pltpu.VMEM((4, 2, 4, 4, 64, 128), BF16),
            pltpu.VMEM((4, 4, 4, 64, 128), BF16),
            pltpu.VMEM((4, 4, 4, 64, 128), BF16),
            pltpu.VMEM((4, 16, 64, 128), BF16),
            dma((8,)), dma((8,)),
            dma((4, 2)), dma((4, 2)), dma((3, 2)), dma((3, 2)), dma((4,)), dma((4,)), dma((4,)), dma((4,)),
            dma((3, 15)), dma((3, 15)), dma(()), dma(()),
            dma((15,)), dma((15,)), dma((2,)), dma((2,)), dma((4, 16)), dma((4, 16)), dma((6,)), dma((6,)),
            dma((4,)), dma((4,)), dma((4, 15)), dma((4, 15)), dma((3,)),
        ],
        compiler_params=pltpu.CompilerParams(
            collective_id=0, has_side_effects=True, vmem_limit_bytes=60 * 1024 * 1024
        ),
        cost_estimate=pl.CostEstimate(flops=36_000_000_000, bytes_accessed=16_000_000, transcendentals=12_000_000),
        name="step",
    )(
        fine_input.reshape(4, 128, 512),
        jnp.asarray(sel, BF16),
        jnp.asarray(place),
        jnp.asarray(query),
        gain_fine.reshape(1, 512),
        fine_qkv,
        fine_out,
        fine_scale.reshape(1, 8),
        merge_weight,
        gain_coarse.reshape(1, 1024),
        cotangent.reshape(32, 4, 1024),
        coarse_qkv.transpose(0, 2, 1),
        coarse_out,
        coarse_scale.reshape(1, 1),
    )
    output, grad, qkv_grad, out_grad = pl.pallas_call(
        store_kernel,
        out_shape=tuple(jax.ShapeDtypeStruct(v.shape, v.dtype) for v in results),
        in_specs=[vmem] * 4,
        out_specs=(vmem,) * 4,
        compiler_params=pltpu.CompilerParams(vmem_limit_bytes=60 * 1024 * 1024),
        name="store",
    )(*results)
    return (
        output.reshape(4, 8, 4, 1024),
        grad.reshape(4, 8, 4, 1024),
        qkv_grad.transpose(0, 2, 1),
        out_grad,
    )


def solution(mesh):
    return jax.shard_map(
        per_device,
        mesh=mesh,
        in_specs=(
            P(None, "row", "col", None),
            P(),
            P(),
            P(),
            P(),
            P(),
            P(),
            P(None, None, "col"),
            P("col", None),
            P("col"),
            P(None, "row", "col", None),
        ),
        out_specs=(
            P(None, "row", "col", None),
            P(None, "row", "col", None),
            P(None, "row", "col"),
            P("col", "row"),
        ),
        check_vma=False,
    )
```

time: 125 us -> 119 us (0.952)
  local copies, waits for them, and re-layouts: 8.83 us -> 0 us
  Pallas kernels: 114 us -> 118 us
    unnamed x5 -> x0, local copies, waits for them, and re-layouts: 8.83 us -> none
    pallas_call x0 -> x1, Pallas kernels: none -> 2.07 us  [per_device(): pl.pallas_call(store_kernel, out_shape=tuple((jax.ShapeDtypeStruct(v.shap...]
    pallas_call x1, Pallas kernels: 114 us -> 116 us  [per_device(): pl.pallas_call(kernel, out_shape=(jax.ShapeDtypeStruct((32, 4, 1024), BF1...]
where the time goes in v5:
time: 119 us
  Pallas kernels  118 us (99%)
  between operations  1.29 us (1%)
    pallas_call x1, Pallas kernels, per_device(): pl.pallas_call(kernel, out_shape=(jax.ShapeDtypeStruct((32, 4, 1024), BF1...  116 us

profile of v5, /device:TPU:1, one launch (start us, length us, event | category | flops | bytes accessed | tf_op | source)
XLA Modules:
  0.0 118.9 jit_solution(1358307845039068065)
XLA Ops:
  1.3 115.5 %step.1 = (bf16[32,4,1024]{2,1,0:T(4,128)(2,1)}, f32[32,4,1024]{2,1,0:T(4,128)}, f32[3,64,128]{2,1,0:T(8,128)}, f32[64,128]{1,0:T(8,128)}) custom-call(bf16[4,128,512]{2,1,0:T(8,128)(2,1)} %bitcast.11, bf16[384,128]{1,0:T(8,128)(2,1)} %constant.6.clone.sel_ref, s32[8,384]{1,0:T(8,128)} %constant.7.clone.place_ref, s32[256,128]{1,0:T(8,128)} %constant.8.clone.query_ref, ...), custom_call_target="tpu_custom_call" | custom-call | flops 35999997952 | bytes 16000000 | tf_op jit(solution)/shard_map/step/pallas_call | solution.py:588
  116.8 2.1 %store.1 = (bf16[32,4,1024]{2,1,0:T(4,128)(2,1)}, f32[32,4,1024]{2,1,0:T(4,128)}, f32[3,64,128]{2,1,0:T(8,128)}, f32[64,128]{1,0:T(8,128)}) custom-call(bf16[32,4,1024]{2,1,0:T(4,128)(2,1)} %get-tuple-element.12.a_ref, f32[32,4,1024]{2,1,0:T(4,128)} %get-tuple-element.13.b_ref, f32[3,64,128]{2,1,0:T(8,128)} %get-tuple-element.14.c_ref, ...), custom_call_target="tpu_custom_call" | custom-call | tf_op jit(solution)/shard_map/store/pallas_call | solution.py:665

commit v6 on v5

--- a/solution.py
+++ b/solution.py
@@ -14,7 +14,7 @@
 KEYS = 384
 RING = (1, 3, 2)
 BLOCK = 512
-KEY, VALUE, QUERY, ATTN = range(4)
+ATTN, VALUE, KEY, QUERY = range(4)
 LOG2E = 1.4426950408889634
 LN2 = 0.6931471805599453
 
@@ -69,9 +69,10 @@
 
 
 def kernel(
-    x_ref, sel_ref, place_ref, query_ref, gain_ref, wqkv_hbm, wout_hbm, scale_ref, wmerge_hbm, gain2_ref,
-    cot_ref, heads_ref, proj_ref, scale2_ref,
+    x_hbm, sel_hbm, place_hbm, query_hbm, gain_ref, wqkv_hbm, wout_hbm, scale_ref, wmerge_hbm, gain2_ref,
+    cot_hbm, heads_hbm, proj_hbm, scale2_ref,
     out_ref, grad_ref, dw_ref, do_ref,
+    x_ref, sel_ref, place_ref, query_ref, cot_ref, heads_ref, proj_ref,
     inner_ref, ng, cg, wg, tr, gr, qg, kv,
     keys_in, send, kn, vv, qn, fr, bias, tk, tq, gs,
     powers, ones_v, kvt, vt, g_aug, g_turn, q_turn, gq_turn, outs_turn, inv, own_v,
@@ -93,23 +94,22 @@
     wqkv_ref = powers.at[0:512, 1024:2560]
     wout_ref = powers.at[512:1024, 1024:1536]
     wmerge_ref = powers.at[:, 0:1024]
-    loads = [
-        pltpu.make_async_copy(wqkv_hbm, wqkv_ref, l_s.at[0]),
-        pltpu.make_async_copy(wout_hbm, wout_ref, l_s.at[1]),
-        pltpu.make_async_copy(wmerge_hbm, wmerge_ref, l_s.at[2]),
-    ]
+    pairs = (
+        (x_hbm, x_ref), (sel_hbm, sel_ref), (heads_hbm, heads_ref), (proj_hbm, proj_ref), (cot_hbm, cot_ref),
+        (place_hbm, place_ref), (query_hbm, query_ref), (wqkv_hbm, wqkv_ref), (wout_hbm, wout_ref),
+        (wmerge_hbm, wmerge_ref),
+    )
+    loads = [pltpu.make_async_copy(pair[0], pair[1], l_s.at[n]) for n, pair in enumerate(pairs)]
     for load in loads:
         load.start()
-    own_kv = pl.ds(pl.multiple_of(x * 128, 128), 128)
-    own_qo = pl.ds(pl.multiple_of(512 + x * 128, 128), 128)
-    wg[:, own_kv] = jnp.concatenate([heads_ref[1], heads_ref[2]], axis=0).astype(F32).T.astype(BF16)
-    wg[:, own_qo] = jnp.concatenate([heads_ref[0], proj_ref[...]], axis=0).astype(F32).T.astype(BF16)
-    cg[0] = cot_ref[...].reshape(128, 1024)
     back = scale2_ref[...] * (1.0 / 64)
     head_of = lax.shift_right_logical(lax.broadcasted_iota(jnp.int32, (1, 512), 1), 6)
     fine_scale = jnp.zeros((1, 512), F32)
     for h in range(8):
         fine_scale = jnp.where(head_of == h, scale_ref[0:1, h : h + 1] * (1.0 / 64), fine_scale)
+
+    loads[0].wait()
+    loads[1].wait()
 
     @pl.loop(0, 4)
     def _(img):
@@ -132,6 +132,14 @@
         copy.start()
         copies.append(copy)
 
+    for load in loads[2:7]:
+        load.wait()
+    own_kv = pl.ds(pl.multiple_of(x * 128, 128), 128)
+    own_qo = pl.ds(pl.multiple_of(512 + x * 128, 128), 128)
+    wg[:, own_kv] = jnp.concatenate([heads_ref[1], heads_ref[2]], axis=0).astype(F32).T.astype(BF16)
+    wg[:, own_qo] = jnp.concatenate([heads_ref[0], proj_ref[...]], axis=0).astype(F32).T.astype(BF16)
+    cg[0] = cot_ref[...].reshape(128, 1024)
+
     seen = (
         (jnp.abs(place_ref[0:1, :] - query_ref[:, 0:1]) <= 3)
         & (jnp.abs(place_ref[1:2, :] - query_ref[:, 1:2]) <= 3)
@@ -156,7 +164,7 @@
         parts = [dot(sq[:, k * 128 : k * 128 + 128], same) for k in range(4)]
         return vf * lax.rsqrt(jnp.concatenate(parts, axis=1) + 1e-06)
 
-    loads[0].wait()
+    loads[7].wait()
 
     @pl.loop(0, 4)
     def _(img):
@@ -168,7 +176,6 @@
     for copy in copies:
         copy.wait()
     half = pl.ds(pl.multiple_of(core * 512, 512), 512)
-    quarters = [pl.ds(pl.multiple_of(core * 512 + n * 256, 256), 256) for n in range(2)]
 
     def head_copies(block, rows, sems, peer, target):
         copies = []
@@ -177,20 +184,16 @@
             copies.append(start_copy(piece, piece, sems[0].at[target, n], sems[1].at[target, n], peer))
         return copies
 
-    w_copies = [head_copies(x, half, (w_s, w_r), x_peers[k], k) for k in range(2)]
-
-    @pl.loop(0, 4)
-    def _(img):
+    w_copies = [head_copies(x, half, (w_s, w_r), x_peers[k], k) for k in range(3)]
+
+    ones = jnp.ones((KEYS, 128), BF16)
+    loads[8].wait()
+    loads[9].wait()
+
+    def tokens_out(img):
         nx = token_norm(keys_in[img, 128:384, :])
         kn[img, 128:384, :] = head_norm(dot(nx, wqkv_ref[:, 512:1024])).astype(BF16)
         vv[img, 128:384, :] = dot(nx, wqkv_ref[:, 1024:1536]).astype(BF16)
-
-    ones = jnp.ones((KEYS, 128), BF16)
-    loads[1].wait()
-    loads[2].wait()
-
-    @pl.loop(0, 4)
-    def _(img):
         mixed = []
         for pair in range(4):
             at = slice(pair * 128, pair * 128 + 128)
@@ -204,37 +207,35 @@
         mix = jnp.concatenate(mixed, axis=1)
         fr[img] = (keys_in[img, 0:128, :].astype(F32) + dot(mix, wout_ref[...])).astype(BF16)
 
-    left, right, across = lax.rem(x + 3, 4), lax.rem(x + 1, 4), lax.rem(x + 2, 4)
-    w_far = []
+    n_copies = []
+    for part in range(2):
+        pl.loop(part * 2, part * 2 + 2)(tokens_out)
+        rows = slice(part * 64, part * 64 + 64)
+        merged = jnp.zeros((64, 1024), F32)
+        for p in range(4):
+            group = jnp.concatenate([fr[part * 2 + n, p * 32 : p * 32 + 32, :] for n in range(2)], axis=0)
+            merged = merged + dot(group, wmerge_ref[p * 512 : p * 512 + 512, :])
+        inner = merged.astype(BF16)
+        inner_ref[rows, :] = inner
+        xf = inner.astype(F32)
+        factor = lax.rsqrt(jnp.mean(xf * xf, axis=-1, keepdims=True) + 1e-06)
+        ng[0, rows, :] = (xf * factor * gain2_ref[...]).astype(BF16)
+        n_copies.append([
+            start_copy(ng.at[0, rows, :], ng.at[1 + k, rows, :], n_s.at[part, k], n_r.at[part, k], z_peers[k])
+            for k in range(3)
+        ])
+    c_copies = [start_copy(cg.at[0], cg.at[1 + k], c_s.at[k], c_r.at[k], z_peers[k]) for k in range(3)]
     f_copies = []
-    for k, (block, peer) in enumerate(((left, x_peers[0]), (right, x_peers[1]))):
+    for k, off in enumerate(RING):
         for copy in w_copies[k]:
             copy.wait()
-        w_far += head_copies(block, quarters[k], (w_s, w_r), peer, 2 + k)
-        f_copies += head_copies(block, half, (f_s, f_r), twin, k)
-
-    merged = jnp.zeros((128, 1024), F32)
-    for p in range(4):
-        part = jnp.concatenate([fr[img, p * 32 : p * 32 + 32, :] for img in range(4)], axis=0)
-        merged = merged + dot(part, wmerge_ref[p * 512 : p * 512 + 512, :])
-    inner = merged.astype(BF16)
-    inner_ref[...] = inner
-    xf = inner.astype(F32)
-    factor = lax.rsqrt(jnp.mean(xf * xf, axis=-1, keepdims=True) + 1e-06)
-    ng[0] = (xf * factor * gain2_ref[...]).astype(BF16)
-    up, down = z_peers[0], z_peers[1]
-    from_below = start_copy(ng.at[0], ng.at[1], n_s.at[0], n_r.at[0], up)
-    from_above = start_copy(ng.at[0], ng.at[2], n_s.at[1], n_r.at[1], down)
-    for copy in w_far:
-        copy.wait()
-    f_copies += head_copies(across, half, (f_s, f_r), twin, 2)
+        f_copies += head_copies(lax.rem(x - off + 4, 4), half, (f_s, f_r), twin, k)
     for copy in f_copies:
         copy.wait()
 
     mine = pl.ds(pl.multiple_of(y * 32, 32), 32)
     here = x * 4 + y
     a_copies = []
-    far_copies = []
 
     def project(j):
         value = dot(ng[j], wg[...]).astype(BF16)
@@ -259,36 +260,20 @@
 
     project(0)
     a_copies.append(spread(tk, tr, slice(0, 1), (a_s.at[0], a_r.at[0])))
-    from_below.wait()
-    far_copies.append(
-        start_copy(ng.at[1, 0:64, :], ng.at[3, 0:64, :], n_s.at[2], n_r.at[2], up)
-    )
-    from_above.wait()
-    far_copies.append(
-        start_copy(ng.at[2, 64:128, :], ng.at[3, 64:128, :], n_s.at[3], n_r.at[3], down)
-    )
-    c_copies = [
-        start_copy(cg.at[0], cg.at[1 + k], c_s.at[k], c_r.at[k], z_peers[k]) for k in range(2)
-    ]
+    for part in range(2):
+        n_copies[part][0].wait()
+        n_copies[part][1].wait()
     project(1)
     project(2)
     a_copies.append(spread(tk, tr, slice(1, 3), (a_s.at[1], a_r.at[1])))
-    for copy in far_copies:
-        copy.wait()
+    for part in range(2):
+        n_copies[part][2].wait()
     project(3)
     for h in range(4):
         for n in range(2):
             high = swap_halves(tq[h, n + 2].astype(F32))
             tk[h, 4 + n] = jnp.where(lane < 64, tq[h, n].astype(F32), high).astype(BF16)
     a_copies.append(spread(tk, tr, slice(3, 6), (a_s.at[2], a_r.at[2])))
-    c_far = []
-    for k, peer in enumerate((up, down)):
-        c_copies[k].wait()
-        rows = slice(k * 64, k * 64 + 64)
-        c_far.append(
-            start_copy(cg.at[1 + k, rows, :], cg.at[3, rows, :], c_s.at[2 + k], c_r.at[2 + k], peer)
-        )
-
     low = jnp.where(sub < 64, 1.0 / 64, 0.0).astype(BF16)
     lane64 = lane[0:64]
     for d in range(16):
@@ -307,7 +292,7 @@
         qg[at, :] = jnp.where(lane < 64, q_n, 0.0).astype(BF16)
     k_copy = start_copy(kv.at[0:2048, :], kv.at[2048:4096, :], k_s, k_r, twin)
 
-    for copy in c_far:
+    for copy in c_copies:
         copy.wait()
     for n in range(2):
         first = dot(cg[n], wg[:, 512:1024])
@@ -440,29 +425,29 @@
         value = dot(jnp.concatenate(parts, axis=0), tokens).astype(BF16)
         for h in range(4):
             for band in range(8):
-                ws[kind, band % 2, h, band // 2] = value[h * 64 : h * 64 + 64, band * 128 : band * 128 + 128]
-        return start_copy(ws.at[kind, 1 - core], wt.at[kind], t_s.at[kind], t_r.at[kind], twin)
+                piece = value[h * 64 : h * 64 + 64, band * 128 : band * 128 + 128]
+                ws[band % 2, kind, h, band // 2] = piece
+
+    def weight_twin(kinds, n):
+        return start_copy(ws.at[1 - core, kinds], wt.at[kinds], t_s.at[n], t_r.at[n], twin)
 
     d_copies = []
 
-    def weight_send(kind, copy):
-        copy.wait()
-        for h in range(4):
-            for py in range(4):
-                total = ws[kind, core, h, py].astype(F32) + wt[kind, h, py].astype(F32)
-                wsum[kind, h, py] = total.astype(BF16)
+    def weight_send(kinds, n):
+        for kind in range(kinds.start, kinds.stop):
+            for h in range(4):
+                for py in range(4):
+                    total = ws[core, kind, h, py].astype(F32) + wt[kind, h, py].astype(F32)
+                    wsum[h, py, kind] = total.astype(BF16)
         for d, (px, py, peer) in enumerate(swap):
             d_copies.append(
-                start_copy(
-                    wsum.at[kind, px, py], wr.at[kind, here], d_s.at[kind, d], d_r.at[kind, d], peer
-                )
+                start_copy(wsum.at[px, py, kinds], wr.at[here, kinds], d_s.at[n, d], d_r.at[n, d], peer)
             )
-        wr[kind, here] = wsum[kind, x, y]
+        wr[here, kinds] = wsum[x, y, kinds]
 
     block_finish(ATTN)
     for k, j in ((2, 3), (0, 2), (1, 1)):
         send_part(0, k, out_part(j))
-    t_attn = weight_part(ATTN)
     twin_v.wait()
 
     @pl.loop(0, 4)
@@ -487,9 +472,6 @@
         gsend[0, :, at] = key_block(pl.ds(pl.multiple_of(2048 + i * 512, 512), 512)).astype(BF16)
 
     start_copy(gsend.at[0], grecv.at[0], g_s.at[0], g_r.at[0], twin)
-    weight_send(ATTN, t_attn)
-    block_finish(VALUE)
-    t_value = weight_part(VALUE)
 
     @pl.loop(0, 4)
     def _(i):
@@ -522,17 +504,23 @@
             r[QUERY, slot] = head_back(raw, part).astype(BF16).reshape(2, 32, 128)
         block_start(QUERY, i)
 
-    weight_send(VALUE, t_value)
+    block_finish(VALUE)
+    weight_part(ATTN)
+    weight_part(VALUE)
+    first = weight_twin(slice(0, 2), 0)
     block_finish(KEY)
-    t_key = weight_part(KEY)
+    weight_part(KEY)
+    first.wait()
+    weight_send(slice(0, 2), 0)
     term = out_part(0)
     block_finish(QUERY)
     for k, j in ((2, 3), (0, 2), (1, 1)):
         send_part(1, k, grad_part(j))
-    t_query = weight_part(QUERY)
-    weight_send(KEY, t_key)
+    weight_part(QUERY)
+    last = weight_twin(slice(2, 4), 1)
     grad = grad_part(0)
-    weight_send(QUERY, t_query)
+    last.wait()
+    weight_send(slice(2, 4), 1)
 
     for copy in p_copies:
         copy.wait()
@@ -554,11 +542,11 @@
     for kind in range(4):
         total = jnp.zeros((64, 128), F32)
         for n in range(16):
-            total = total + wr[kind, n].astype(F32)
+            total = total + wr[n, kind].astype(F32)
         if kind == ATTN:
             do_ref[...] = total
         else:
-            dw_ref[(1, 2, 0)[kind]] = total
+            dw_ref[(3, 2, 1, 0)[kind]] = total
 
 
 def store_kernel(a_ref, b_ref, c_ref, d_ref, a_out, b_out, c_out, d_out):
@@ -593,9 +581,16 @@
             jax.ShapeDtypeStruct((3, 64, 128), F32),
             jax.ShapeDtypeStruct((64, 128), F32),
         ),
-        in_specs=[vmem] * 5 + [hbm, hbm, vmem, hbm] + [vmem] * 5,
+        in_specs=[hbm] * 4 + [vmem, hbm, hbm, vmem, hbm, vmem] + [hbm] * 3 + [vmem],
         out_specs=(vmem,) * 4,
         scratch_shapes=[
+            pltpu.VMEM((4, 128, 512), BF16),
+            pltpu.VMEM((KEYS, 128), BF16),
+            pltpu.VMEM((8, KEYS), jnp.int32),
+            pltpu.VMEM((256, 128), jnp.int32),
+            pltpu.VMEM((32, 4, 1024), BF16),
+            pltpu.VMEM((3, 64, 1024), BF16),
+            pltpu.VMEM((64, 1024), BF16),
             pltpu.VMEM((128, 1024), BF16),
             pltpu.VMEM((4, 128, 1024), BF16),
             pltpu.VMEM((4, 128, 1024), BF16),
@@ -631,15 +626,15 @@
             pltpu.VMEM((2, 64, 2048), BF16),
             pltpu.VMEM((2, 3, 128, 1024), BF16),
             pltpu.VMEM((2, 3, 128, 1024), BF16),
-            pltpu.VMEM((4, 2, 4, 4, 64, 128), BF16),
+            pltpu.VMEM((2, 4, 4, 4, 64, 128), BF16),
             pltpu.VMEM((4, 4, 4, 64, 128), BF16),
             pltpu.VMEM((4, 4, 4, 64, 128), BF16),
-            pltpu.VMEM((4, 16, 64, 128), BF16),
+            pltpu.VMEM((16, 4, 64, 128), BF16),
             dma((8,)), dma((8,)),
-            dma((4, 2)), dma((4, 2)), dma((3, 2)), dma((3, 2)), dma((4,)), dma((4,)), dma((4,)), dma((4,)),
+            dma((3, 2)), dma((3, 2)), dma((3, 2)), dma((3, 2)), dma((3,)), dma((3,)), dma((2, 3)), dma((2, 3)),
             dma((3, 15)), dma((3, 15)), dma(()), dma(()),
             dma((15,)), dma((15,)), dma((2,)), dma((2,)), dma((4, 16)), dma((4, 16)), dma((6,)), dma((6,)),
-            dma((4,)), dma((4,)), dma((4, 15)), dma((4, 15)), dma((3,)),
+            dma((2,)), dma((2,)), dma((2, 15)), dma((2, 15)), dma((10,)),
         ],
         compiler_params=pltpu.CompilerParams(
             collective_id=0, has_side_effects=True, vmem_limit_bytes=60 * 1024 * 1024

time: 119 us -> 114 us (0.958)
  Pallas kernels: 118 us -> 113 us
    pallas_call x1, Pallas kernels: 116 us -> 111 us  [per_device(): pl.pallas_call(kernel, out_shape=(jax.ShapeDtypeStruct((32, 4, 1024), BF1...]
where the time goes in v6:
time: 114 us
  Pallas kernels  113 us (99%)
  between operations  1.29 us (1%)
    pallas_call x1, Pallas kernels, per_device(): pl.pallas_call(kernel, out_shape=(jax.ShapeDtypeStruct((32, 4, 1024), BF1...  111 us

profile of v6, /device:TPU:1, one launch (start us, length us, event | category | flops | bytes accessed | tf_op | source)
XLA Modules:
  0.0 114.2 jit_solution(10826443725141697332)
XLA Ops:
  1.3 110.8 %step.1 = (bf16[32,4,1024]{2,1,0:T(4,128)(2,1)}, f32[32,4,1024]{2,1,0:T(4,128)}, f32[3,64,128]{2,1,0:T(8,128)}, f32[64,128]{1,0:T(8,128)}) custom-call(bf16[4,128,512]{2,1,0:T(8,128)(2,1)} %bitcast.11, bf16[384,128]{1,0:T(8,128)(2,1)} %constant.6.clone.sel_hbm, s32[8,384]{1,0:T(8,128)} %constant.7.clone.place_hbm, s32[256,128]{1,0:T(8,128)} %constant.8.clone.query_hbm, ...), custom_call_target="tpu_custom_call" | custom-call | flops 35999997952 | bytes 16000000 | tf_op jit(solution)/shard_map/step/pallas_call | solution.py:576
  112.1 2.1 %store.1 = (bf16[32,4,1024]{2,1,0:T(4,128)(2,1)}, f32[32,4,1024]{2,1,0:T(4,128)}, f32[3,64,128]{2,1,0:T(8,128)}, f32[64,128]{1,0:T(8,128)}) custom-call(bf16[32,4,1024]{2,1,0:T(4,128)(2,1)} %get-tuple-element.12.a_ref, f32[32,4,1024]{2,1,0:T(4,128)} %get-tuple-element.13.b_ref, f32[3,64,128]{2,1,0:T(8,128)} %get-tuple-element.14.c_ref, ...), custom_call_target="tpu_custom_call" | custom-call | tf_op jit(solution)/shard_map/store/pallas_call | solution.py:660

commit v7 on v6

--- a/solution.py
+++ b/solution.py
@@ -237,11 +237,13 @@
     here = x * 4 + y
     a_copies = []
 
-    def project(j):
-        value = dot(ng[j], wg[...]).astype(BF16)
-        for h in range(4):
-            tk[h, j] = value[:, h * 128 : h * 128 + 128]
-            tq[h, j] = value[:, 512 + h * 128 : 640 + h * 128]
+    def project(first, last):
+        value = dot(ng[first:last].reshape((last - first) * 128, 1024), wg[...]).astype(BF16)
+        for j in range(first, last):
+            rows = slice((j - first) * 128, (j - first) * 128 + 128)
+            for h in range(4):
+                tk[h, j] = value[rows, h * 128 : h * 128 + 128]
+                tq[h, j] = value[rows, 512 + h * 128 : 640 + h * 128]
 
     def spread(source, target, pieces, sems):
         copies = []
@@ -258,22 +260,17 @@
     def swap_halves(values):
         return pltpu.roll(values, 64, 1)
 
-    project(0)
+    project(0, 1)
     a_copies.append(spread(tk, tr, slice(0, 1), (a_s.at[0], a_r.at[0])))
     for part in range(2):
-        n_copies[part][0].wait()
-        n_copies[part][1].wait()
-    project(1)
-    project(2)
-    a_copies.append(spread(tk, tr, slice(1, 3), (a_s.at[1], a_r.at[1])))
-    for part in range(2):
-        n_copies[part][2].wait()
-    project(3)
+        for copy in n_copies[part]:
+            copy.wait()
+    project(1, 4)
     for h in range(4):
         for n in range(2):
             high = swap_halves(tq[h, n + 2].astype(F32))
             tk[h, 4 + n] = jnp.where(lane < 64, tq[h, n].astype(F32), high).astype(BF16)
-    a_copies.append(spread(tk, tr, slice(3, 6), (a_s.at[2], a_r.at[2])))
+    a_copies.append(spread(tk, tr, slice(1, 6), (a_s.at[1], a_r.at[1])))
     low = jnp.where(sub < 64, 1.0 / 64, 0.0).astype(BF16)
     lane64 = lane[0:64]
     for d in range(16):
@@ -632,7 +629,7 @@
             pltpu.VMEM((16, 4, 64, 128), BF16),
             dma((8,)), dma((8,)),
             dma((3, 2)), dma((3, 2)), dma((3, 2)), dma((3, 2)), dma((3,)), dma((3,)), dma((2, 3)), dma((2, 3)),
-            dma((3, 15)), dma((3, 15)), dma(()), dma(()),
+            dma((2, 15)), dma((2, 15)), dma(()), dma(()),
             dma((15,)), dma((15,)), dma((2,)), dma((2,)), dma((4, 16)), dma((4, 16)), dma((6,)), dma((6,)),
             dma((2,)), dma((2,)), dma((2, 15)), dma((2, 15)), dma((10,)),
         ],

time: 114 us -> 117 us (1.026)
  Pallas kernels: 113 us -> 115 us
    pallas_call x1, Pallas kernels: 111 us -> 113 us  [per_device(): pl.pallas_call(kernel, out_shape=(jax.ShapeDtypeStruct((32, 4, 1024), BF1...]
where the time goes in v7:
time: 117 us; the launch traced here: 116 us
  Pallas kernels  115 us (98%)
  between operations  1.29 us (1%)
    pallas_call x1, Pallas kernels, per_device(): pl.pallas_call(kernel, out_shape=(jax.ShapeDtypeStruct((32, 4, 1024), BF1...  113 us

profile of v7, /device:TPU:1, one launch (start us, length us, event | category | flops | bytes accessed | tf_op | source)
XLA Modules:
  0.0 116.4 jit_solution(2799851780715145523)
XLA Ops:
  1.3 113.0 %step.1 = (bf16[32,4,1024]{2,1,0:T(4,128)(2,1)}, f32[32,4,1024]{2,1,0:T(4,128)}, f32[3,64,128]{2,1,0:T(8,128)}, f32[64,128]{1,0:T(8,128)}) custom-call(bf16[4,128,512]{2,1,0:T(8,128)(2,1)} %bitcast.11, bf16[384,128]{1,0:T(8,128)(2,1)} %constant.6.clone.sel_hbm, s32[8,384]{1,0:T(8,128)} %constant.7.clone.place_hbm, s32[256,128]{1,0:T(8,128)} %constant.8.clone.query_hbm, ...), custom_call_target="tpu_custom_call" | custom-call | flops 35999997952 | bytes 16000000 | tf_op jit(solution)/shard_map/step/pallas_call | solution.py:573
  114.3 2.1 %store.1 = (bf16[32,4,1024]{2,1,0:T(4,128)(2,1)}, f32[32,4,1024]{2,1,0:T(4,128)}, f32[3,64,128]{2,1,0:T(8,128)}, f32[64,128]{1,0:T(8,128)}) custom-call(bf16[32,4,1024]{2,1,0:T(4,128)(2,1)} %get-tuple-element.12.a_ref, f32[32,4,1024]{2,1,0:T(4,128)} %get-tuple-element.13.b_ref, f32[3,64,128]{2,1,0:T(8,128)} %get-tuple-element.14.c_ref, ...), custom_call_target="tpu_custom_call" | custom-call | tf_op jit(solution)/shard_map/store/pallas_call | solution.py:657

commit v8 on v6

--- a/solution.py
+++ b/solution.py
@@ -15,6 +15,7 @@
 RING = (1, 3, 2)
 BLOCK = 512
 ATTN, VALUE, KEY, QUERY = range(4)
+FAR_FIRST = sorted(range(15), key=lambda d: -((0, 1, 2, 1)[(d + 1) // 4] + (0, 1, 2, 1)[(d + 1) % 4]))
 LOG2E = 1.4426950408889634
 LN2 = 0.6931471805599453
 
@@ -244,13 +245,12 @@
             tq[h, j] = value[:, 512 + h * 128 : 640 + h * 128]
 
     def spread(source, target, pieces, sems):
-        copies = []
-        for d, (px, py, peer) in enumerate(swap):
+        copies = [None] * 15
+        for d in FAR_FIRST:
+            px, py, peer = swap[d]
             rows = pl.ds(pl.multiple_of(py * 32, 32), 32)
-            copies.append(
-                start_copy(
-                    source.at[px, pieces, rows, :], target.at[here, pieces], sems[0].at[d], sems[1].at[d], peer
-                )
+            copies[d] = start_copy(
+                source.at[px, pieces, rows, :], target.at[here, pieces], sems[0].at[d], sems[1].at[d], peer
             )
         target[here, pieces] = source[x, pieces, mine, :]
         return copies
@@ -439,7 +439,8 @@
                 for py in range(4):
                     total = ws[core, kind, h, py].astype(F32) + wt[kind, h, py].astype(F32)
                     wsum[h, py, kind] = total.astype(BF16)
-        for d, (px, py, peer) in enumerate(swap):
+        for d in FAR_FIRST:
+            px, py, peer = swap[d]
             d_copies.append(
                 start_copy(wsum.at[px, py, kinds], wr.at[here, kinds], d_s.at[n, d], d_r.at[n, d], peer)
             )

time: 114 us -> 114 us (level)
  no operation moved by 1% of the time
where the time goes in v8:
time: 114 us
  Pallas kernels  112 us (98%)
  between operations  1.29 us (1%)
    pallas_call x1, Pallas kernels, per_device(): pl.pallas_call(kernel, out_shape=(jax.ShapeDtypeStruct((32, 4, 1024), BF1...  110 us

profile of v8, /device:TPU:1, one launch (start us, length us, event | category | flops | bytes accessed | tf_op | source)
XLA Modules:
  0.0 113.8 jit_solution(1506632285563224721)
XLA Ops:
  1.3 110.4 %step.1 = (bf16[32,4,1024]{2,1,0:T(4,128)(2,1)}, f32[32,4,1024]{2,1,0:T(4,128)}, f32[3,64,128]{2,1,0:T(8,128)}, f32[64,128]{1,0:T(8,128)}) custom-call(bf16[4,128,512]{2,1,0:T(8,128)(2,1)} %bitcast.11, bf16[384,128]{1,0:T(8,128)(2,1)} %constant.6.clone.sel_hbm, s32[8,384]{1,0:T(8,128)} %constant.7.clone.place_hbm, s32[256,128]{1,0:T(8,128)} %constant.8.clone.query_hbm, ...), custom_call_target="tpu_custom_call" | custom-call | flops 35999997952 | bytes 16000000 | tf_op jit(solution)/shard_map/step/pallas_call | solution.py:577
  111.7 2.1 %store.1 = (bf16[32,4,1024]{2,1,0:T(4,128)(2,1)}, f32[32,4,1024]{2,1,0:T(4,128)}, f32[3,64,128]{2,1,0:T(8,128)}, f32[64,128]{1,0:T(8,128)}) custom-call(bf16[32,4,1024]{2,1,0:T(4,128)(2,1)} %get-tuple-element.12.a_ref, f32[32,4,1024]{2,1,0:T(4,128)} %get-tuple-element.13.b_ref, f32[3,64,128]{2,1,0:T(8,128)} %get-tuple-element.14.c_ref, ...), custom_call_target="tpu_custom_call" | custom-call | tf_op jit(solution)/shard_map/store/pallas_call | solution.py:661
